TPU v7x, 128 devices: a whole 4x4x4 slice. The times are simulated.
128 devices in a mesh: ctx: 16 (over x, y), tp: 8 (over z, core).
Axes of the slice: x: 4, y: 4, z: 4, core: 2. Of those that a mesh axis runs over, the one named last changes fastest.
Arguments:
- tokens: bfloat16 [4096, 8192], P(('ctx', 'tp')), may hold values from -6 to 6
- in_weight: bfloat16 [8192, 3, 4096], P(None, None, 'tp'), may hold values from -0.0625 to 0.0625
- short_filter: float32 [3, 3, 4096], P(None, None, 'tp'), may hold values from -3 to 3
- mr_filter: float32 [128, 256], P(None, 'tp'), may hold values from -0.35355338 to 0.35355338
- mr_bias: float32 [4096], P('tp'), may hold values from -4 to 4
- out_weight: bfloat16 [4096, 8192], P('tp', 'ctx'), may hold values from -0.09375 to 0.09375
Outputs:
- mixed: bfloat16 [4096, 8192], P(('ctx', 'tp'))
All inputs are finite; a program needn't handle non-finite values.
Results may differ from a plain program's by a relative error of at most 0.018.
Values may be sent and summed in bfloat16 or wider, within the bound.
No kernel may reach another device: no remote copies, remote signals or barrier semaphores. Data moves between devices by JAX's collectives and lax.ppermute only.
A program may use at most 192 MiB of HBM per device.

v0:
```python
import jax
import jax.numpy as jnp
from jax import lax
from jax.sharding import PartitionSpec as P


def passed_along(shard, axis, by):
    count = lax.axis_size(axis)
    pairs = [(i, i + by) for i in range(count) if 0 <= i + by < count]
    return lax.ppermute(shard, axis, pairs)


def featurize(extended, filters):
    values = extended.astype(jnp.float32)
    out_length = values.shape[0] - 2
    return (
        filters[0] * values[2:]
        + filters[1] * values[1 : out_length + 1]
        + filters[2] * values[:out_length]
    )


def convolve(product, mr_filter, length):
    taps_count = mr_filter.shape[0]
    group_count = mr_filter.shape[1]
    channels = product.shape[1]
    group_width = channels // group_count
    block_count = -(-length // taps_count)
    tail_rows = block_count * taps_count - length
    values = jnp.pad(product.astype(jnp.float32), ((1, tail_rows), (0, 0)))
    columns = values.T.reshape(group_count, group_width, block_count + 1, taps_count)
    rows_out = lax.broadcasted_iota(jnp.int32, (taps_count, taps_count), 0)
    rows_in = lax.broadcasted_iota(jnp.int32, (taps_count, taps_count), 1)
    offsets = (rows_out - rows_in)[None, :, :]
    lag_table = lax.broadcasted_iota(jnp.int32, (taps_count, taps_count, taps_count), 0)
    near_mask = (offsets == lag_table).astype(jnp.float32)
    far_mask = (offsets + taps_count == lag_table).astype(jnp.float32)
    near_taps = jnp.einsum("jg,jtu->gtu", mr_filter, near_mask, precision=lax.Precision.HIGHEST)
    far_taps = jnp.einsum("jg,jtu->gtu", mr_filter, far_mask, precision=lax.Precision.HIGHEST)
    filtered = jnp.einsum(
        "gcbu,gtu->gcbt", columns[:, :, 1:], near_taps, precision=lax.Precision.HIGHEST
    )
    filtered = filtered + jnp.einsum(
        "gcbu,gtu->gcbt", columns[:, :, :block_count], far_taps, precision=lax.Precision.HIGHEST
    )
    filtered = filtered.reshape(channels, block_count * taps_count)
    return filtered.T


def shards(tokens, in_weight, short_filter, mr_filter, mr_bias, out_weight):
    in_width = in_weight.shape[0]
    channels = in_weight.shape[2]
    flat_weight = in_weight.reshape(in_width, 3 * channels)
    projected = jnp.dot(
        lax.all_gather(tokens, "tp", axis=0, tiled=True),
        flat_weight,
        preferred_element_type=jnp.float32,
    ).astype(jnp.bfloat16)
    length = projected.shape[0]
    projected = projected.reshape(length, 3, channels)
    taps_count = mr_filter.shape[0]
    earlier = passed_along(projected[length - 2 :], "ctx", 1)
    featured = featurize(jnp.concatenate([earlier, projected], 0), short_filter)
    own_product = (featured[:, 1, :] * featured[:, 2, :]).astype(jnp.bfloat16)
    earlier_product = passed_along(own_product[length - taps_count + 1 :], "ctx", 1)
    product = jnp.concatenate([earlier_product, own_product], 0)
    queries = featured[:, 0, :]
    filtered = convolve(product, mr_filter, length)
    direct = product[taps_count - 1 :].astype(jnp.float32)
    gated = (queries * (filtered + mr_bias * direct)).astype(jnp.bfloat16)
    partial_sum = jnp.dot(
        gated,
        lax.all_gather(out_weight, "ctx", axis=1, tiled=True),
        preferred_element_type=jnp.float32,
    )
    partial_sum = lax.optimization_barrier(partial_sum.astype(jnp.bfloat16)).astype(jnp.float32)
    summed = lax.psum_scatter(
        partial_sum.astype(jnp.bfloat16), "tp", scatter_dimension=0, tiled=True
    )
    return summed


def solution(mesh):
    return jax.shard_map(
        shards,
        mesh=mesh,
        in_specs=(
            P(("ctx", "tp"), None),
            P(None, None, "tp"),
            P(None, None, "tp"),
            P(None, "tp"),
            P("tp"),
            P("tp", "ctx"),
        ),
        out_specs=P(("ctx", "tp"), None),
        check_vma=False,
    )
```

profile of v0, /device:TPU:2, one launch (start us, length us, event | category | flops | bytes accessed | tf_op | source)
XLA Modules:
  0.0 176.1 jit_solution(17493240563666853546)
XLA Ops:
  6.5 0.0 copy-start
  6.5 0.0 all-gather.3.cloned.1.call-start
  6.5 0.7 all-gather.3.cloned.1.call-update
  7.3 0.0 all-gather.5.cloned.1.call-start
  7.3 0.7 all-gather.5.cloned.1.call-update
  8.0 0.0 reduce-scatter.2.cloned.1.call-start
  8.1 33.4 %copy.9 = bf16[8192,3,512]{0,2,1:T(8,128)(2,1)} copy(bf16[8192,3,512]{2,0,1:T(8,128)(2,1)} %param.7) | data formatting | bytes 50331648 | tf_op args[1]
  41.5 1.2 iota_compare_fusion
  42.7 0.0 copy-done
  42.8 5.8 %fusion = f32[128,128,32]{1,2,0:T(8,128)} fusion(pred[128,128,128]{2,1,0:T(32,128)(4,1)S(1)} %iota_compare_fusion, f32[128,32]{0,1:T(8,128)S(1)} %copy-done), kind=kOutput, calls=%fused_computation.3 | convolution fusion | flops 805306368 | bytes 4210688 | tf_op jit(solution)/shard_map/jg,jtu->gtu/dot_general | solution.py:39
  48.5 2.6 %iota_compare_fusion.1 = pred[128,128,128]{2,1,0:T(32,128)(4,1)} fusion(s32[128,128]{1,0:T(8,128)S(1)} %iota_subtract_fusion), kind=kLoop, calls=%fused_computation.2 | loop fusion | flops 2097152 | bytes 2162688 | tf_op jit(solution)/shard_map/eq | solution.py:36
  51.1 0.0 all-gather.3.cloned.1.call-done
  51.1 0.0 copy-start.4
  51.1 13.4 %convolution_convert_fusion.1 = bf16[256,1536]{1,0:T(8,128)(2,1)S(1)} fusion(bf16[256,8192]{1,0:T(8,128)(2,1)} %all-gather.3.cloned.1.call-done, bf16[8192,1536]{0,1:T(8,128)(2,1)} %bitcast.67), kind=kOutput, calls=%fused_computation.7 | convolution fusion | flops 6442844160 | bytes 30146560 | tf_op jit(solution)/shard_map/dot_general | solution.py:54
  64.5 3.5 %collective-permute-start = (bf16[2,3,512]{2,1,0:T(4,128)(2,1)S(1)}, bf16[2,3,512]{2,1,0:T(4,128)(2,1)S(1)}, u32[]{:S(2)}, u32[]{:S(2)}) collective-permute-start(bf16[2,3,512]{2,1,0:T(4,128)(2,1)S(1)} %slice.47), channel_id=1, source_target_pairs={{0,8},{8,16},{16,24},{24,32},{32,40},{40,48},{48,56},{56,64},{64,7... | collective-permute-start | bytes 18440 | tf_op jit(solution)/shard_map/ppermute | solution.py:10
  68.0 0.0 copy-done.4
  68.0 0.3 copy.10
  68.3 3.9 %collective-permute-done = bf16[2,3,512]{2,1,0:T(4,128)(2,1)S(1)} collective-permute-done((bf16[2,3,512]{2,1,0:T(4,128)(2,1)S(1)}, bf16[2,3,512]{2,1,0:T(4,128)(2,1)S(1)}, u32[]{:S(2)}, u32[]{:S(2)}) %collective-permute-start) | collective-permute-done | bytes 6176 | tf_op jit(solution)/shard_map/ppermute | solution.py:10
  72.2 0.3 copy.11
  72.4 0.5 maximum_convert_fusion
  73.0 0.0 copy-start.1
  73.0 1.6 fusion.10
  74.6 0.1 fusion.20
  74.7 0.1 slice_bitcast_fusion.1
  74.8 2.1 %collective-permute-start.1 = (bf16[127,512]{0,1:T(8,128)(2,1)S(1)}, bf16[127,512]{0,1:T(8,128)(2,1)S(1)}, u32[]{:S(2)}, u32[]{:S(2)}) collective-permute-start(bf16[127,512]{0,1:T(8,128)(2,1)S(1)} %slice_bitcast_fusion.1), channel_id=1, source_target_pairs={{0,8},{8,16},{16,24},{24,32},{32,40},{40,48},{48,56},{56,64},{64,7... | collective-permute-start | bytes 390152 | tf_op jit(solution)/shard_map/ppermute | solution.py:10
  76.9 0.0 copy-done.1
  76.9 5.7 %fusion.2 = f32[128,128,32]{1,2,0:T(8,128)} fusion(pred[128,128,128]{2,1,0:T(32,128)(4,1)S(1)} %copy-done.1, f32[128,32]{0,1:T(8,128)S(1)} %copy-done), kind=kOutput, calls=%fused_computation.5 | convolution fusion | flops 805306368 | bytes 4210688 | tf_op jit(solution)/shard_map/jg,jtu->gtu/dot_general | solution.py:38
  82.6 0.1 copy.12
  82.8 1.0 collective-permute-done.1
  83.7 0.1 copy.13
  83.9 0.2 copy.14
  84.1 0.1 reshape.35
  84.3 0.0 copy-start.2
  84.3 0.4 fusion.30
  84.6 4.7 %fusion.4 = f32[32,16,2,128]{3,1,2,0:T(8,128)S(1)} fusion(f32[128,128,32]{1,2,0:T(8,128)} %fusion, bf16[32,16,2,128]{3,2,1,0:T(2,128)(2,1)S(1)} %get-tuple-element.6), kind=kOutput, calls=%fused_computation.8 | convolution fusion | flops 201326592 | bytes 2883584 | tf_op jit(solution)/shard_map/gcbu,gtu->gcbt/dot_general | solution.py:43
  89.3 0.0 copy-done.2
  89.3 0.0 copy-start.3
  89.3 2.8 %fusion.12 = f32[32,16,2,128]{3,1,2,0:T(8,128)S(1)} fusion(f32[32,16,2,128]{3,1,2,0:T(8,128)S(1)} %fusion.4, f32[128,128,32]{1,2,0:T(8,128)S(1)} %copy-done.2, bf16[32,16,2,128]{3,2,1,0:T(2,128)(2,1)S(1)} %get-tuple-element.5), kind=kOutput, calls=%fused_computation.19 | convolution fusion | flops 201457664 | bytes 3407872 | tf_op jit(solution)/shard_map/gcbu,gtu->gcbt/dot_general | solution.py:40
  92.1 0.3 copy.17
  92.4 31.3 %all-gather.5.cloned.1.call-done = bf16[512,8192]{1,0:T(8,128)(2,1)} async-done(((bf16[512,512]{1,0:T(8,128)(2,1)}), bf16[512,8192]{1,0:T(8,128)(2,1)}) %all-gather.5.cloned.1.call-update) | async-done | bytes 8388624 | tf_op jit(solution)/shard_map/all_gather | solution.py:73
  123.7 0.0 copy-done.3
  123.7 7.8 %convolution_convert_fusion = bf16[256,8192]{1,0:T(8,128)(2,1)} fusion(bf16[512,8192]{1,0:T(8,128)(2,1)} %all-gather.5.cloned.1.call-done, f32[64,8,2,128]{3,2,1,0:T(2,128)S(1)} %bitcast.69, f32[256,3,512]{0,2,1:T(8,128)S(1)} %fusion.10, bf16[256,1,512]{0,2,1:T(8,128)(2,1)S(1)} %fusion.20, f32[512]{0:T(512)S(1)} %copy-done.3), kind=kOutput, calls=%fused_computation | convolution fusion | flops 2150236160 | bytes 13895680 | tf_op jit(solution)/shard_map/dot_general | solution.py:71
  131.5 0.0 reduce-scatter.2.cloned.1.call-update
  131.5 38.1 %reduce-scatter.2.cloned.1.call-done = bf16[32,8192]{1,0:T(8,128)(2,1)} async-done(((bf16[256,8192]{1,0:T(8,128)(2,1)}), bf16[32,8192]{1,0:T(8,128)(2,1)}) %reduce-scatter.2.cloned.1.call-update) | async-done | bytes 524304 | tf_op jit(solution)/shard_map/reduce_scatter | solution.py:77
  (6 shorter events, 0.1 us)
Async XLA Ops:
  6.5 36.2 %copy-start = (f32[128,32]{0,1:T(8,128)S(1)}, f32[128,32]{0,1:T(8,128)}, u32[]{:S(2)}) copy-start(f32[128,32]{0,1:T(8,128)} %param.9) | copy-start | bytes 49156
  6.5 44.6 %all-gather.3.cloned.1.call-start = ((), (), s32[]{:S(2)}) async-start(), calls=%async_computation.1 | async-start | bytes 4718592 | tf_op jit(solution)/shard_map/all_gather | solution.py:55
  7.3 116.4 %all-gather.5.cloned.1.call-start = ((), (), s32[]{:S(2)}) async-start(), calls=%async_computation.2 | async-start | bytes 8912896 | tf_op jit(solution)/shard_map/all_gather | solution.py:73
  8.0 161.6 %reduce-scatter.2.cloned.1.call-start = ((), (), s32[]{:S(2)}) async-start(), calls=%async_computation.3 | async-start | bytes 4718592 | tf_op jit(solution)/shard_map/reduce_scatter | solution.py:77
  51.1 16.9 %copy-start.4 = (f32[3,3,512]{2,1,0:T(4,128)S(1)}, f32[3,3,512]{2,1,0:T(4,128)}, u32[]{:S(2)}) copy-start(f32[3,3,512]{2,1,0:T(4,128)} %param.8) | copy-start | bytes 55300
  64.5 7.7 %collective-permute-start = (bf16[2,3,512]{2,1,0:T(4,128)(2,1)S(1)}, bf16[2,3,512]{2,1,0:T(4,128)(2,1)S(1)}, u32[]{:S(2)}, u32[]{:S(2)}) collective-permute-start(bf16[2,3,512]{2,1,0:T(4,128)(2,1)S(1)} %slice.47), channel_id=1, source_target_pairs={{0,8},{8,16},{16,24},{24,32},{32,40},{40,48},{48,56},{56,64},{64,7... | collective-permute-start | bytes 18440 | tf_op jit(solution)/shard_map/ppermute | solution.py:10
  73.0 3.9 %copy-start.1 = (pred[128,128,128]{2,1,0:T(32,128)(4,1)S(1)}, pred[128,128,128]{2,1,0:T(32,128)(4,1)}, u32[]{:S(2)}) copy-start(pred[128,128,128]{2,1,0:T(32,128)(4,1)} %iota_compare_fusion.1) | copy-start | bytes 6291460
  74.8 9.0 %collective-permute-start.1 = (bf16[127,512]{0,1:T(8,128)(2,1)S(1)}, bf16[127,512]{0,1:T(8,128)(2,1)S(1)}, u32[]{:S(2)}, u32[]{:S(2)}) collective-permute-start(bf16[127,512]{0,1:T(8,128)(2,1)S(1)} %slice_bitcast_fusion.1), channel_id=1, source_target_pairs={{0,8},{8,16},{16,24},{24,32},{32,40},{40,48},{48,56},{56,64},{64,7... | collective-permute-start | bytes 390152 | tf_op jit(solution)/shard_map/ppermute | solution.py:10
  84.3 5.0 %copy-start.2 = (f32[128,128,32]{1,2,0:T(8,128)S(1)}, f32[128,128,32]{1,2,0:T(8,128)}, u32[]{:S(2)}) copy-start(f32[128,128,32]{1,2,0:T(8,128)} %fusion.2) | copy-start | bytes 6291460
  89.3 34.4 %copy-start.3 = (f32[512]{0:T(512)S(1)}, f32[512]{0:T(512)}, u32[]{:S(2)}) copy-start(f32[512]{0:T(512)} %param.10) | copy-start | bytes 6148
Sparse Core Ops, SparseCore 0:
  9.1 34.6 all-gather.2
  45.9 77.7 all-gather.4
  131.6 37.9 reduce-scatter.1
where the time goes:
time: 177 us; the launch traced here: 176 us
  waiting for transfers between devices  75.7 us (43%)
  matrix products  40.1 us (23%)
  local copies, waits for them, and re-layouts  35.3 us (20%)
  between operations  13.3 us (8%)
  other arithmetic  6.08 us (3%)
  starting transfers between devices  5.64 us (3%)
    reduce_scatter x1, waiting for transfers between devices, shards(): lax.psum_scatter(partial_sum.astype(jnp.bfloat16), 'tp', scatter_dimensio...  38.1 us
    unnamed x11, local copies, waits for them, and re-layouts  33.4 us
    all_gather x1, waiting for transfers between devices, shards(): lax.all_gather(out_weight, 'ctx', axis=1, tiled=True)  31.3 us
    dot_general x1, matrix products, shards(): jnp.dot(lax.all_gather(tokens, 'tp', axis=0, tiled=True), flat_weight, pr...  13.4 us
    dot_general x1, matrix products, shards(): jnp.dot(gated, lax.all_gather(out_weight, 'ctx', axis=1, tiled=True), pre...  7.82 us
    dot_general x1, matrix products, convolve(): jnp.einsum('jg,jtu->gtu', mr_filter, far_mask, precision=lax.Precision.HI...  5.75 us
    dot_general x1, matrix products, convolve(): jnp.einsum('jg,jtu->gtu', mr_filter, near_mask, precision=lax.Precision.H...  5.75 us
    ppermute x2, starting transfers between devices, passed_along(): return lax.ppermute(shard, axis, pairs)  5.56 us
  transfers between devices with their start and end apart: 5, of which 4 were waited for; matrix products, arithmetic and copies ran while one was open for 42% of the time, Pallas kernels for 0%

commit v1 on v0

v1 whole, which is shorter than its diff:
```python
import functools

import jax
import jax.numpy as jnp
from jax import lax
from jax.experimental import pallas as pl
from jax.experimental.pallas import tpu as pltpu
from jax.sharding import Mesh, PartitionSpec as P

F32 = jnp.float32
BF16 = jnp.bfloat16
SHIFTS = (0, 1, -1, 2)
VM = pl.BlockSpec(memory_space=pltpu.VMEM)
SM = pl.BlockSpec(memory_space=pltpu.SMEM)
HB = pl.BlockSpec(memory_space=pl.ANY)
MIB = 1024 * 1024


def take(shard, axis, by):
    count = lax.axis_size(axis)
    return lax.ppermute(shard, axis, [((i + by) % count, i) for i in range(count)])


def give(shard, axis, by):
    count = lax.axis_size(axis)
    return lax.ppermute(shard, axis, [(i, (i + by) % count) for i in range(count)])


def call(body, out, name, ins, scratch=(), cost=(0, 0), **extra):
    return pl.pallas_call(
        body,
        out_shape=out,
        scratch_shapes=list(scratch),
        name=name,
        cost_estimate=pl.CostEstimate(flops=cost[0], bytes_accessed=cost[1], transcendentals=0),
        compiler_params=pltpu.CompilerParams(vmem_limit_bytes=48 * MIB),
        **extra,
    )(*ins)


def shape(*sizes, dtype=BF16):
    return jax.ShapeDtypeStruct(sizes, dtype)


def bands_kernel(base, out):
    groups, width = base.shape
    taps = width // 2
    for g in range(groups):
        row = jnp.broadcast_to(base[g : g + 1, :], (taps, width))
        out[g * taps : (g + 1) * taps, :] = pltpu.roll(
            row, 0, 1, stride=1, stride_axis=0
        ).astype(BF16)


def three_taps(work, taps, stream, rows):
    return (
        taps[stream : stream + 1, :] * work[8 : 8 + rows, :]
        + taps[3 + stream : 4 + stream, :] * work[7 : 7 + rows, :]
        + taps[6 + stream : 7 + stream, :] * work[6 : 6 + rows, :]
    )


def project_kernel(first, last, steps, tile, place, *refs):
    pieces = refs[:8]
    weight = refs[8]
    at = 9
    if not first:
        before = refs[at]
        at += 1
    if last:
        taps = refs[at]
        out, edge, rows, total, work = refs[at + 1 :]
    else:
        out, rows, total = refs[at:]
    step = pl.program_id(0)

    @pl.when(step == 0)
    def _():
        for n, shift in enumerate(SHIFTS):
            for c in range(2):
                z = lax.rem(place[0] + shift + 4, 4)
                core = place[1] if c == 0 else 1 - place[1]
                row = pl.multiple_of(z * 64 + core * 32, 32)
                for k in range(steps):
                    rows[k, pl.ds(row, 32), :] = pieces[2 * n + c][:, k * tile : (k + 1) * tile]
        if first:
            total[...] = jnp.zeros_like(total)
        else:
            total[...] = before[...]

    left = rows[step]
    for s in range(3):
        total[:, s * 512 : (s + 1) * 512] += jnp.dot(
            left, weight[s], preferred_element_type=F32
        )

    @pl.when(step == steps - 1)
    def _():
        if not last:
            out[...] = total[...]
        else:
            projected = total[...].astype(BF16)
            out[...] = projected
            streams = []
            for s in (1, 2):
                work[...] = projected[112:256, s * 512 : (s + 1) * 512].astype(F32)[8:, :]
                streams.append(three_taps(work, taps, s, 128))
            edge[0:128, :] = (streams[0] * streams[1]).astype(BF16)
            for s in range(3):
                edge[128 + 16 * s : 144 + 16 * s, :] = projected[
                    240:256, s * 512 : (s + 1) * 512
                ]


def project(place, pieces, weight, chunk, chunks, before, taps):
    depth = weight.shape[1] // chunks
    tile = 512
    steps = depth // tile
    first, last = chunk == 0, chunk == chunks - 1
    ins = [place, *pieces, weight]
    specs = [SM] + [pl.BlockSpec((32, depth), lambda k: (0, 0))] * 8
    specs.append(pl.BlockSpec((3, tile, 512), lambda k: (0, k + chunk * steps, 0)))
    if not first:
        ins.append(before)
        specs.append(pl.BlockSpec((256, 1536), lambda k: (0, 0)))
    scratch = [pltpu.VMEM((steps, 256, tile), BF16), pltpu.VMEM((256, 1536), F32)]
    if last:
        ins.append(taps)
        specs.append(pl.BlockSpec((9, 512), lambda k: (0, 0)))
        out = (shape(256, 1536), shape(176, 512))
        out_specs = (
            pl.BlockSpec((256, 1536), lambda k: (0, 0)),
            pl.BlockSpec((176, 512), lambda k: (0, 0)),
        )
        scratch.append(pltpu.VMEM((136, 512), F32))
    else:
        out = shape(256, 1536, dtype=F32)
        out_specs = pl.BlockSpec((256, 1536), lambda k: (0, 0))
    return call(
        functools.partial(project_kernel, first, last, steps, tile),
        out,
        "project",
        ins,
        scratch,
        (2 * 256 * depth * 1536, depth * 3072 + 4 * MIB),
        grid=(steps,),
        in_specs=specs,
        out_specs=out_specs,
    )


def mix_kernel(projected, edge, taps, bias, bands, out, work, window, query):
    streams = []
    for s in range(3):
        work[0:8, :] = edge[128 + 16 * s : 144 + 16 * s, :].astype(F32)[8:16, :]
        work[8:264, :] = projected[:, s * 512 : (s + 1) * 512].astype(F32)
        featured = three_taps(work, taps, s, 256)
        if s == 0:
            query[...] = featured
        else:
            streams.append(featured)
    product = (streams[0] * streams[1]).astype(BF16)
    window[0:128, :] = edge[0:128, :]
    window[128:384, :] = product
    lane = lax.broadcasted_iota(jnp.int32, (128, 128), 1) // 16
    for j in range(4):
        columns = slice(j * 128, (j + 1) * 128)
        right = jnp.concatenate([window[0:256, columns], window[128:384, columns]], axis=1)
        result = jnp.dot(
            bands[j * 1024 : (j + 1) * 1024, :], right, preferred_element_type=F32
        )
        for block in range(2):
            filtered = jnp.zeros((128, 128), F32)
            for g in range(8):
                filtered = jnp.where(
                    lane == g,
                    result[g * 128 : (g + 1) * 128, block * 128 : (block + 1) * 128],
                    filtered,
                )
            rows = slice(block * 128, (block + 1) * 128)
            direct = window[128 + block * 128 : 256 + block * 128, columns].astype(F32)
            out[rows, columns] = (
                query[rows, columns] * (filtered + bias[:, columns] * direct)
            ).astype(BF16)


def out_kernel(place, own, partner, weight, o0, o1, o2, o3, left, held, sems):
    copies = []
    for n in range(16):
        copy = pltpu.make_async_copy(
            weight.at[n], held.at[n // 2, :, pl.ds((n % 2) * 128, 128)], sems.at[n]
        )
        copy.start()
        copies.append(copy)
    outs = (o0, o1, o2, o3)
    for n, shift in enumerate(SHIFTS):
        z = lax.rem(place[0] + shift + 4, 4)
        row = pl.multiple_of(z * 64, 64)
        left[n * 64 : (n + 1) * 64, 0:512] = own[pl.ds(row, 64), :]
        left[n * 64 : (n + 1) * 64, 512:1024] = partner[pl.ds(row, 64), :]
    for j in range(8):
        copies[2 * j].wait()
        copies[2 * j + 1].wait()
        result = jnp.dot(left[...], held[j], preferred_element_type=F32)
        for n in range(4):
            outs[n][:, j * 256 : (j + 1) * 256] = result[n * 64 : (n + 1) * 64].astype(BF16)


def sum_kernel(place, a, b, c, d, keep, send):
    mine = pl.multiple_of(place[1] * 32, 32)
    theirs = pl.multiple_of((1 - place[1]) * 32, 32)
    for out, row in ((keep, mine), (send, theirs)):
        rows = pl.ds(row, 32)
        out[...] = (
            a[rows, :].astype(F32)
            + b[rows, :].astype(F32)
            + c[rows, :].astype(F32)
            + d[rows, :].astype(F32)
        ).astype(BF16)


def place_kernel(place, k0, k1, y0, y1, out):
    for h, (kept, got) in enumerate(((k0, y0), (k1, y1))):
        for c in range(16):
            for source, core in ((kept, place[1]), (got, 1 - place[1])):
                column = pl.multiple_of(c * 512 + h * 128 + core * 256, 128)
                out[:, pl.ds(column, 128)] = source[:, c * 128 : (c + 1) * 128]


def shards(tokens, in_weight, short_filter, mr_filter, mr_bias, out_weight):
    core = lax.axis_index("core")
    place = jnp.stack([lax.axis_index("z"), core]).astype(jnp.int32)

    mine = lax.dynamic_slice(out_weight, (0, core * 256), (512, 256))
    other = lax.dynamic_slice(out_weight, (0, (1 - core) * 256), (512, 256))
    pair = jnp.concatenate([mine, take(other, "core", 1)], axis=0)
    gathered = [
        lax.all_gather(pair[:, h * 128 : (h + 1) * 128], ("x", "y"), axis=0, tiled=False)
        for h in range(2)
    ]

    reversed_taps = jnp.flip(mr_filter, 0).T
    base = jnp.pad(reversed_taps, ((0, 0), (1, 127)))
    bands = call(
        bands_kernel, shape(4096, 256), "bands", [base], cost=(0, 4 * MIB), in_specs=[VM], out_specs=VM
    )
    taps = short_filter.reshape(9, 512)

    weight = jnp.transpose(in_weight, (1, 0, 2))
    chunks = 2
    depth = tokens.shape[1] // chunks
    pieces = []
    for c in range(chunks):
        part = tokens[:, c * depth : (c + 1) * depth]
        got = [part] + [take(part, "z", by) for by in SHIFTS[1:]]
        pieces.append([q for block in got for q in (block, take(block, "core", 1))])
    total = None
    for c in range(chunks):
        total = project(place, pieces[c], weight, c, chunks, total, taps)
    projected, edge = total

    count = lax.axis_size(("x", "y"))
    earlier = lax.ppermute(edge, ("x", "y"), [(i, i + 1) for i in range(count - 1)])
    gated = call(
        mix_kernel,
        shape(256, 512),
        "mix",
        [projected, earlier, taps, mr_bias.reshape(1, 512), bands],
        [pltpu.VMEM((264, 512), F32), pltpu.VMEM((384, 512), BF16), pltpu.VMEM((256, 512), F32)],
        (2 * 4096 * 256 * 256, 4 * MIB),
        in_specs=[VM] * 5,
        out_specs=VM,
    )
    partner = take(gated, "core", 1)

    kept, got = [], []
    for h in range(2):
        partials = call(
            out_kernel,
            (shape(64, 2048),) * 4,
            "out",
            [place, gated, partner, gathered[h]],
            [
                pltpu.VMEM((256, 1024), BF16),
                pltpu.VMEM((8, 1024, 256), BF16),
                pltpu.SemaphoreType.DMA((16,)),
            ],
            (2 * 256 * 1024 * 2048, 6 * MIB),
            in_specs=[SM, VM, VM, HB],
            out_specs=(VM,) * 4,
        )
        arrived = [give(partials[n], "z", SHIFTS[n]) for n in range(1, 4)]
        keep, send = call(
            sum_kernel,
            (shape(32, 2048),) * 2,
            "sum",
            [place, partials[0], *arrived],
            cost=(0, 2 * MIB),
            in_specs=[SM] + [VM] * 4,
            out_specs=(VM, VM),
        )
        kept.append(keep)
        got.append(take(send, "core", 1))
    return call(
        place_kernel,
        shape(32, 8192),
        "place",
        [place, *kept, *got],
        cost=(0, MIB),
        in_specs=[SM] + [VM] * 4,
        out_specs=VM,
    )


def solution(mesh):
    grid = Mesh(mesh.devices.reshape(4, 4, 4, 2), ("x", "y", "z", "core"))
    channels = ("z", "core")
    context = ("x", "y")
    return jax.shard_map(
        shards,
        mesh=grid,
        in_specs=(
            P(context + channels, None),
            P(None, None, channels),
            P(None, None, channels),
            P(None, channels),
            P(channels),
            P(channels, context),
        ),
        out_specs=P(context + channels, None),
        check_vma=False,
    )
```

time: 177 us -> 152 us (0.86)
  matrix products: 40.1 us -> 0 us
  Pallas kernels: 0 us -> 33.2 us
  local copies, waits for them, and re-layouts: 35.3 us -> 7.58 us
  starting transfers between devices: 5.64 us -> 25.2 us
  waiting for transfers between devices: 75.7 us -> 70.3 us
  other arithmetic: 6.08 us -> 0.92 us
    dot_general x6 -> x0, matrix products: 40.1 us -> none  [the longest x1 13.4 us: shards(): jnp.dot(lax.all_gather(tokens, 'tp', axis=0, tiled=True), flat_weight, pr...]
    reduce_scatter x1 -> x0, waiting for transfers between devices: 38.1 us -> none  [shards(): lax.psum_scatter(partial_sum.astype(jnp.bfloat16), 'tp', scatter_dimensio...]
    pallas_call x0 -> x9, Pallas kernels: none -> 33.2 us  [call(): pl.pallas_call(body, out_shape=out, scratch_shapes=list(scratch), name=na...]
    ppermute x2 -> x25, waiting for transfers between devices: 4.86 us -> 37.6 us  [the longest x18 20.8 us: take(): lax.ppermute(shard, axis, [((i + by) % count, i) for i in range(count)])]
    unnamed x11 -> x8, local copies, waits for them, and re-layouts: 33.4 us -> 4.55 us
    ppermute x2 -> x25, starting transfers between devices: 5.56 us -> 25.1 us  [the longest x18 12.4 us: take(): lax.ppermute(shard, axis, [((i + by) % count, i) for i in range(count)])]
    eq x2 -> x0, other arithmetic: 3.83 us -> none  [the longest x1 2.58 us: convolve(): near_mask = (offsets == lag_table).astype(jnp.float32)]
  transfers between devices with their start and end apart: 5 -> 27, of which waited for: 4 -> 13; matrix products, arithmetic and copies ran while one was open for 42% -> 1% of each run, Pallas kernels for 0% -> 21%
where the time goes in v1:
time: 152 us; the launch traced here: 151 us
  waiting for transfers between devices  70.3 us (46%)
  Pallas kernels  33.2 us (22%)
  starting transfers between devices  25.2 us (17%)
  between operations  13.6 us (9%)
  local copies, waits for them, and re-layouts  7.58 us (5%)
    pallas_call x9, Pallas kernels, call(): pl.pallas_call(body, out_shape=out, scratch_shapes=list(scratch), name=na...  33.2 us
    all_gather x2, waiting for transfers between devices, shards(): lax.all_gather(pair[:, h * 128:(h + 1) * 128], ('x', 'y'), axis=0, tiled=...  31.9 us
    ppermute x18, waiting for transfers between devices, take(): lax.ppermute(shard, axis, [((i + by) % count, i) for i in range(count)])  20.8 us
    ppermute x18, starting transfers between devices, take(): lax.ppermute(shard, axis, [((i + by) % count, i) for i in range(count)])  12.4 us
    ppermute x6, waiting for transfers between devices, give(): lax.ppermute(shard, axis, [(i, (i + by) % count) for i in range(count)])  10.1 us
    ppermute x6, starting transfers between devices, give(): lax.ppermute(shard, axis, [(i, (i + by) % count) for i in range(count)])  9.23 us
    ppermute x1, waiting for transfers between devices, shards(): lax.ppermute(edge, ('x', 'y'), [(i, i + 1) for i in range(count - 1)])  6.69 us
    unnamed x8, local copies, waits for them, and re-layouts  4.55 us
  transfers between devices with their start and end apart: 27, of which 13 were waited for; matrix products, arithmetic and copies ran while one was open for 1% of the time, Pallas kernels for 21%

profile of v1, /device:TPU:2, one launch (start us, length us, event | category | flops | bytes accessed | tf_op | source)
XLA Modules:
  0.0 150.8 jit_solution(8871772805216080739)
XLA Ops:
  6.5 1.1 constant_dynamic-slice_fusion
  7.6 0.1 collective-permute-start.16
  7.7 1.5 %collective-permute-done.16 = bf16[512,256]{1,0:T(8,128)(2,1)S(1)} collective-permute-done((bf16[512,256]{1,0:T(8,128)(2,1)S(1)}, bf16[512,256]{1,0:T(8,128)(2,1)S(1)}, u32[]{:S(2)}, u32[]{:S(2)}) %collective-permute-start.16) | collective-permute-done | bytes 262176 | tf_op jit(solution)/shard_map/ppermute | solution.py:21
  9.2 0.8 pad_maximum_fusion
  10.1 0.0 all-gather.7.cloned.1.call-update
  10.1 0.0 all-gather.5.cloned.1.call-start
  10.1 0.7 all-gather.5.cloned.1.call-update
  10.8 1.1 fusion.1
  11.9 2.0 %collective-permute-start.10 = (bf16[32,4096]{1,0:T(8,128)(2,1)S(1)}, bf16[32,4096]{1,0:T(8,128)(2,1)S(1)}, u32[]{:S(2)}, u32[]{:S(2)}) collective-permute-start(bf16[32,4096]{1,0:T(8,128)(2,1)S(1)} %get-tuple-element.37.refs_0_), channel_id=1, source_target_pairs={{6,0},{0,2},{2,4},{4,6},{7,1},{1,3},{3,5},{5,7},{14,8},{8,10},{10,... | collective-permute-start | bytes 786440 | tf_op jit(solution)/shard_map/ppermute | solution.py:21
  13.9 3.6 %collective-permute-start.12 = (bf16[32,4096]{1,0:T(8,128)(2,1)S(1)}, bf16[32,4096]{1,0:T(8,128)(2,1)S(1)}, u32[]{:S(2)}, u32[]{:S(2)}) collective-permute-start(bf16[32,4096]{1,0:T(8,128)(2,1)S(1)} %get-tuple-element.37.refs_0_), channel_id=1, source_target_pairs={{4,0},{6,2},{0,4},{2,6},{5,1},{7,3},{1,5},{3,7},{12,8},{14,10},{8,... | collective-permute-start | bytes 786440 | tf_op jit(solution)/shard_map/ppermute | solution.py:21
  17.5 1.0 collective-permute-start.8
  18.5 0.0 collective-permute-start.1
  18.5 4.1 %collective-permute-done.10.refs_4_ = bf16[32,4096]{1,0:T(8,128)(2,1)S(1)} collective-permute-done((bf16[32,4096]{1,0:T(8,128)(2,1)S(1)}, bf16[32,4096]{1,0:T(8,128)(2,1)S(1)}, u32[]{:S(2)}, u32[]{:S(2)}) %collective-permute-start.10) | collective-permute-done | bytes 262176 | tf_op jit(solution)/shard_map/ppermute | solution.py:21
  22.6 4.4 %collective-permute-start.3 = (bf16[32,4096]{1,0:T(8,128)(2,1)S(1)}, bf16[32,4096]{1,0:T(8,128)(2,1)S(1)}, u32[]{:S(2)}, u32[]{:S(2)}) collective-permute-start(bf16[32,4096]{1,0:T(8,128)(2,1)S(1)} %get-tuple-element.38.refs_0_), channel_id=1, source_target_pairs={{6,0},{0,2},{2,4},{4,6},{7,1},{1,3},{3,5},{5,7},{14,8},{8,10},{10,... | collective-permute-start | bytes 786440 | tf_op jit(solution)/shard_map/ppermute | solution.py:21
  27.0 3.3 %collective-permute-done.12.refs_6_ = bf16[32,4096]{1,0:T(8,128)(2,1)S(1)} collective-permute-done((bf16[32,4096]{1,0:T(8,128)(2,1)S(1)}, bf16[32,4096]{1,0:T(8,128)(2,1)S(1)}, u32[]{:S(2)}, u32[]{:S(2)}) %collective-permute-start.12) | collective-permute-done | bytes 262176 | tf_op jit(solution)/shard_map/ppermute | solution.py:21
  30.3 0.0 collective-permute-start.5
  30.3 0.0 collective-permute-done.8.refs_2_
  30.3 0.0 collective-permute-start.11
  30.3 0.5 collective-permute-start.13
  30.8 4.6 %collective-permute-done.1.refs_2_ = bf16[32,4096]{1,0:T(8,128)(2,1)S(1)} collective-permute-done((bf16[32,4096]{1,0:T(8,128)(2,1)S(1)}, bf16[32,4096]{1,0:T(8,128)(2,1)S(1)}, u32[]{:S(2)}, u32[]{:S(2)}) %collective-permute-start.1) | collective-permute-done | bytes 262176 | tf_op jit(solution)/shard_map/ppermute | solution.py:21
  35.4 0.0 collective-permute-start.9
  35.4 0.8 reshape.6.refs_10_.taps
  36.1 0.1 pad_add_fusion.place
  36.2 0.9 collective-permute-done.3.refs_4_
  37.1 0.0 collective-permute-start
  37.1 3.6 %collective-permute-done.5.refs_6_ = bf16[32,4096]{1,0:T(8,128)(2,1)S(1)} collective-permute-done((bf16[32,4096]{1,0:T(8,128)(2,1)S(1)}, bf16[32,4096]{1,0:T(8,128)(2,1)S(1)}, u32[]{:S(2)}, u32[]{:S(2)}) %collective-permute-start.5) | collective-permute-done | bytes 262176 | tf_op jit(solution)/shard_map/ppermute | solution.py:21
  40.7 0.5 collective-permute-start.4
  41.2 0.0 collective-permute-done.13.refs_7_
  41.2 0.1 collective-permute-start.6
  41.3 0.0 collective-permute-done.9.refs_3_
  41.3 9.4 %project.2.refs_9_ = f32[256,1536]{1,0:T(8,128)S(1)} custom-call(s32[2]{0:T(128)S(1)} %pad_add_fusion.place, bf16[32,4096]{1,0:T(8,128)(2,1)S(1)} %get-tuple-element.37.refs_0_, bf16[32,4096]{1,0:T(8,128)(2,1)S(1)} %collective-permute-done.7.refs_1_, bf16[32,4096]{1,0:T(8,128)(2,1)S(1)} %collective-permute-done.8.refs_2_, ...), custom_call_target="tpu_custom_call" | custom-call | flops 3221225472 | bytes 16777216 | tf_op jit(solution)/shard_map/project/pallas_call | solution.py:30
  50.7 0.0 copy-start.3
  50.7 0.0 copy-start.2
  50.7 0.0 collective-permute-done.4.refs_5_
  50.8 9.7 %project.3 = (bf16[256,1536]{1,0:T(8,128)(2,1)S(1)}, bf16[176,512]{1,0:T(8,128)(2,1)S(1)}) custom-call(s32[2]{0:T(128)S(1)} %pad_add_fusion.place, bf16[32,4096]{1,0:T(8,128)(2,1)S(1)} %get-tuple-element.38.refs_0_, bf16[32,4096]{1,0:T(8,128)(2,1)S(1)} %collective-permute-done.refs_1_, bf16[32,4096]{1,0:T(8,128)(2,1)S(1)} %collective-permute-done.1.refs_2_, ...), custom_call_target="tpu_custom_call" | custom-call | flops 3221225472 | bytes 16777216 | tf_op jit(solution)/shard_map/project/pallas_call | solution.py:30
  60.5 3.5 %collective-permute-start.14 = (bf16[176,512]{1,0:T(8,128)(2,1)S(1)}, bf16[176,512]{1,0:T(8,128)(2,1)S(1)}, u32[]{:S(2)}, u32[]{:S(2)}) collective-permute-start(bf16[176,512]{1,0:T(8,128)(2,1)S(1)} %get-tuple-element.20), channel_id=1, source_target_pairs={{0,8},{8,16},{16,24},{24,32},{32,40},{40,48},{48,56},{56,64},{64,7... | collective-permute-start | bytes 540680 | tf_op jit(solution)/shard_map/ppermute | solution.py:263
  64.0 0.1 rev.4
  64.1 0.1 pad.4.base
  64.2 0.6 bands.1
  64.8 6.7 %collective-permute-done.14.edge = bf16[176,512]{1,0:T(8,128)(2,1)S(1)} collective-permute-done((bf16[176,512]{1,0:T(8,128)(2,1)S(1)}, bf16[176,512]{1,0:T(8,128)(2,1)S(1)}, u32[]{:S(2)}, u32[]{:S(2)}) %collective-permute-start.14) | collective-permute-done | bytes 180256 | tf_op jit(solution)/shard_map/ppermute | solution.py:263
  71.5 1.1 mix.1.own
  72.6 0.1 collective-permute-start.15
  72.7 1.5 %collective-permute-done.15.partner = bf16[256,512]{1,0:T(8,128)(2,1)S(1)} collective-permute-done((bf16[256,512]{1,0:T(8,128)(2,1)S(1)}, bf16[256,512]{1,0:T(8,128)(2,1)S(1)}, u32[]{:S(2)}, u32[]{:S(2)}) %collective-permute-start.15) | collective-permute-done | bytes 262176 | tf_op jit(solution)/shard_map/ppermute | solution.py:21
  74.2 2.3 %copy-done.1 = bf16[16384,128]{1,0:T(8,128)(2,1)S(1)} copy-done((bf16[16384,128]{1,0:T(8,128)(2,1)S(1)}, bf16[16384,128]{1,0:T(8,128)(2,1)}, u32[]{:S(2)}) %copy-start.1) | copy-done | bytes 4194328
  76.5 4.8 %out.3 = (bf16[64,2048]{1,0:T(8,128)(2,1)S(1)}, bf16[64,2048]{1,0:T(8,128)(2,1)S(1)}, bf16[64,2048]{1,0:T(8,128)(2,1)S(1)}, bf16[64,2048]{1,0:T(8,128)(2,1)S(1)}) custom-call(s32[2]{0:T(128)S(1)} %pad_add_fusion.place, bf16[256,512]{1,0:T(8,128)(2,1)S(1)} %mix.1.own, bf16[256,512]{1,0:T(8,128)(2,1)S(1)} %collective-permute-done.15.partner, ...), custom_call_target="tpu_custom_call" | custom-call | flops 1073741824 | bytes 6291456 | tf_op jit(solution)/shard_map/out/pallas_call | solution.py:30
  81.4 1.7 %collective-permute-start.20 = (bf16[64,2048]{1,0:T(8,128)(2,1)S(1)}, bf16[64,2048]{1,0:T(8,128)(2,1)S(1)}, u32[]{:S(2)}, u32[]{:S(2)}) collective-permute-start(bf16[64,2048]{1,0:T(8,128)(2,1)S(1)} %get-tuple-element.27), channel_id=1, source_target_pairs={{0,2},{2,4},{4,6},{6,0},{1,3},{3,5},{5,7},{7,1},{8,10},{10,12},{12... | collective-permute-start | bytes 786440 | tf_op jit(solution)/shard_map/ppermute | solution.py:26
  83.0 1.7 %collective-permute-start.21 = (bf16[64,2048]{1,0:T(8,128)(2,1)S(1)}, bf16[64,2048]{1,0:T(8,128)(2,1)S(1)}, u32[]{:S(2)}, u32[]{:S(2)}) collective-permute-start(bf16[64,2048]{1,0:T(8,128)(2,1)S(1)} %get-tuple-element.28), channel_id=1, source_target_pairs={{0,6},{2,0},{4,2},{6,4},{1,7},{3,1},{5,3},{7,5},{8,14},{10,8},{12,... | collective-permute-start | bytes 786440 | tf_op jit(solution)/shard_map/ppermute | solution.py:26
  84.7 0.7 collective-permute-start.22
  85.3 31.9 %all-gather.5.cloned.1.call-done = bf16[16384,128]{1,0:T(8,128)(2,1)} async-done(((bf16[1024,128]{1,0:T(8,128)(2,1)}), bf16[16384,128]{1,0:T(8,128)(2,1)}) %all-gather.5.cloned.1.call-update) | async-done | bytes 4194320 | tf_op jit(solution)/shard_map/all_gather | solution.py:238
  117.3 2.2 %copy-done = bf16[16384,128]{1,0:T(8,128)(2,1)S(1)} copy-done((bf16[16384,128]{1,0:T(8,128)(2,1)S(1)}, bf16[16384,128]{1,0:T(8,128)(2,1)}, u32[]{:S(2)}) %copy-start) | copy-done | bytes 4194328
  119.5 4.8 %out.2 = (bf16[64,2048]{1,0:T(8,128)(2,1)S(1)}, bf16[64,2048]{1,0:T(8,128)(2,1)S(1)}, bf16[64,2048]{1,0:T(8,128)(2,1)S(1)}, bf16[64,2048]{1,0:T(8,128)(2,1)S(1)}) custom-call(s32[2]{0:T(128)S(1)} %pad_add_fusion.place, bf16[256,512]{1,0:T(8,128)(2,1)S(1)} %mix.1.own, bf16[256,512]{1,0:T(8,128)(2,1)S(1)} %collective-permute-done.15.partner, ...), custom_call_target="tpu_custom_call" | custom-call | flops 1073741824 | bytes 6291456 | tf_op jit(solution)/shard_map/out/pallas_call | solution.py:30
  124.3 1.6 %collective-permute-start.17 = (bf16[64,2048]{1,0:T(8,128)(2,1)S(1)}, bf16[64,2048]{1,0:T(8,128)(2,1)S(1)}, u32[]{:S(2)}, u32[]{:S(2)}) collective-permute-start(bf16[64,2048]{1,0:T(8,128)(2,1)S(1)} %get-tuple-element.22), channel_id=1, source_target_pairs={{0,2},{2,4},{4,6},{6,0},{1,3},{3,5},{5,7},{7,1},{8,10},{10,12},{12... | collective-permute-start | bytes 786440 | tf_op jit(solution)/shard_map/ppermute | solution.py:26
  125.9 1.7 %collective-permute-start.18 = (bf16[64,2048]{1,0:T(8,128)(2,1)S(1)}, bf16[64,2048]{1,0:T(8,128)(2,1)S(1)}, u32[]{:S(2)}, u32[]{:S(2)}) collective-permute-start(bf16[64,2048]{1,0:T(8,128)(2,1)S(1)} %get-tuple-element.23), channel_id=1, source_target_pairs={{0,6},{2,0},{4,2},{6,4},{1,7},{3,1},{5,3},{7,5},{8,14},{10,8},{12,... | collective-permute-start | bytes 786440 | tf_op jit(solution)/shard_map/ppermute | solution.py:26
  127.6 1.9 %collective-permute-start.19 = (bf16[64,2048]{1,0:T(8,128)(2,1)S(1)}, bf16[64,2048]{1,0:T(8,128)(2,1)S(1)}, u32[]{:S(2)}, u32[]{:S(2)}) collective-permute-start(bf16[64,2048]{1,0:T(8,128)(2,1)S(1)} %get-tuple-element.24), channel_id=1, source_target_pairs={{0,4},{2,6},{4,0},{6,2},{1,5},{3,7},{5,1},{7,3},{8,12},{10,14},{12... | collective-permute-start | bytes 786440 | tf_op jit(solution)/shard_map/ppermute | solution.py:26
  129.6 0.0 collective-permute-done.21.c
  129.6 0.7 sum.3
  130.3 0.1 collective-permute-start.24
  130.4 3.3 %collective-permute-done.17.b = bf16[64,2048]{1,0:T(8,128)(2,1)S(1)} collective-permute-done((bf16[64,2048]{1,0:T(8,128)(2,1)S(1)}, bf16[64,2048]{1,0:T(8,128)(2,1)S(1)}, u32[]{:S(2)}, u32[]{:S(2)}) %collective-permute-start.17) | collective-permute-done | bytes 262176 | tf_op jit(solution)/shard_map/ppermute | solution.py:26
  133.6 5.0 %collective-permute-done.18.c = bf16[64,2048]{1,0:T(8,128)(2,1)S(1)} collective-permute-done((bf16[64,2048]{1,0:T(8,128)(2,1)S(1)}, bf16[64,2048]{1,0:T(8,128)(2,1)S(1)}, u32[]{:S(2)}, u32[]{:S(2)}) %collective-permute-start.18) | collective-permute-done | bytes 262176 | tf_op jit(solution)/shard_map/ppermute | solution.py:26
  138.6 1.8 %collective-permute-done.19.d = bf16[64,2048]{1,0:T(8,128)(2,1)S(1)} collective-permute-done((bf16[64,2048]{1,0:T(8,128)(2,1)S(1)}, bf16[64,2048]{1,0:T(8,128)(2,1)S(1)}, u32[]{:S(2)}, u32[]{:S(2)}) %collective-permute-start.19) | collective-permute-done | bytes 262176 | tf_op jit(solution)/shard_map/ppermute | solution.py:26
  140.4 0.7 sum.2
  141.1 0.1 collective-permute-start.23
  141.2 1.3 collective-permute-done.23.y0
  142.5 1.4 place.1
  (16 shorter events, 0.0 us)
Async XLA Ops:
  6.5 67.6 %all-gather.7.cloned.1.call-start = ((), (), s32[]{:S(2)}) async-start(), calls=%async_computation.1 | async-start | bytes 4456448 | tf_op jit(solution)/shard_map/all_gather | solution.py:238
  7.6 1.6 %collective-permute-start.16 = (bf16[512,256]{1,0:T(8,128)(2,1)S(1)}, bf16[512,256]{1,0:T(8,128)(2,1)S(1)}, u32[]{:S(2)}, u32[]{:S(2)}) collective-permute-start(bf16[512,256]{1,0:T(8,128)(2,1)S(1)} %get-tuple-element.35), channel_id=1, source_target_pairs={{1,0},{0,1},{3,2},{2,3},{5,4},{4,5},{7,6},{6,7},{9,8},{8,9},{11,10... | collective-permute-start | bytes 786440 | tf_op jit(solution)/shard_map/ppermute | solution.py:21
  10.1 107.2 %all-gather.5.cloned.1.call-start = ((), (), s32[]{:S(2)}) async-start(), calls=%async_computation | async-start | bytes 4456448 | tf_op jit(solution)/shard_map/all_gather | solution.py:238
  11.9 10.7 %collective-permute-start.10 = (bf16[32,4096]{1,0:T(8,128)(2,1)S(1)}, bf16[32,4096]{1,0:T(8,128)(2,1)S(1)}, u32[]{:S(2)}, u32[]{:S(2)}) collective-permute-start(bf16[32,4096]{1,0:T(8,128)(2,1)S(1)} %get-tuple-element.37.refs_0_), channel_id=1, source_target_pairs={{6,0},{0,2},{2,4},{4,6},{7,1},{1,3},{3,5},{5,7},{14,8},{8,10},{10,... | collective-permute-start | bytes 786440 | tf_op jit(solution)/shard_map/ppermute | solution.py:21
  13.9 16.4 %collective-permute-start.12 = (bf16[32,4096]{1,0:T(8,128)(2,1)S(1)}, bf16[32,4096]{1,0:T(8,128)(2,1)S(1)}, u32[]{:S(2)}, u32[]{:S(2)}) collective-permute-start(bf16[32,4096]{1,0:T(8,128)(2,1)S(1)} %get-tuple-element.37.refs_0_), channel_id=1, source_target_pairs={{4,0},{6,2},{0,4},{2,6},{5,1},{7,3},{1,5},{3,7},{12,8},{14,10},{8,... | collective-permute-start | bytes 786440 | tf_op jit(solution)/shard_map/ppermute | solution.py:21
  17.5 12.8 %collective-permute-start.8 = (bf16[32,4096]{1,0:T(8,128)(2,1)S(1)}, bf16[32,4096]{1,0:T(8,128)(2,1)S(1)}, u32[]{:S(2)}, u32[]{:S(2)}) collective-permute-start(bf16[32,4096]{1,0:T(8,128)(2,1)S(1)} %get-tuple-element.37.refs_0_), channel_id=1, source_target_pairs={{2,0},{4,2},{6,4},{0,6},{3,1},{5,3},{7,5},{1,7},{10,8},{12,10},{14... | collective-permute-start | bytes 786440 | tf_op jit(solution)/shard_map/ppermute | solution.py:21
  18.5 11.8 %collective-permute-start.7 = (bf16[32,4096]{1,0:T(8,128)(2,1)S(1)}, bf16[32,4096]{1,0:T(8,128)(2,1)S(1)}, u32[]{:S(2)}, u32[]{:S(2)}) collective-permute-start(bf16[32,4096]{1,0:T(8,128)(2,1)S(1)} %get-tuple-element.37.refs_0_), channel_id=1, source_target_pairs={{1,0},{0,1},{3,2},{2,3},{5,4},{4,5},{7,6},{6,7},{9,8},{8,9},{11,10... | collective-permute-start | bytes 786440 | tf_op jit(solution)/shard_map/ppermute | solution.py:21
  18.5 16.9 %collective-permute-start.1 = (bf16[32,4096]{1,0:T(8,128)(2,1)S(1)}, bf16[32,4096]{1,0:T(8,128)(2,1)S(1)}, u32[]{:S(2)}, u32[]{:S(2)}) collective-permute-start(bf16[32,4096]{1,0:T(8,128)(2,1)S(1)} %get-tuple-element.38.refs_0_), channel_id=1, source_target_pairs={{2,0},{4,2},{6,4},{0,6},{3,1},{5,3},{7,5},{1,7},{10,8},{12,10},{14... | collective-permute-start | bytes 786440 | tf_op jit(solution)/shard_map/ppermute | solution.py:21
  22.6 14.5 %collective-permute-start.3 = (bf16[32,4096]{1,0:T(8,128)(2,1)S(1)}, bf16[32,4096]{1,0:T(8,128)(2,1)S(1)}, u32[]{:S(2)}, u32[]{:S(2)}) collective-permute-start(bf16[32,4096]{1,0:T(8,128)(2,1)S(1)} %get-tuple-element.38.refs_0_), channel_id=1, source_target_pairs={{6,0},{0,2},{2,4},{4,6},{7,1},{1,3},{3,5},{5,7},{14,8},{8,10},{10,... | collective-permute-start | bytes 786440 | tf_op jit(solution)/shard_map/ppermute | solution.py:21
  30.3 10.4 %collective-permute-start.5 = (bf16[32,4096]{1,0:T(8,128)(2,1)S(1)}, bf16[32,4096]{1,0:T(8,128)(2,1)S(1)}, u32[]{:S(2)}, u32[]{:S(2)}) collective-permute-start(bf16[32,4096]{1,0:T(8,128)(2,1)S(1)} %get-tuple-element.38.refs_0_), channel_id=1, source_target_pairs={{4,0},{6,2},{0,4},{2,6},{5,1},{7,3},{1,5},{3,7},{12,8},{14,10},{8,... | collective-permute-start | bytes 786440 | tf_op jit(solution)/shard_map/ppermute | solution.py:21
  30.3 10.4 %collective-permute-start.11 = (bf16[32,4096]{1,0:T(8,128)(2,1)S(1)}, bf16[32,4096]{1,0:T(8,128)(2,1)S(1)}, u32[]{:S(2)}, u32[]{:S(2)}) collective-permute-start(bf16[32,4096]{1,0:T(8,128)(2,1)S(1)} %collective-permute-done.10.refs_4_), channel_id=1, source_target_pairs={{1,0},{0,1},{3,2},{2,3},{5,4},{4,5},{7,6},{6,7},{9,8},{8,9},{11,10... | collective-permute-start | bytes 786440 | tf_op jit(solution)/shard_map/ppermute | solution.py:21
  30.3 10.9 %collective-permute-start.13 = (bf16[32,4096]{1,0:T(8,128)(2,1)S(1)}, bf16[32,4096]{1,0:T(8,128)(2,1)S(1)}, u32[]{:S(2)}, u32[]{:S(2)}) collective-permute-start(bf16[32,4096]{1,0:T(8,128)(2,1)S(1)} %collective-permute-done.12.refs_6_), channel_id=1, source_target_pairs={{1,0},{0,1},{3,2},{2,3},{5,4},{4,5},{7,6},{6,7},{9,8},{8,9},{11,10... | collective-permute-start | bytes 786440 | tf_op jit(solution)/shard_map/ppermute | solution.py:21
  35.4 5.9 %collective-permute-start.9 = (bf16[32,4096]{1,0:T(8,128)(2,1)S(1)}, bf16[32,4096]{1,0:T(8,128)(2,1)S(1)}, u32[]{:S(2)}, u32[]{:S(2)}) collective-permute-start(bf16[32,4096]{1,0:T(8,128)(2,1)S(1)} %collective-permute-done.8.refs_2_), channel_id=1, source_target_pairs={{1,0},{0,1},{3,2},{2,3},{5,4},{4,5},{7,6},{6,7},{9,8},{8,9},{11,10... | collective-permute-start | bytes 786440 | tf_op jit(solution)/shard_map/ppermute | solution.py:21
  37.1 13.6 %collective-permute-start = (bf16[32,4096]{1,0:T(8,128)(2,1)S(1)}, bf16[32,4096]{1,0:T(8,128)(2,1)S(1)}, u32[]{:S(2)}, u32[]{:S(2)}) collective-permute-start(bf16[32,4096]{1,0:T(8,128)(2,1)S(1)} %get-tuple-element.38.refs_0_), channel_id=1, source_target_pairs={{1,0},{0,1},{3,2},{2,3},{5,4},{4,5},{7,6},{6,7},{9,8},{8,9},{11,10... | collective-permute-start | bytes 786440 | tf_op jit(solution)/shard_map/ppermute | solution.py:21
  40.7 10.0 %collective-permute-start.2 = (bf16[32,4096]{1,0:T(8,128)(2,1)S(1)}, bf16[32,4096]{1,0:T(8,128)(2,1)S(1)}, u32[]{:S(2)}, u32[]{:S(2)}) collective-permute-start(bf16[32,4096]{1,0:T(8,128)(2,1)S(1)} %collective-permute-done.1.refs_2_), channel_id=1, source_target_pairs={{1,0},{0,1},{3,2},{2,3},{5,4},{4,5},{7,6},{6,7},{9,8},{8,9},{11,10... | collective-permute-start | bytes 786440 | tf_op jit(solution)/shard_map/ppermute | solution.py:21
  40.7 10.0 %collective-permute-start.4 = (bf16[32,4096]{1,0:T(8,128)(2,1)S(1)}, bf16[32,4096]{1,0:T(8,128)(2,1)S(1)}, u32[]{:S(2)}, u32[]{:S(2)}) collective-permute-start(bf16[32,4096]{1,0:T(8,128)(2,1)S(1)} %collective-permute-done.3.refs_4_), channel_id=1, source_target_pairs={{1,0},{0,1},{3,2},{2,3},{5,4},{4,5},{7,6},{6,7},{9,8},{8,9},{11,10... | collective-permute-start | bytes 786440 | tf_op jit(solution)/shard_map/ppermute | solution.py:21
  41.2 9.5 %collective-permute-start.6 = (bf16[32,4096]{1,0:T(8,128)(2,1)S(1)}, bf16[32,4096]{1,0:T(8,128)(2,1)S(1)}, u32[]{:S(2)}, u32[]{:S(2)}) collective-permute-start(bf16[32,4096]{1,0:T(8,128)(2,1)S(1)} %collective-permute-done.5.refs_6_), channel_id=1, source_target_pairs={{1,0},{0,1},{3,2},{2,3},{5,4},{4,5},{7,6},{6,7},{9,8},{8,9},{11,10... | collective-permute-start | bytes 786440 | tf_op jit(solution)/shard_map/ppermute | solution.py:21
  50.7 13.3 %copy-start.3 = (f32[128,32]{0,1:T(8,128)S(1)}, f32[128,32]{0,1:T(8,128)}, u32[]{:S(2)}) copy-start(f32[128,32]{0,1:T(8,128)} %param.9) | copy-start | bytes 49156
  50.7 20.8 %copy-start.2 = (f32[512]{0:T(512)S(1)}, f32[512]{0:T(512)}, u32[]{:S(2)}) copy-start(f32[512]{0:T(512)} %param.10) | copy-start | bytes 6148
  60.5 11.0 %collective-permute-start.14 = (bf16[176,512]{1,0:T(8,128)(2,1)S(1)}, bf16[176,512]{1,0:T(8,128)(2,1)S(1)}, u32[]{:S(2)}, u32[]{:S(2)}) collective-permute-start(bf16[176,512]{1,0:T(8,128)(2,1)S(1)} %get-tuple-element.20), channel_id=1, source_target_pairs={{0,8},{8,16},{16,24},{24,32},{32,40},{40,48},{48,56},{56,64},{64,7... | collective-permute-start | bytes 540680 | tf_op jit(solution)/shard_map/ppermute | solution.py:263
  72.6 1.6 %collective-permute-start.15 = (bf16[256,512]{1,0:T(8,128)(2,1)S(1)}, bf16[256,512]{1,0:T(8,128)(2,1)S(1)}, u32[]{:S(2)}, u32[]{:S(2)}) collective-permute-start(bf16[256,512]{1,0:T(8,128)(2,1)S(1)} %mix.1.own), channel_id=1, source_target_pairs={{1,0},{0,1},{3,2},{2,3},{5,4},{4,5},{7,6},{6,7},{9,8},{8,9},{11,10... | collective-permute-start | bytes 786440 | tf_op jit(solution)/shard_map/ppermute | solution.py:21
  74.2 2.4 %copy-start.1 = (bf16[16384,128]{1,0:T(8,128)(2,1)S(1)}, bf16[16384,128]{1,0:T(8,128)(2,1)}, u32[]{:S(2)}) copy-start(bf16[16384,128]{1,0:T(8,128)(2,1)} %all-gather.7.cloned.1.call-done) | copy-start | bytes 12582916
  81.4 46.3 %collective-permute-start.20 = (bf16[64,2048]{1,0:T(8,128)(2,1)S(1)}, bf16[64,2048]{1,0:T(8,128)(2,1)S(1)}, u32[]{:S(2)}, u32[]{:S(2)}) collective-permute-start(bf16[64,2048]{1,0:T(8,128)(2,1)S(1)} %get-tuple-element.27), channel_id=1, source_target_pairs={{0,2},{2,4},{4,6},{6,0},{1,3},{3,5},{5,7},{7,1},{8,10},{10,12},{12... | collective-permute-start | bytes 786440 | tf_op jit(solution)/shard_map/ppermute | solution.py:26
  83.0 46.6 %collective-permute-start.21 = (bf16[64,2048]{1,0:T(8,128)(2,1)S(1)}, bf16[64,2048]{1,0:T(8,128)(2,1)S(1)}, u32[]{:S(2)}, u32[]{:S(2)}) collective-permute-start(bf16[64,2048]{1,0:T(8,128)(2,1)S(1)} %get-tuple-element.28), channel_id=1, source_target_pairs={{0,6},{2,0},{4,2},{6,4},{1,7},{3,1},{5,3},{7,5},{8,14},{10,8},{12,... | collective-permute-start | bytes 786440 | tf_op jit(solution)/shard_map/ppermute | solution.py:26
  84.7 44.9 %collective-permute-start.22 = (bf16[64,2048]{1,0:T(8,128)(2,1)S(1)}, bf16[64,2048]{1,0:T(8,128)(2,1)S(1)}, u32[]{:S(2)}, u32[]{:S(2)}) collective-permute-start(bf16[64,2048]{1,0:T(8,128)(2,1)S(1)} %get-tuple-element.29), channel_id=1, source_target_pairs={{0,4},{2,6},{4,0},{6,2},{1,5},{3,7},{5,1},{7,3},{8,12},{10,14},{12... | collective-permute-start | bytes 786440 | tf_op jit(solution)/shard_map/ppermute | solution.py:26
  117.3 2.2 %copy-start = (bf16[16384,128]{1,0:T(8,128)(2,1)S(1)}, bf16[16384,128]{1,0:T(8,128)(2,1)}, u32[]{:S(2)}) copy-start(bf16[16384,128]{1,0:T(8,128)(2,1)} %all-gather.5.cloned.1.call-done) | copy-start | bytes 12582916
  124.3 9.3 %collective-permute-start.17 = (bf16[64,2048]{1,0:T(8,128)(2,1)S(1)}, bf16[64,2048]{1,0:T(8,128)(2,1)S(1)}, u32[]{:S(2)}, u32[]{:S(2)}) collective-permute-start(bf16[64,2048]{1,0:T(8,128)(2,1)S(1)} %get-tuple-element.22), channel_id=1, source_target_pairs={{0,2},{2,4},{4,6},{6,0},{1,3},{3,5},{5,7},{7,1},{8,10},{10,12},{12... | collective-permute-start | bytes 786440 | tf_op jit(solution)/shard_map/ppermute | solution.py:26
  125.9 12.7 %collective-permute-start.18 = (bf16[64,2048]{1,0:T(8,128)(2,1)S(1)}, bf16[64,2048]{1,0:T(8,128)(2,1)S(1)}, u32[]{:S(2)}, u32[]{:S(2)}) collective-permute-start(bf16[64,2048]{1,0:T(8,128)(2,1)S(1)} %get-tuple-element.23), channel_id=1, source_target_pairs={{0,6},{2,0},{4,2},{6,4},{1,7},{3,1},{5,3},{7,5},{8,14},{10,8},{12,... | collective-permute-start | bytes 786440 | tf_op jit(solution)/shard_map/ppermute | solution.py:26
  127.6 12.8 %collective-permute-start.19 = (bf16[64,2048]{1,0:T(8,128)(2,1)S(1)}, bf16[64,2048]{1,0:T(8,128)(2,1)S(1)}, u32[]{:S(2)}, u32[]{:S(2)}) collective-permute-start(bf16[64,2048]{1,0:T(8,128)(2,1)S(1)} %get-tuple-element.24), channel_id=1, source_target_pairs={{0,4},{2,6},{4,0},{6,2},{1,5},{3,7},{5,1},{7,3},{8,12},{10,14},{12... | collective-permute-start | bytes 786440 | tf_op jit(solution)/shard_map/ppermute | solution.py:26
  130.3 11.0 %collective-permute-start.24 = (bf16[32,2048]{1,0:T(8,128)(2,1)S(1)}, bf16[32,2048]{1,0:T(8,128)(2,1)S(1)}, u32[]{:S(2)}, u32[]{:S(2)}) collective-permute-start(bf16[32,2048]{1,0:T(8,128)(2,1)S(1)} %get-tuple-element.32), channel_id=1, source_target_pairs={{1,0},{0,1},{3,2},{2,3},{5,4},{4,5},{7,6},{6,7},{9,8},{8,9},{11,10... | collective-permute-start | bytes 393224 | tf_op jit(solution)/shard_map/ppermute | solution.py:21
  141.1 1.4 collective-permute-start.23
Sparse Core Ops, SparseCore 0:
  10.2 53.7 all-gather.6
  66.1 51.1 all-gather.4

commit v2 on v1

v2 whole, which is shorter than its diff:
```python
import functools

import jax
import jax.numpy as jnp
from jax import lax
from jax.experimental import pallas as pl
from jax.experimental.pallas import tpu as pltpu
from jax.sharding import Mesh, PartitionSpec as P

F32 = jnp.float32
BF16 = jnp.bfloat16
SHIFTS = (0, 1, -1, 2)
VM = pl.BlockSpec(memory_space=pltpu.VMEM)
SM = pl.BlockSpec(memory_space=pltpu.SMEM)
HB = pl.BlockSpec(memory_space=pltpu.MemorySpace.HBM)
MIB = 1024 * 1024


def take(shard, axis, by):
    count = lax.axis_size(axis)
    return lax.ppermute(shard, axis, [((i + by) % count, i) for i in range(count)])


def give(shard, axis, by):
    count = lax.axis_size(axis)
    return lax.ppermute(shard, axis, [(i, (i + by) % count) for i in range(count)])


def step(shard, axis, by=1):
    count = lax.axis_size(axis)
    pairs = []
    for i in range(count):
        for core in range(2):
            source = (i + (by if core == 0 else -by)) % count
            pairs.append((source * 2 + core, i * 2 + core))
    return lax.ppermute(shard, (axis, "core"), pairs)


def call(body, out, name, ins, scratch=(), cost=(0, 0), room=8, **extra):
    return pl.pallas_call(
        body,
        out_shape=out,
        scratch_shapes=list(scratch),
        name=name,
        cost_estimate=pl.CostEstimate(flops=cost[0], bytes_accessed=cost[1], transcendentals=0),
        compiler_params=pltpu.CompilerParams(vmem_limit_bytes=room * MIB),
        **extra,
    )(*ins)


def shape(*sizes, dtype=BF16):
    return jax.ShapeDtypeStruct(sizes, dtype)


def bands_kernel(filters, short, bias, out, taps, direct):
    groups, count = filters.shape
    lag = lax.broadcasted_iota(jnp.int32, (count, 2 * count), 0)
    column = lax.broadcasted_iota(jnp.int32, (count, 2 * count), 1)
    turned = (lag + column == count).astype(BF16)
    base = jnp.dot(filters[...].astype(BF16), turned, preferred_element_type=F32)
    for g in range(groups):
        row = jnp.broadcast_to(base[g : g + 1, :], (count, 2 * count))
        out[g * count : (g + 1) * count, :] = pltpu.roll(
            row, 0, 1, stride=1, stride_axis=0
        ).astype(BF16)
    for j in range(3):
        taps[3 * j : 3 * j + 3, :] = short[j]
    direct[...] = bias[...]


def three_taps(work, taps, stream, rows):
    return (
        taps[stream : stream + 1, :] * work[8 : 8 + rows, :]
        + taps[3 + stream : 4 + stream, :] * work[7 : 7 + rows, :]
        + taps[6 + stream : 7 + stream, :] * work[6 : 6 + rows, :]
    )


def project_kernel(place, *refs):
    pieces = refs[:8]
    weight, taps, out, edge, total, held, work, sems = refs[8:]
    slots, _, tile, _ = held.shape
    steps = weight.shape[1] // tile

    def fetch(k):
        slot = lax.rem(k, slots)
        rows = pl.ds(pl.multiple_of(k * tile, tile), tile)
        return pltpu.make_async_copy(weight.at[:, rows, :], held.at[slot], sems.at[slot])

    for k in range(slots):
        fetch(k).start()
    total[...] = jnp.zeros_like(total)

    @pl.loop(0, steps)
    def _(k):
        depth = pl.ds(pl.multiple_of(k * tile, tile), tile)
        left = jnp.concatenate([piece[:, depth] for piece in pieces], axis=0)
        fetch(k).wait()
        slot = lax.rem(k, slots)
        for s in range(3):
            total[:, s * 512 : (s + 1) * 512] += jnp.dot(
                left, held[slot, s], preferred_element_type=F32
            )

        @pl.when(k + slots < steps)
        def _():
            fetch(k + slots).start()

    sign = 1 - 2 * place[1]
    for n in range(4):
        for c in range(2):
            z = lax.rem(place[0] + (sign * n if c == 0 else -sign * n) + 4, 4)
            core = place[1] if c == 0 else 1 - place[1]
            row = pl.multiple_of(z * 64 + core * 32, 32)
            at = (2 * n + c) * 32
            out[pl.ds(row, 32), :] = total[at : at + 32, :].astype(BF16)
    streams = []
    for s in (1, 2):
        work[...] = out[112:256, s * 512 : (s + 1) * 512].astype(F32)[8:, :]
        streams.append(three_taps(work, taps, s, 128))
    edge[0:128, :] = (streams[0] * streams[1]).astype(BF16)
    for s in range(3):
        edge[128 + 16 * s : 144 + 16 * s, :] = out[240:256, s * 512 : (s + 1) * 512]


def mix_kernel(projected, edge, taps, bias, bands, out, work, window, query):
    streams = []
    for s in range(3):
        work[0:8, :] = edge[128 + 16 * s : 144 + 16 * s, :].astype(F32)[8:16, :]
        work[8:264, :] = projected[:, s * 512 : (s + 1) * 512].astype(F32)
        featured = three_taps(work, taps, s, 256)
        if s == 0:
            query[...] = featured
        else:
            streams.append(featured)
    product = (streams[0] * streams[1]).astype(BF16)
    window[0:128, :] = edge[0:128, :]
    window[128:384, :] = product
    lane = lax.broadcasted_iota(jnp.int32, (128, 128), 1) // 16
    for j in range(4):
        columns = slice(j * 128, (j + 1) * 128)
        right = jnp.concatenate([window[0:256, columns], window[128:384, columns]], axis=1)
        result = jnp.dot(
            bands[j * 1024 : (j + 1) * 1024, :], right, preferred_element_type=F32
        )
        for block in range(2):
            filtered = jnp.zeros((128, 128), F32)
            for g in range(8):
                filtered = jnp.where(
                    lane == g,
                    result[g * 128 : (g + 1) * 128, block * 128 : (block + 1) * 128],
                    filtered,
                )
            rows = slice(block * 128, (block + 1) * 128)
            direct = window[128 + block * 128 : 256 + block * 128, columns].astype(F32)
            out[rows, columns] = (
                query[rows, columns] * (filtered + bias[:, columns] * direct)
            ).astype(BF16)


def out_kernel(count, place, own, partner, *refs):
    groups = refs[:count]
    outs = refs[count : count + 4]
    left = refs[-1]
    for n, shift in enumerate(SHIFTS):
        z = lax.rem(place[0] + shift + 4, 4)
        row = pl.multiple_of(z * 64, 64)
        left[n * 64 : (n + 1) * 64, 0:512] = own[pl.ds(row, 64), :]
        left[n * 64 : (n + 1) * 64, 512:1024] = partner[pl.ds(row, 64), :]
    for j in range(2 * count):
        group, m = groups[j // 2], 2 * (j % 2)
        right = jnp.concatenate([group[m], group[m + 1]], axis=1)
        result = jnp.dot(left[...], right, preferred_element_type=F32)
        for n in range(4):
            outs[n][:, j * 256 : (j + 1) * 256] = result[n * 64 : (n + 1) * 64].astype(BF16)


def sum_kernel(place, a, b, c, d, keep, send):
    mine = pl.multiple_of(place[1] * 32, 32)
    theirs = pl.multiple_of((1 - place[1]) * 32, 32)
    for out, row in ((keep, mine), (send, theirs)):
        rows = pl.ds(row, 32)
        out[...] = (
            a[rows, :].astype(F32)
            + b[rows, :].astype(F32)
            + c[rows, :].astype(F32)
            + d[rows, :].astype(F32)
        ).astype(BF16)


def place_kernel(plan, place, *refs):
    out = refs[-1]
    for h, groups in enumerate(plan):
        for m in range(2):
            source = refs[2 * h + m]
            core = place[1] if m == 0 else 1 - place[1]
            sign = 1 - 2 * core
            for g, (half, far) in enumerate(groups):
                for near in range(4):
                    x_by, y_by = (near, far) if half == 0 else (far, near)
                    x = lax.rem(place[2] + sign * x_by + 4, 4)
                    y = lax.rem(place[3] + sign * y_by + 4, 4)
                    column = (x * 4 + y) * 512 + core * 256 + half * 128
                    at = (4 * g + near) * 128
                    out[:, pl.ds(pl.multiple_of(column, 128), 128)] = source[:, at : at + 128]


def ring(block, axis, steps):
    blocks = [block]
    for _ in range(steps):
        blocks.append(step(blocks[-1], axis))
    return blocks


def spread(block, half, near, far):
    own = jnp.stack(ring(block, near, 3))
    ahead = step(own, far)
    behind = step(own, far, -1)
    return [(half, 0, own), (half, 1, ahead), (half, -1, behind), (half, 2, step(ahead, far))]


def shards(tokens, in_weight, short_filter, mr_filter, mr_bias, out_weight):
    core = lax.axis_index("core")
    place = jnp.stack(
        [lax.axis_index("z"), core, lax.axis_index("x"), lax.axis_index("y")]
    ).astype(jnp.int32)

    pieces = []
    for block in ring(tokens, "z", 3):
        pieces += [block, take(block, "core", 1)]

    mine = lax.dynamic_slice(out_weight, (0, core * 256), (512, 256))
    other = lax.dynamic_slice(out_weight, (0, (1 - core) * 256), (512, 256))
    pair = jnp.concatenate([mine, take(other, "core", 1)], axis=0)
    one = spread(pair[:, :128], 0, "x", "y")
    two = spread(pair[:, 128:], 1, "y", "x")

    bands, taps, direct = call(
        bands_kernel,
        (shape(4096, 256), shape(9, 512, dtype=F32), shape(1, 512, dtype=F32)),
        "bands",
        [mr_filter.T, short_filter, mr_bias.reshape(1, 512)],
        cost=(0, 4 * MIB),
        in_specs=[VM] * 3,
        out_specs=(VM,) * 3,
    )

    weight = pltpu.with_memory_space_constraint(
        jnp.transpose(in_weight, (1, 0, 2)), pltpu.MemorySpace.HBM
    )
    projected, edge = call(
        project_kernel,
        (shape(256, 1536), shape(176, 512)),
        "project",
        [place, *pieces, weight, taps],
        [
            pltpu.VMEM((256, 1536), F32),
            pltpu.VMEM((6, 3, 512, 512), BF16),
            pltpu.VMEM((136, 512), F32),
            pltpu.SemaphoreType.DMA((6,)),
        ],
        (2 * 256 * 8192 * 1536, 28 * MIB),
        24,
        in_specs=[SM] + [VM] * 8 + [HB, VM],
        out_specs=(VM, VM),
    )

    context = ("x", "y")
    count = lax.axis_size(context)
    earlier = lax.ppermute(edge, context, [(i, i + 1) for i in range(count - 1)])
    gated = call(
        mix_kernel,
        shape(256, 512),
        "mix",
        [projected, earlier, taps, direct, bands],
        [pltpu.VMEM((264, 512), F32), pltpu.VMEM((384, 512), BF16), pltpu.VMEM((256, 512), F32)],
        (2 * 4096 * 256 * 256, 4 * MIB),
        in_specs=[VM] * 5,
        out_specs=VM,
    )
    partner = take(gated, "core", 1)

    parts = []
    plan = []
    for groups in (one[:3] + two[:3], one[3:] + two[3:]):
        width = 512 * len(groups)
        partials = call(
            functools.partial(out_kernel, len(groups)),
            (shape(64, width),) * 4,
            "out",
            [place, gated, partner] + [group[2] for group in groups],
            [pltpu.VMEM((256, 1024), BF16)],
            (2 * 256 * 1024 * width, 1024 * width * 2),
            in_specs=[SM] + [VM] * (2 + len(groups)),
            out_specs=(VM,) * 4,
        )
        arrived = [give(partials[m], "z", SHIFTS[m]) for m in range(1, 4)]
        keep, send = call(
            sum_kernel,
            (shape(32, width),) * 2,
            "sum",
            [place, partials[0], *arrived],
            cost=(0, 600 * width),
            in_specs=[SM] + [VM] * 4,
            out_specs=(VM, VM),
        )
        parts += [keep, take(send, "core", 1)]
        plan.append(tuple(group[:2] for group in groups))
    return call(
        functools.partial(place_kernel, tuple(plan)),
        shape(32, 8192),
        "place",
        [place, *parts],
        cost=(0, MIB),
        in_specs=[SM] + [VM] * len(parts),
        out_specs=VM,
    )


def solution(mesh):
    grid = Mesh(mesh.devices.reshape(4, 4, 4, 2), ("x", "y", "z", "core"))
    channels = ("z", "core")
    context = ("x", "y")
    return jax.shard_map(
        shards,
        mesh=grid,
        in_specs=(
            P(context + channels, None),
            P(None, None, channels),
            P(None, None, channels),
            P(None, channels),
            P(channels),
            P(channels, context),
        ),
        out_specs=P(context + channels, None),
        check_vma=False,
    )
```

time: 152 us -> 115 us (0.76)
  waiting for transfers between devices: 70.3 us -> 44.3 us
  starting transfers between devices: 25.2 us -> 41.3 us
  between operations: 13.6 us -> 0.16 us
  Pallas kernels: 33.2 us -> 22.2 us
    all_gather x2 -> x0, waiting for transfers between devices: 31.9 us -> none  [shards(): lax.all_gather(pair[:, h * 128:(h + 1) * 128], ('x', 'y'), axis=0, tiled=...]
    ppermute x1 -> x16, starting transfers between devices: 3.5 us -> 32.5 us  [the longest x15 30.6 us: step(): return lax.ppermute(shard, (axis, 'core'), pairs)]
    ppermute x18 -> x8, waiting for transfers between devices: 20.8 us -> 3.92 us  [take(): lax.ppermute(shard, axis, [((i + by) % count, i) for i in range(count)])]
    ppermute x1 -> x16, waiting for transfers between devices: 6.69 us -> 22.4 us  [the longest x15 12.9 us: step(): return lax.ppermute(shard, (axis, 'core'), pairs)]
    ppermute x18 -> x8, starting transfers between devices: 12.4 us -> 1.22 us  [take(): lax.ppermute(shard, axis, [((i + by) % count, i) for i in range(count)])]
    pallas_call x9 -> x8, Pallas kernels: 33.2 us -> 22.2 us  [call(): pl.pallas_call(body, out_shape=out, scratch_shapes=list(scratch), name=na...]
    ppermute x6, waiting for transfers between devices: 10.1 us -> 18 us  [give(): lax.ppermute(shard, axis, [(i, (i + by) % count) for i in range(count)])]
    ppermute x6, starting transfers between devices: 9.23 us -> 7.63 us  [give(): lax.ppermute(shard, axis, [(i, (i + by) % count) for i in range(count)])]
  transfers between devices with their start and end apart: 27 -> 30, of which waited for: 13 -> 14; matrix products, arithmetic and copies ran while one was open for 1% -> 0% of each run, Pallas kernels for 21% -> 18%
where the time goes in v2:
time: 115 us; the launch traced here: 114 us
  waiting for transfers between devices  44.3 us (39%)
  starting transfers between devices  41.3 us (36%)
  Pallas kernels  22.2 us (19%)
  local copies, waits for them, and re-layouts  6.07 us (5%)
    ppermute x15, starting transfers between devices, step(): return lax.ppermute(shard, (axis, 'core'), pairs)  30.6 us
    pallas_call x8, Pallas kernels, call(): pl.pallas_call(body, out_shape=out, scratch_shapes=list(scratch), name=na...  22.2 us
    ppermute x6, waiting for transfers between devices, give(): lax.ppermute(shard, axis, [(i, (i + by) % count) for i in range(count)])  18 us
    ppermute x15, waiting for transfers between devices, step(): return lax.ppermute(shard, (axis, 'core'), pairs)  12.9 us
    ppermute x1, waiting for transfers between devices, shards(): lax.ppermute(edge, context, [(i, i + 1) for i in range(count - 1)])  9.57 us
    ppermute x6, starting transfers between devices, give(): lax.ppermute(shard, axis, [(i, (i + by) % count) for i in range(count)])  7.63 us
    unnamed x12, local copies, waits for them, and re-layouts  5.01 us
    ppermute x8, waiting for transfers between devices, take(): lax.ppermute(shard, axis, [((i + by) % count, i) for i in range(count)])  3.92 us
  transfers between devices with their start and end apart: 30, of which 14 were waited for; matrix products, arithmetic and copies ran while one was open for 0% of the time, Pallas kernels for 18%

profile of v2, /device:TPU:2, one launch (start us, length us, event | category | flops | bytes accessed | tf_op | source)
XLA Modules:
  0.0 114.5 jit_solution(15123899849537779518)
XLA Ops:
  0.0 1.1 constant_dynamic-slice_fusion
  1.1 0.1 collective-permute-start.9
  1.2 1.5 %collective-permute-done.9 = bf16[512,256]{1,0:T(8,128)(2,1)S(1)} collective-permute-done((bf16[512,256]{1,0:T(8,128)(2,1)S(1)}, bf16[512,256]{1,0:T(8,128)(2,1)S(1)}, u32[]{:S(2)}, u32[]{:S(2)}) %collective-permute-start.9) | collective-permute-done | bytes 262176 | tf_op jit(solution)/shard_map/ppermute | solution.py:21
  2.7 0.5 collective-permute-start.10
  3.2 4.1 %collective-permute-start.1 = (bf16[32,8192]{1,0:T(8,128)(2,1)}, bf16[32,8192]{1,0:T(8,128)(2,1)}, u32[]{:S(2)}, u32[]{:S(2)}) collective-permute-start(bf16[32,8192]{1,0:T(8,128)(2,1)} %refs_0_.1), channel_id=1, source_target_pairs={{2,0},{7,1},{4,2},{1,3},{6,4},{3,5},{0,6},{5,7},{10,8},{15,9},{12,... | collective-permute-start | bytes 1572872 | tf_op jit(solution)/shard_map/ppermute | solution.py:36
  7.4 3.0 %collective-permute-start.15 = (bf16[1024,128]{1,0:T(8,128)(2,1)S(1)}, bf16[1024,128]{1,0:T(8,128)(2,1)S(1)}, u32[]{:S(2)}, u32[]{:S(2)}) collective-permute-start(bf16[1024,128]{1,0:T(8,128)(2,1)S(1)} %get-tuple-element.39), channel_id=1, source_target_pairs={{8,0},{25,1},{16,8},{1,9},{24,16},{9,17},{0,24},{17,25},{10,2},{27... | collective-permute-start | bytes 786440 | tf_op jit(solution)/shard_map/ppermute | solution.py:36
  10.4 0.0 collective-permute-done.10
  10.4 2.8 %collective-permute-start.11 = (bf16[1024,128]{1,0:T(8,128)(2,1)S(1)}, bf16[1024,128]{1,0:T(8,128)(2,1)S(1)}, u32[]{:S(2)}, u32[]{:S(2)}) collective-permute-start(bf16[1024,128]{1,0:T(8,128)(2,1)S(1)} %collective-permute-done.10), channel_id=1, source_target_pairs={{32,0},{97,1},{64,32},{1,33},{96,64},{33,65},{0,96},{65,97},{34,2}... | collective-permute-start | bytes 786440 | tf_op jit(solution)/shard_map/ppermute | solution.py:36
  13.1 1.1 collective-permute-done.15
  14.3 3.7 %collective-permute-start.16 = (bf16[1024,128]{1,0:T(8,128)(2,1)S(1)}, bf16[1024,128]{1,0:T(8,128)(2,1)S(1)}, u32[]{:S(2)}, u32[]{:S(2)}) collective-permute-start(bf16[1024,128]{1,0:T(8,128)(2,1)S(1)} %collective-permute-done.15), channel_id=1, source_target_pairs={{8,0},{25,1},{16,8},{1,9},{24,16},{9,17},{0,24},{17,25},{10,2},{27... | collective-permute-start | bytes 786440 | tf_op jit(solution)/shard_map/ppermute | solution.py:36
  18.0 0.0 collective-permute-done.11
  18.0 2.8 %collective-permute-start.12 = (bf16[1024,128]{1,0:T(8,128)(2,1)S(1)}, bf16[1024,128]{1,0:T(8,128)(2,1)S(1)}, u32[]{:S(2)}, u32[]{:S(2)}) collective-permute-start(bf16[1024,128]{1,0:T(8,128)(2,1)S(1)} %collective-permute-done.11), channel_id=1, source_target_pairs={{32,0},{97,1},{64,32},{1,33},{96,64},{33,65},{0,96},{65,97},{34,2}... | collective-permute-start | bytes 786440 | tf_op jit(solution)/shard_map/ppermute | solution.py:36
  20.7 0.9 collective-permute-start.3
  21.6 0.3 collective-permute-done.16
  21.9 3.7 %collective-permute-start.17 = (bf16[1024,128]{1,0:T(8,128)(2,1)S(1)}, bf16[1024,128]{1,0:T(8,128)(2,1)S(1)}, u32[]{:S(2)}, u32[]{:S(2)}) collective-permute-start(bf16[1024,128]{1,0:T(8,128)(2,1)S(1)} %collective-permute-done.16), channel_id=1, source_target_pairs={{8,0},{25,1},{16,8},{1,9},{24,16},{9,17},{0,24},{17,25},{10,2},{27... | collective-permute-start | bytes 786440 | tf_op jit(solution)/shard_map/ppermute | solution.py:36
  25.6 0.1 pad_maximum_fusion.refs_0_
  25.7 0.1 collective-permute-start.13
  25.8 3.7 %collective-permute-done.17 = bf16[1024,128]{1,0:T(8,128)(2,1)S(1)} collective-permute-done((bf16[1024,128]{1,0:T(8,128)(2,1)S(1)}, bf16[1024,128]{1,0:T(8,128)(2,1)S(1)}, u32[]{:S(2)}, u32[]{:S(2)}) %collective-permute-start.17) | collective-permute-done | bytes 262176 | tf_op jit(solution)/shard_map/ppermute | solution.py:36
  29.4 0.1 pad_maximum_fusion.1.refs_3_
  29.6 2.8 %collective-permute-start.18 = (bf16[4,1024,128]{2,1,0:T(8,128)(2,1)S(1)}, bf16[4,1024,128]{2,1,0:T(8,128)(2,1)}, u32[]{:S(2)}, u32[]{:S(2)}) collective-permute-start(bf16[4,1024,128]{2,1,0:T(8,128)(2,1)S(1)} %pad_maximum_fusion.1.refs_3_), channel_id=1, source_target_pairs={{32,0},{97,1},{64,32},{1,33},{96,64},{33,65},{0,96},{65,97},{34,2}... | collective-permute-start | bytes 3145736 | tf_op jit(solution)/shard_map/ppermute | solution.py:36
  32.4 0.4 collective-permute-start.5
  32.8 0.0 collective-permute-start.2
  32.8 0.0 collective-permute-done.refs_1_
  32.8 0.8 copy-done.1
  33.6 0.5 collective-permute-start.4
  34.1 7.8 %collective-permute-done.5.refs_6_ = bf16[32,8192]{1,0:T(8,128)(2,1)} collective-permute-done((bf16[32,8192]{1,0:T(8,128)(2,1)}, bf16[32,8192]{1,0:T(8,128)(2,1)}, u32[]{:S(2)}, u32[]{:S(2)}) %collective-permute-start.5) | collective-permute-done | bytes 524320 | tf_op jit(solution)/shard_map/ppermute | solution.py:36
  41.9 0.0 collective-permute-start.6
  41.9 0.7 copy-done.3
  42.7 0.7 copy-done.4
  43.4 0.7 copy-done.5
  44.0 0.7 bands.1
  44.8 0.1 pad_add_fusion.place
  44.9 0.0 collective-permute-done.2.refs_3_
  44.9 1.1 collective-permute-start.14
  45.9 0.0 collective-permute-done.4.refs_5_
  46.0 2.8 %collective-permute-start.24 = (bf16[4,1024,128]{2,1,0:T(8,128)(2,1)S(1)}, bf16[4,1024,128]{2,1,0:T(8,128)(2,1)S(1)}, u32[]{:S(2)}, u32[]{:S(2)}) collective-permute-start(bf16[4,1024,128]{2,1,0:T(8,128)(2,1)S(1)} %collective-permute-done.13.refs_1_), channel_id=1, source_target_pairs={{8,0},{25,1},{16,8},{1,9},{24,16},{9,17},{0,24},{17,25},{10,2},{27... | collective-permute-start | bytes 3145736 | tf_op jit(solution)/shard_map/ppermute | solution.py:36
  48.8 1.9 %collective-permute-start.25 = (bf16[4,1024,128]{2,1,0:T(8,128)(2,1)}, bf16[4,1024,128]{2,1,0:T(8,128)(2,1)S(1)}, u32[]{:S(2)}, u32[]{:S(2)}) collective-permute-start(bf16[4,1024,128]{2,1,0:T(8,128)(2,1)} %collective-permute-done.18.refs_4_), channel_id=1, source_target_pairs={{32,0},{97,1},{64,32},{1,33},{96,64},{33,65},{0,96},{65,97},{34,2}... | collective-permute-start | bytes 3145736 | tf_op jit(solution)/shard_map/ppermute | solution.py:36
  50.7 1.0 copy-done
  51.8 1.0 copy-done.2
  52.8 13.2 %project.1 = (bf16[256,1536]{1,0:T(8,128)(2,1)S(1)}, bf16[176,512]{1,0:T(8,128)(2,1)S(1)}) custom-call(s32[4]{0:T(128)S(1)} %pad_add_fusion.place, bf16[32,8192]{1,0:T(8,128)(2,1)S(1)} %copy-done, bf16[32,8192]{1,0:T(8,128)(2,1)S(1)} %copy-done.2, bf16[32,8192]{1,0:T(8,128)(2,1)} %collective-permute-done.1.refs_2_, ...), custom_call_target="tpu_custom_call" | custom-call | flops 6442450944 | bytes 29360128 | tf_op jit(solution)/shard_map/project/pallas_call | solution.py:40
  66.0 1.9 %collective-permute-start.7 = (bf16[176,512]{1,0:T(8,128)(2,1)S(1)}, bf16[176,512]{1,0:T(8,128)(2,1)S(1)}, u32[]{:S(2)}, u32[]{:S(2)}) collective-permute-start(bf16[176,512]{1,0:T(8,128)(2,1)S(1)} %get-tuple-element.24), channel_id=1, source_target_pairs={{0,8},{8,16},{16,24},{24,32},{32,40},{40,48},{48,56},{56,64},{64,7... | collective-permute-start | bytes 540680 | tf_op jit(solution)/shard_map/ppermute | solution.py:270
  67.9 9.6 %collective-permute-done.7.edge = bf16[176,512]{1,0:T(8,128)(2,1)S(1)} collective-permute-done((bf16[176,512]{1,0:T(8,128)(2,1)S(1)}, bf16[176,512]{1,0:T(8,128)(2,1)S(1)}, u32[]{:S(2)}, u32[]{:S(2)}) %collective-permute-start.7) | collective-permute-done | bytes 180256 | tf_op jit(solution)/shard_map/ppermute | solution.py:270
  77.5 1.1 mix.1.own
  78.6 0.4 collective-permute-start.8
  79.0 1.2 %collective-permute-done.8.partner = bf16[256,512]{1,0:T(8,128)(2,1)S(1)} collective-permute-done((bf16[256,512]{1,0:T(8,128)(2,1)S(1)}, bf16[256,512]{1,0:T(8,128)(2,1)S(1)}, u32[]{:S(2)}, u32[]{:S(2)}) %collective-permute-start.8) | collective-permute-done | bytes 262176 | tf_op jit(solution)/shard_map/ppermute | solution.py:21
  80.2 3.1 %out.2 = (bf16[64,3072]{1,0:T(8,128)(2,1)S(1)}, bf16[64,3072]{1,0:T(8,128)(2,1)S(1)}, bf16[64,3072]{1,0:T(8,128)(2,1)S(1)}, bf16[64,3072]{1,0:T(8,128)(2,1)S(1)}) custom-call(s32[4]{0:T(128)S(1)} %pad_add_fusion.place, bf16[256,512]{1,0:T(8,128)(2,1)S(1)} %mix.1.own, bf16[256,512]{1,0:T(8,128)(2,1)S(1)} %collective-permute-done.8.partner, ...), custom_call_target="tpu_custom_call" | custom-call | flops 1610612736 | bytes 6291456 | tf_op jit(solution)/shard_map/out/pallas_call | solution.py:40
  83.3 0.3 collective-permute-start.20
  83.5 3.2 %collective-permute-start.21 = (bf16[64,3072]{1,0:T(8,128)(2,1)S(1)}, bf16[64,3072]{1,0:T(8,128)(2,1)S(1)}, u32[]{:S(2)}, u32[]{:S(2)}) collective-permute-start(bf16[64,3072]{1,0:T(8,128)(2,1)S(1)} %get-tuple-element.29), channel_id=1, source_target_pairs={{0,6},{2,0},{4,2},{6,4},{1,7},{3,1},{5,3},{7,5},{8,14},{10,8},{12,... | collective-permute-start | bytes 1179656 | tf_op jit(solution)/shard_map/ppermute | solution.py:26
  86.8 0.8 collective-permute-start.22
  87.6 1.2 %out.3 = (bf16[64,1024]{1,0:T(8,128)(2,1)S(1)}, bf16[64,1024]{1,0:T(8,128)(2,1)S(1)}, bf16[64,1024]{1,0:T(8,128)(2,1)S(1)}, bf16[64,1024]{1,0:T(8,128)(2,1)S(1)}) custom-call(s32[4]{0:T(128)S(1)} %pad_add_fusion.place, bf16[256,512]{1,0:T(8,128)(2,1)S(1)} %mix.1.own, bf16[256,512]{1,0:T(8,128)(2,1)S(1)} %collective-permute-done.8.partner, ...), custom_call_target="tpu_custom_call" | custom-call | flops 536870912 | bytes 2097152 | tf_op jit(solution)/shard_map/out/pallas_call | solution.py:40
  88.9 1.5 %collective-permute-start.26 = (bf16[64,1024]{1,0:T(8,128)(2,1)S(1)}, bf16[64,1024]{1,0:T(8,128)(2,1)S(1)}, u32[]{:S(2)}, u32[]{:S(2)}) collective-permute-start(bf16[64,1024]{1,0:T(8,128)(2,1)S(1)} %get-tuple-element.34), channel_id=1, source_target_pairs={{0,2},{2,4},{4,6},{6,0},{1,3},{3,5},{5,7},{7,1},{8,10},{10,12},{12... | collective-permute-start | bytes 393224 | tf_op jit(solution)/shard_map/ppermute | solution.py:26
  90.3 1.8 %collective-permute-start.27 = (bf16[64,1024]{1,0:T(8,128)(2,1)S(1)}, bf16[64,1024]{1,0:T(8,128)(2,1)S(1)}, u32[]{:S(2)}, u32[]{:S(2)}) collective-permute-start(bf16[64,1024]{1,0:T(8,128)(2,1)S(1)} %get-tuple-element.35), channel_id=1, source_target_pairs={{0,6},{2,0},{4,2},{6,4},{1,7},{3,1},{5,3},{7,5},{8,14},{10,8},{12,... | collective-permute-start | bytes 393224 | tf_op jit(solution)/shard_map/ppermute | solution.py:26
  92.2 4.9 %collective-permute-done.20.b = bf16[64,3072]{1,0:T(8,128)(2,1)S(1)} collective-permute-done((bf16[64,3072]{1,0:T(8,128)(2,1)S(1)}, bf16[64,3072]{1,0:T(8,128)(2,1)S(1)}, u32[]{:S(2)}, u32[]{:S(2)}) %collective-permute-start.20) | collective-permute-done | bytes 393248 | tf_op jit(solution)/shard_map/ppermute | solution.py:26
  97.1 7.6 %collective-permute-done.21.c = bf16[64,3072]{1,0:T(8,128)(2,1)S(1)} collective-permute-done((bf16[64,3072]{1,0:T(8,128)(2,1)S(1)}, bf16[64,3072]{1,0:T(8,128)(2,1)S(1)}, u32[]{:S(2)}, u32[]{:S(2)}) %collective-permute-start.21) | collective-permute-done | bytes 393248 | tf_op jit(solution)/shard_map/ppermute | solution.py:26
  104.7 1.3 %collective-permute-done.22.d = bf16[64,3072]{1,0:T(8,128)(2,1)S(1)} collective-permute-done((bf16[64,3072]{1,0:T(8,128)(2,1)S(1)}, bf16[64,3072]{1,0:T(8,128)(2,1)S(1)}, u32[]{:S(2)}, u32[]{:S(2)}) %collective-permute-start.22) | collective-permute-done | bytes 393248 | tf_op jit(solution)/shard_map/ppermute | solution.py:26
  106.0 0.7 sum.2
  106.7 0.1 collective-permute-start.23
  106.8 0.5 collective-permute-done.26.b
  107.3 2.1 %collective-permute-done.27.c = bf16[64,1024]{1,0:T(8,128)(2,1)S(1)} collective-permute-done((bf16[64,1024]{1,0:T(8,128)(2,1)S(1)}, bf16[64,1024]{1,0:T(8,128)(2,1)S(1)}, u32[]{:S(2)}, u32[]{:S(2)}) %collective-permute-start.27) | collective-permute-done | bytes 131104 | tf_op jit(solution)/shard_map/ppermute | solution.py:26
  109.4 1.5 %collective-permute-done.28.d = bf16[64,1024]{1,0:T(8,128)(2,1)S(1)} collective-permute-done((bf16[64,1024]{1,0:T(8,128)(2,1)S(1)}, bf16[64,1024]{1,0:T(8,128)(2,1)S(1)}, u32[]{:S(2)}, u32[]{:S(2)}) %collective-permute-start.28) | collective-permute-done | bytes 131104 | tf_op jit(solution)/shard_map/ppermute | solution.py:26
  111.0 0.6 sum.3
  111.6 0.1 collective-permute-start.29
  111.7 1.2 %collective-permute-done.29.refs_3_ = bf16[32,1024]{1,0:T(8,128)(2,1)S(1)} collective-permute-done((bf16[32,1024]{1,0:T(8,128)(2,1)S(1)}, bf16[32,1024]{1,0:T(8,128)(2,1)S(1)}, u32[]{:S(2)}, u32[]{:S(2)}) %collective-permute-start.29) | collective-permute-done | bytes 65568 | tf_op jit(solution)/shard_map/ppermute | solution.py:21
  112.9 1.6 %place.1 = bf16[32,8192]{1,0:T(8,128)(2,1)} custom-call(s32[4]{0:T(128)S(1)} %pad_add_fusion.place, bf16[32,3072]{1,0:T(8,128)(2,1)S(1)} %get-tuple-element.31.refs_0_, bf16[32,3072]{1,0:T(8,128)(2,1)S(1)} %collective-permute-done.23.refs_1_, bf16[32,1024]{1,0:T(8,128)(2,1)S(1)} %get-tuple-element.37.refs_2_, ...), custom_call_target="tpu_custom_call" | custom-call | bytes 1048576 | tf_op jit(solution)/shard_map/place/pallas_call | solution.py:40
  (21 shorter events, 0.1 us)
Async XLA Ops:
  1.1 1.6 %collective-permute-start.9 = (bf16[512,256]{1,0:T(8,128)(2,1)S(1)}, bf16[512,256]{1,0:T(8,128)(2,1)S(1)}, u32[]{:S(2)}, u32[]{:S(2)}) collective-permute-start(bf16[512,256]{1,0:T(8,128)(2,1)S(1)} %get-tuple-element.41), channel_id=1, source_target_pairs={{1,0},{0,1},{3,2},{2,3},{5,4},{4,5},{7,6},{6,7},{9,8},{8,9},{11,10... | collective-permute-start | bytes 786440 | tf_op jit(solution)/shard_map/ppermute | solution.py:21
  2.7 7.7 %collective-permute-start.10 = (bf16[1024,128]{1,0:T(8,128)(2,1)S(1)}, bf16[1024,128]{1,0:T(8,128)(2,1)S(1)}, u32[]{:S(2)}, u32[]{:S(2)}) collective-permute-start(bf16[1024,128]{1,0:T(8,128)(2,1)S(1)} %get-tuple-element.40), channel_id=1, source_target_pairs={{32,0},{97,1},{64,32},{1,33},{96,64},{33,65},{0,96},{65,97},{34,2}... | collective-permute-start | bytes 786440 | tf_op jit(solution)/shard_map/ppermute | solution.py:36
  3.2 17.5 %collective-permute-start.1 = (bf16[32,8192]{1,0:T(8,128)(2,1)}, bf16[32,8192]{1,0:T(8,128)(2,1)}, u32[]{:S(2)}, u32[]{:S(2)}) collective-permute-start(bf16[32,8192]{1,0:T(8,128)(2,1)} %refs_0_.1), channel_id=1, source_target_pairs={{2,0},{7,1},{4,2},{1,3},{6,4},{3,5},{0,6},{5,7},{10,8},{15,9},{12,... | collective-permute-start | bytes 1572872 | tf_op jit(solution)/shard_map/ppermute | solution.py:36
  7.4 6.9 %collective-permute-start.15 = (bf16[1024,128]{1,0:T(8,128)(2,1)S(1)}, bf16[1024,128]{1,0:T(8,128)(2,1)S(1)}, u32[]{:S(2)}, u32[]{:S(2)}) collective-permute-start(bf16[1024,128]{1,0:T(8,128)(2,1)S(1)} %get-tuple-element.39), channel_id=1, source_target_pairs={{8,0},{25,1},{16,8},{1,9},{24,16},{9,17},{0,24},{17,25},{10,2},{27... | collective-permute-start | bytes 786440 | tf_op jit(solution)/shard_map/ppermute | solution.py:36
  10.4 7.6 %collective-permute-start.11 = (bf16[1024,128]{1,0:T(8,128)(2,1)S(1)}, bf16[1024,128]{1,0:T(8,128)(2,1)S(1)}, u32[]{:S(2)}, u32[]{:S(2)}) collective-permute-start(bf16[1024,128]{1,0:T(8,128)(2,1)S(1)} %collective-permute-done.10), channel_id=1, source_target_pairs={{32,0},{97,1},{64,32},{1,33},{96,64},{33,65},{0,96},{65,97},{34,2}... | collective-permute-start | bytes 786440 | tf_op jit(solution)/shard_map/ppermute | solution.py:36
  14.3 7.6 %collective-permute-start.16 = (bf16[1024,128]{1,0:T(8,128)(2,1)S(1)}, bf16[1024,128]{1,0:T(8,128)(2,1)S(1)}, u32[]{:S(2)}, u32[]{:S(2)}) collective-permute-start(bf16[1024,128]{1,0:T(8,128)(2,1)S(1)} %collective-permute-done.15), channel_id=1, source_target_pairs={{8,0},{25,1},{16,8},{1,9},{24,16},{9,17},{0,24},{17,25},{10,2},{27... | collective-permute-start | bytes 786440 | tf_op jit(solution)/shard_map/ppermute | solution.py:36
  18.0 7.6 %collective-permute-start.12 = (bf16[1024,128]{1,0:T(8,128)(2,1)S(1)}, bf16[1024,128]{1,0:T(8,128)(2,1)S(1)}, u32[]{:S(2)}, u32[]{:S(2)}) collective-permute-start(bf16[1024,128]{1,0:T(8,128)(2,1)S(1)} %collective-permute-done.11), channel_id=1, source_target_pairs={{32,0},{97,1},{64,32},{1,33},{96,64},{33,65},{0,96},{65,97},{34,2}... | collective-permute-start | bytes 786440 | tf_op jit(solution)/shard_map/ppermute | solution.py:36
  20.7 11.7 %collective-permute-start.3 = (bf16[32,8192]{1,0:T(8,128)(2,1)}, bf16[32,8192]{1,0:T(8,128)(2,1)}, u32[]{:S(2)}, u32[]{:S(2)}) collective-permute-start(bf16[32,8192]{1,0:T(8,128)(2,1)} %collective-permute-done.1.refs_2_), channel_id=1, source_target_pairs={{2,0},{7,1},{4,2},{1,3},{6,4},{3,5},{0,6},{5,7},{10,8},{15,9},{12,... | collective-permute-start | bytes 1572872 | tf_op jit(solution)/shard_map/ppermute | solution.py:36
  21.9 7.6 %collective-permute-start.17 = (bf16[1024,128]{1,0:T(8,128)(2,1)S(1)}, bf16[1024,128]{1,0:T(8,128)(2,1)S(1)}, u32[]{:S(2)}, u32[]{:S(2)}) collective-permute-start(bf16[1024,128]{1,0:T(8,128)(2,1)S(1)} %collective-permute-done.16), channel_id=1, source_target_pairs={{8,0},{25,1},{16,8},{1,9},{24,16},{9,17},{0,24},{17,25},{10,2},{27... | collective-permute-start | bytes 786440 | tf_op jit(solution)/shard_map/ppermute | solution.py:36
  25.5 7.3 %collective-permute-start = (bf16[32,8192]{1,0:T(8,128)(2,1)}, bf16[32,8192]{1,0:T(8,128)(2,1)S(1)}, u32[]{:S(2)}, u32[]{:S(2)}) collective-permute-start(bf16[32,8192]{1,0:T(8,128)(2,1)} %refs_0_.1), channel_id=1, source_target_pairs={{1,0},{0,1},{3,2},{2,3},{5,4},{4,5},{7,6},{6,7},{9,8},{8,9},{11,10... | collective-permute-start | bytes 1572872 | tf_op jit(solution)/shard_map/ppermute | solution.py:21
  25.7 20.3 %collective-permute-start.13 = (bf16[4,1024,128]{2,1,0:T(8,128)(2,1)S(1)}, bf16[4,1024,128]{2,1,0:T(8,128)(2,1)S(1)}, u32[]{:S(2)}, u32[]{:S(2)}) collective-permute-start(bf16[4,1024,128]{2,1,0:T(8,128)(2,1)S(1)} %pad_maximum_fusion.refs_0_), channel_id=1, source_target_pairs={{8,0},{25,1},{16,8},{1,9},{24,16},{9,17},{0,24},{17,25},{10,2},{27... | collective-permute-start | bytes 3145736 | tf_op jit(solution)/shard_map/ppermute | solution.py:36
  29.6 19.2 %collective-permute-start.18 = (bf16[4,1024,128]{2,1,0:T(8,128)(2,1)S(1)}, bf16[4,1024,128]{2,1,0:T(8,128)(2,1)}, u32[]{:S(2)}, u32[]{:S(2)}) collective-permute-start(bf16[4,1024,128]{2,1,0:T(8,128)(2,1)S(1)} %pad_maximum_fusion.1.refs_3_), channel_id=1, source_target_pairs={{32,0},{97,1},{64,32},{1,33},{96,64},{33,65},{0,96},{65,97},{34,2}... | collective-permute-start | bytes 3145736 | tf_op jit(solution)/shard_map/ppermute | solution.py:36
  32.4 9.5 %collective-permute-start.5 = (bf16[32,8192]{1,0:T(8,128)(2,1)}, bf16[32,8192]{1,0:T(8,128)(2,1)}, u32[]{:S(2)}, u32[]{:S(2)}) collective-permute-start(bf16[32,8192]{1,0:T(8,128)(2,1)} %collective-permute-done.3.refs_4_), channel_id=1, source_target_pairs={{2,0},{7,1},{4,2},{1,3},{6,4},{3,5},{0,6},{5,7},{10,8},{15,9},{12,... | collective-permute-start | bytes 1572872 | tf_op jit(solution)/shard_map/ppermute | solution.py:36
  32.8 12.1 %collective-permute-start.2 = (bf16[32,8192]{1,0:T(8,128)(2,1)}, bf16[32,8192]{1,0:T(8,128)(2,1)}, u32[]{:S(2)}, u32[]{:S(2)}) collective-permute-start(bf16[32,8192]{1,0:T(8,128)(2,1)} %collective-permute-done.1.refs_2_), channel_id=1, source_target_pairs={{1,0},{0,1},{3,2},{2,3},{5,4},{4,5},{7,6},{6,7},{9,8},{8,9},{11,10... | collective-permute-start | bytes 1572872 | tf_op jit(solution)/shard_map/ppermute | solution.py:21
  32.8 0.8 copy-start.1
  33.6 12.3 %collective-permute-start.4 = (bf16[32,8192]{1,0:T(8,128)(2,1)}, bf16[32,8192]{1,0:T(8,128)(2,1)}, u32[]{:S(2)}, u32[]{:S(2)}) collective-permute-start(bf16[32,8192]{1,0:T(8,128)(2,1)} %collective-permute-done.3.refs_4_), channel_id=1, source_target_pairs={{1,0},{0,1},{3,2},{2,3},{5,4},{4,5},{7,6},{6,7},{9,8},{8,9},{11,10... | collective-permute-start | bytes 1572872 | tf_op jit(solution)/shard_map/ppermute | solution.py:21
  41.9 8.8 %collective-permute-start.6 = (bf16[32,8192]{1,0:T(8,128)(2,1)}, bf16[32,8192]{1,0:T(8,128)(2,1)}, u32[]{:S(2)}, u32[]{:S(2)}) collective-permute-start(bf16[32,8192]{1,0:T(8,128)(2,1)} %collective-permute-done.5.refs_6_), channel_id=1, source_target_pairs={{1,0},{0,1},{3,2},{2,3},{5,4},{4,5},{7,6},{6,7},{9,8},{8,9},{11,10... | collective-permute-start | bytes 1572872 | tf_op jit(solution)/shard_map/ppermute | solution.py:21
  41.9 0.7 copy-start.3
  42.6 0.7 copy-start.4
  43.4 0.7 copy-start.5
  44.9 34.2 %collective-permute-start.14 = (bf16[4,1024,128]{2,1,0:T(8,128)(2,1)S(1)}, bf16[4,1024,128]{2,1,0:T(8,128)(2,1)S(1)}, u32[]{:S(2)}, u32[]{:S(2)}) collective-permute-start(bf16[4,1024,128]{2,1,0:T(8,128)(2,1)S(1)} %pad_maximum_fusion.refs_0_), channel_id=1, source_target_pairs={{24,0},{9,1},{0,8},{17,9},{8,16},{25,17},{16,24},{1,25},{26,2},{11... | collective-permute-start | bytes 3145736 | tf_op jit(solution)/shard_map/ppermute | solution.py:36
  45.9 33.1 %collective-permute-start.19 = (bf16[4,1024,128]{2,1,0:T(8,128)(2,1)S(1)}, bf16[4,1024,128]{2,1,0:T(8,128)(2,1)S(1)}, u32[]{:S(2)}, u32[]{:S(2)}) collective-permute-start(bf16[4,1024,128]{2,1,0:T(8,128)(2,1)S(1)} %pad_maximum_fusion.1.refs_3_), channel_id=1, source_target_pairs={{96,0},{33,1},{0,32},{65,33},{32,64},{97,65},{64,96},{1,97},{98,2}... | collective-permute-start | bytes 3145736 | tf_op jit(solution)/shard_map/ppermute | solution.py:36
  46.0 41.6 %collective-permute-start.24 = (bf16[4,1024,128]{2,1,0:T(8,128)(2,1)S(1)}, bf16[4,1024,128]{2,1,0:T(8,128)(2,1)S(1)}, u32[]{:S(2)}, u32[]{:S(2)}) collective-permute-start(bf16[4,1024,128]{2,1,0:T(8,128)(2,1)S(1)} %collective-permute-done.13.refs_1_), channel_id=1, source_target_pairs={{8,0},{25,1},{16,8},{1,9},{24,16},{9,17},{0,24},{17,25},{10,2},{27... | collective-permute-start | bytes 3145736 | tf_op jit(solution)/shard_map/ppermute | solution.py:36
  48.8 38.8 %collective-permute-start.25 = (bf16[4,1024,128]{2,1,0:T(8,128)(2,1)}, bf16[4,1024,128]{2,1,0:T(8,128)(2,1)S(1)}, u32[]{:S(2)}, u32[]{:S(2)}) collective-permute-start(bf16[4,1024,128]{2,1,0:T(8,128)(2,1)} %collective-permute-done.18.refs_4_), channel_id=1, source_target_pairs={{32,0},{97,1},{64,32},{1,33},{96,64},{33,65},{0,96},{65,97},{34,2}... | collective-permute-start | bytes 3145736 | tf_op jit(solution)/shard_map/ppermute | solution.py:36
  50.7 1.0 copy-start
  51.8 1.0 copy-start.2
  66.0 11.5 %collective-permute-start.7 = (bf16[176,512]{1,0:T(8,128)(2,1)S(1)}, bf16[176,512]{1,0:T(8,128)(2,1)S(1)}, u32[]{:S(2)}, u32[]{:S(2)}) collective-permute-start(bf16[176,512]{1,0:T(8,128)(2,1)S(1)} %get-tuple-element.24), channel_id=1, source_target_pairs={{0,8},{8,16},{16,24},{24,32},{32,40},{40,48},{48,56},{56,64},{64,7... | collective-permute-start | bytes 540680 | tf_op jit(solution)/shard_map/ppermute | solution.py:270
  78.6 1.6 %collective-permute-start.8 = (bf16[256,512]{1,0:T(8,128)(2,1)S(1)}, bf16[256,512]{1,0:T(8,128)(2,1)S(1)}, u32[]{:S(2)}, u32[]{:S(2)}) collective-permute-start(bf16[256,512]{1,0:T(8,128)(2,1)S(1)} %mix.1.own), channel_id=1, source_target_pairs={{1,0},{0,1},{3,2},{2,3},{5,4},{4,5},{7,6},{6,7},{9,8},{8,9},{11,10... | collective-permute-start | bytes 786440 | tf_op jit(solution)/shard_map/ppermute | solution.py:21
  83.3 13.8 %collective-permute-start.20 = (bf16[64,3072]{1,0:T(8,128)(2,1)S(1)}, bf16[64,3072]{1,0:T(8,128)(2,1)S(1)}, u32[]{:S(2)}, u32[]{:S(2)}) collective-permute-start(bf16[64,3072]{1,0:T(8,128)(2,1)S(1)} %get-tuple-element.28), channel_id=1, source_target_pairs={{0,2},{2,4},{4,6},{6,0},{1,3},{3,5},{5,7},{7,1},{8,10},{10,12},{12... | collective-permute-start | bytes 1179656 | tf_op jit(solution)/shard_map/ppermute | solution.py:26
  83.5 21.2 %collective-permute-start.21 = (bf16[64,3072]{1,0:T(8,128)(2,1)S(1)}, bf16[64,3072]{1,0:T(8,128)(2,1)S(1)}, u32[]{:S(2)}, u32[]{:S(2)}) collective-permute-start(bf16[64,3072]{1,0:T(8,128)(2,1)S(1)} %get-tuple-element.29), channel_id=1, source_target_pairs={{0,6},{2,0},{4,2},{6,4},{1,7},{3,1},{5,3},{7,5},{8,14},{10,8},{12,... | collective-permute-start | bytes 1179656 | tf_op jit(solution)/shard_map/ppermute | solution.py:26
  86.8 19.2 %collective-permute-start.22 = (bf16[64,3072]{1,0:T(8,128)(2,1)S(1)}, bf16[64,3072]{1,0:T(8,128)(2,1)S(1)}, u32[]{:S(2)}, u32[]{:S(2)}) collective-permute-start(bf16[64,3072]{1,0:T(8,128)(2,1)S(1)} %get-tuple-element.30), channel_id=1, source_target_pairs={{0,4},{2,6},{4,0},{6,2},{1,5},{3,7},{5,1},{7,3},{8,12},{10,14},{12... | collective-permute-start | bytes 1179656 | tf_op jit(solution)/shard_map/ppermute | solution.py:26
  88.9 18.5 %collective-permute-start.26 = (bf16[64,1024]{1,0:T(8,128)(2,1)S(1)}, bf16[64,1024]{1,0:T(8,128)(2,1)S(1)}, u32[]{:S(2)}, u32[]{:S(2)}) collective-permute-start(bf16[64,1024]{1,0:T(8,128)(2,1)S(1)} %get-tuple-element.34), channel_id=1, source_target_pairs={{0,2},{2,4},{4,6},{6,0},{1,3},{3,5},{5,7},{7,1},{8,10},{10,12},{12... | collective-permute-start | bytes 393224 | tf_op jit(solution)/shard_map/ppermute | solution.py:26
  90.3 19.1 %collective-permute-start.27 = (bf16[64,1024]{1,0:T(8,128)(2,1)S(1)}, bf16[64,1024]{1,0:T(8,128)(2,1)S(1)}, u32[]{:S(2)}, u32[]{:S(2)}) collective-permute-start(bf16[64,1024]{1,0:T(8,128)(2,1)S(1)} %get-tuple-element.35), channel_id=1, source_target_pairs={{0,6},{2,0},{4,2},{6,4},{1,7},{3,1},{5,3},{7,5},{8,14},{10,8},{12,... | collective-permute-start | bytes 393224 | tf_op jit(solution)/shard_map/ppermute | solution.py:26
  97.1 13.9 %collective-permute-start.28 = (bf16[64,1024]{1,0:T(8,128)(2,1)S(1)}, bf16[64,1024]{1,0:T(8,128)(2,1)S(1)}, u32[]{:S(2)}, u32[]{:S(2)}) collective-permute-start(bf16[64,1024]{1,0:T(8,128)(2,1)S(1)} %get-tuple-element.36), channel_id=1, source_target_pairs={{0,4},{2,6},{4,0},{6,2},{1,5},{3,7},{5,1},{7,3},{8,12},{10,14},{12... | collective-permute-start | bytes 393224 | tf_op jit(solution)/shard_map/ppermute | solution.py:26
  106.7 5.0 %collective-permute-start.23 = (bf16[32,3072]{1,0:T(8,128)(2,1)S(1)}, bf16[32,3072]{1,0:T(8,128)(2,1)S(1)}, u32[]{:S(2)}, u32[]{:S(2)}) collective-permute-start(bf16[32,3072]{1,0:T(8,128)(2,1)S(1)} %get-tuple-element.32), channel_id=1, source_target_pairs={{1,0},{0,1},{3,2},{2,3},{5,4},{4,5},{7,6},{6,7},{9,8},{8,9},{11,10... | collective-permute-start | bytes 589832 | tf_op jit(solution)/shard_map/ppermute | solution.py:21
  111.6 1.3 %collective-permute-start.29 = (bf16[32,1024]{1,0:T(8,128)(2,1)S(1)}, bf16[32,1024]{1,0:T(8,128)(2,1)S(1)}, u32[]{:S(2)}, u32[]{:S(2)}) collective-permute-start(bf16[32,1024]{1,0:T(8,128)(2,1)S(1)} %get-tuple-element.38), channel_id=1, source_target_pairs={{1,0},{0,1},{3,2},{2,3},{5,4},{4,5},{7,6},{6,7},{9,8},{8,9},{11,10... | collective-permute-start | bytes 196616 | tf_op jit(solution)/shard_map/ppermute | solution.py:21

commit v3 on v2

v3 whole, which is shorter than its diff:
```python
import functools

import jax
import jax.numpy as jnp
from jax import lax
from jax.experimental import pallas as pl
from jax.experimental.pallas import tpu as pltpu
from jax.sharding import Mesh, PartitionSpec as P

F32 = jnp.float32
BF16 = jnp.bfloat16
VM = pl.BlockSpec(memory_space=pltpu.VMEM)
SM = pl.BlockSpec(memory_space=pltpu.SMEM)
ANY = pl.BlockSpec(memory_space=pl.ANY)
MIB = 1024 * 1024


def turn(shard, axis, by):
    count = lax.axis_size(axis)
    pairs = []
    for i in range(count):
        for core in range(2):
            source = (i + (by if core == 0 else -by)) % count
            pairs.append((source * 2 + core, i * 2 + core))
    return lax.ppermute(shard, (axis, "core"), pairs)


def from_ahead(shard, axis):
    return turn(shard, axis, 1)


def from_behind(shard, axis):
    return turn(shard, axis, -1)


def cross(shard, axes, by):
    sizes = [lax.axis_size(axis) for axis in ("x", "y")]
    pairs = []
    for i in range(sizes[0]):
        for j in range(sizes[1]):
            for core in range(2):
                source = {"x": i, "y": j}
                source[axes[core]] = (source[axes[core]] + by) % sizes[0]
                pairs.append((((source["x"] * sizes[1]) + source["y"]) * 2 + core, (i * sizes[1] + j) * 2 + core))
    return lax.ppermute(shard, ("x", "y", "core"), pairs)


def swap(shard):
    return lax.ppermute(shard, "core", [(0, 1), (1, 0)])


def call(body, out, name, ins, scratch=(), cost=(0, 0), room=8, **extra):
    return pl.pallas_call(
        body,
        out_shape=out,
        scratch_shapes=list(scratch),
        name=name,
        cost_estimate=pl.CostEstimate(flops=cost[0], bytes_accessed=cost[1], transcendentals=0),
        compiler_params=pltpu.CompilerParams(vmem_limit_bytes=room * MIB),
        **extra,
    )(*ins)


def shape(*sizes, dtype=BF16):
    return jax.ShapeDtypeStruct(sizes, dtype)


def in_vmem(array):
    return pltpu.with_memory_space_constraint(array, pltpu.VMEM)


def in_hbm(array):
    return pltpu.with_memory_space_constraint(array, pltpu.MemorySpace.HBM)


def make_bands(filters, out):
    groups, count = filters.shape
    lag = lax.broadcasted_iota(jnp.int32, (count, 2 * count), 0)
    column = lax.broadcasted_iota(jnp.int32, (count, 2 * count), 1)
    turned = (lag + column == count).astype(BF16)
    base = jnp.dot(filters[...].astype(BF16), turned, preferred_element_type=F32)
    for g in range(groups):
        row = jnp.broadcast_to(base[g : g + 1, :], (count, 2 * count))
        out[g * count : (g + 1) * count, :] = pltpu.roll(
            row, 0, 1, stride=1, stride_axis=0
        ).astype(BF16)


def three_taps(work, taps, stream, rows):
    return (
        taps[0, stream : stream + 1, :] * work[8 : 8 + rows, :]
        + taps[1, stream : stream + 1, :] * work[7 : 7 + rows, :]
        + taps[2, stream : stream + 1, :] * work[6 : 6 + rows, :]
    )


def project_kernel(half, place, *refs):
    pieces, weight = refs[:8], refs[8]
    if half == 0:
        filters, short, bias = refs[9:12]
        total, bands, taps, direct = refs[12:16]
        rows, held, row_sems, weight_sems, small, small_sems = refs[16:]
    else:
        before, taps = refs[9:11]
        out, edge = refs[-8:-6]
        rows, held, row_sems, weight_sems, total, work = refs[-6:]
    slots, _, tile, _ = held.shape
    parts, _, span = rows.shape
    per_part = span // tile
    steps = parts * per_part
    sign = 1 - 2 * place[1]

    def bring(n, t):
        far = sign * (n // 2)
        z = lax.rem(place[0] + (far if n % 2 == 0 else -far) + 4, 4)
        core = place[1] if n % 2 == 0 else 1 - place[1]
        row = pl.ds(pl.multiple_of(z * 64 + core * 32, 32), 32)
        depth = pl.ds((half * parts + t) * span, span)
        return pltpu.make_async_copy(pieces[n].at[:, depth], rows.at[t, row, :], row_sems.at[n, t])

    def fetch(k):
        depth = pl.ds((half * steps + k) * tile, tile)
        return pltpu.make_async_copy(
            weight.at[:, depth, :], held.at[k % slots], weight_sems.at[k % slots]
        )

    for n in range(8):
        bring(n, 0).start()
    for k in range(slots):
        fetch(k).start()
    if half == 0:
        little = [
            pltpu.make_async_copy(source, target, small_sems.at[n])
            for n, (source, target) in enumerate(((filters, small), (short, taps), (bias, direct)))
        ]
        for copy in little:
            copy.start()
    for t in range(1, parts):
        for n in range(8):
            bring(n, t).start()
    if half == 0:
        for copy in little:
            copy.wait()
        make_bands(small, bands)
        total[...] = jnp.zeros_like(total)
    else:
        total[...] = before[...]

    for t in range(parts):
        for n in range(8):
            bring(n, t).wait()
        for u in range(per_part):
            k = t * per_part + u
            fetch(k).wait()
            left = rows[t, :, u * tile : (u + 1) * tile]
            for s in range(3):
                total[:, s * 512 : (s + 1) * 512] += jnp.dot(
                    left, held[k % slots, s], preferred_element_type=F32
                )
            if k + slots < steps:
                fetch(k + slots).start()

    if half == 1:
        out[...] = total[...].astype(BF16)
        streams = []
        for s in (1, 2):
            work[...] = out[112:256, s * 512 : (s + 1) * 512].astype(F32)[8:, :]
            streams.append(three_taps(work, taps, s, 128))
        edge[0:128, :] = (streams[0] * streams[1]).astype(BF16)
        for s in range(3):
            edge[128 + 16 * s : 144 + 16 * s, :] = out[240:256, s * 512 : (s + 1) * 512]


def mix_kernel(projected, edge, taps, bias, bands, one, two, out, work, window, query):
    streams = []
    for s in range(3):
        work[0:8, :] = edge[128 + 16 * s : 144 + 16 * s, :].astype(F32)[8:16, :]
        work[8:264, :] = projected[:, s * 512 : (s + 1) * 512].astype(F32)
        featured = three_taps(work, taps, s, 256)
        if s == 0:
            query[...] = featured
        else:
            streams.append(featured)
    product = (streams[0] * streams[1]).astype(BF16)
    window[0:128, :] = edge[0:128, :]
    window[128:384, :] = product
    lane = lax.broadcasted_iota(jnp.int32, (128, 128), 1) // 16
    for j in range(4):
        columns = slice(j * 128, (j + 1) * 128)
        right = jnp.concatenate([window[0:256, columns], window[128:384, columns]], axis=1)
        result = jnp.dot(
            bands[j * 1024 : (j + 1) * 1024, :], right, preferred_element_type=F32
        )
        for block in range(2):
            filtered = jnp.zeros((128, 128), F32)
            for g in range(8):
                filtered = jnp.where(
                    lane == g,
                    result[g * 128 : (g + 1) * 128, block * 128 : (block + 1) * 128],
                    filtered,
                )
            rows = slice(block * 128, (block + 1) * 128)
            direct = window[128 + block * 128 : 256 + block * 128, columns].astype(F32)
            out[rows, columns] = (
                query[rows, columns] * (filtered + bias[:, columns] * direct)
            ).astype(BF16)


def out_kernel(count, blocks, place, gated, *refs):
    groups = refs[:count]
    keep, send, left = refs[count:]
    for m in range(2):
        core = place[1] if m == 0 else 1 - place[1]
        sign = 1 - 2 * core
        for n, by in enumerate((0, 1, -1, 2)):
            z = lax.rem(place[0] + sign * by + 4, 4)
            row = pl.multiple_of(z * 64 + core * 32, 32)
            at = m * 128 + n * 32
            left[at : at + 32, :] = gated[pl.ds(row, 32), :]
    labels = [block[0] for block in blocks]
    for at, ((near, far), group, n) in enumerate(blocks):
        result = jnp.dot(left[...], groups[group][n], preferred_element_type=F32).astype(BF16)
        to = labels.index((far, near))
        keep[:, at * 512 : (at + 1) * 512] = result[0:128]
        send[:, to * 512 : (to + 1) * 512] = result[128:256]


def pair_kernel(kept, got, *outs):
    for n, out in enumerate(outs):
        rows = slice(32 * n, 32 * (n + 1))
        out[...] = (kept[rows, :].astype(F32) + got[rows, :].astype(F32)).astype(BF16)


def join_kernel(a, b, out):
    out[...] = (a[...].astype(F32) + b[...].astype(F32)).astype(BF16)


def finish_kernel(plan, place, *refs):
    out = refs[-1]
    for h, labels in enumerate(plan):
        parts = refs[3 * h : 3 * h + 3]
        for n, (near, far) in enumerate(labels):
            x = lax.rem(place[2] + jnp.where(place[1] == 0, near, far) + 4, 4)
            y = lax.rem(place[3] + jnp.where(place[1] == 0, far, near) + 4, 4)
            column = pl.multiple_of((x * 4 + y) * 512, 512)
            at = slice(n * 512, (n + 1) * 512)
            total = parts[0][:, at].astype(F32)
            for part in parts[1:]:
                total += part[:, at].astype(F32)
            out[:, pl.ds(column, 512)] = total.astype(BF16)


def stack_kernel(count, *refs):
    sources, out, sems = refs[:count], refs[-2], refs[-1]
    copies = [
        pltpu.make_async_copy(source, out.at[n], sems.at[n]) for n, source in enumerate(sources)
    ]
    for copy in copies:
        copy.start()
    for copy in copies:
        copy.wait()


def stacked(arrays, after):
    count = len(arrays)
    return call(
        functools.partial(stack_kernel, count),
        shape(count, *arrays[0].shape),
        "stack",
        [*arrays, *after],
        [pltpu.SemaphoreType.DMA((count,))],
        (0, count * MIB),
        in_specs=[ANY] * (count + len(after)),
        out_specs=VM,
    )


def halves_kernel(ahead, behind, after, one, two, sems):
    copies = [
        pltpu.make_async_copy(ahead.at[pl.ds(0, 2)], one, sems.at[0]),
        pltpu.make_async_copy(behind.at[pl.ds(2, 2)], two, sems.at[1]),
    ]
    for copy in copies:
        copy.start()
    for copy in copies:
        copy.wait()


NEAR, FAR = ("x", "y"), ("y", "x")


def spread(block, after):
    blocks = [block] + [cross(block, NEAR, by) for by in (1, -1, 2)]
    own = stacked([in_hbm(block)] + [in_vmem(block) for block in blocks[1:]], after)
    return [own] + [cross(own, FAR, by) for by in (1, -1)]


def shards(tokens, in_weight, short_filter, mr_filter, mr_bias, out_weight):
    place = jnp.stack([lax.axis_index(a) for a in ("z", "core", "x", "y")]).astype(jnp.int32)

    pieces = []
    ahead = from_ahead(tokens, "z")
    for block in (tokens, ahead, from_ahead(ahead, "z"), from_behind(tokens, "z")):
        pieces += [block, swap(block)]
    pieces = [in_hbm(tokens)] + [in_vmem(piece) for piece in pieces[1:]]

    weights = spread(out_weight, [pieces[2], pieces[6]])

    weight = in_hbm(jnp.transpose(in_weight, (1, 0, 2)))
    parts, span, slots = 2, 2048, 5
    scratch = [
        pltpu.VMEM((parts, 256, span), BF16),
        pltpu.VMEM((slots, 3, 512, 512), BF16),
        pltpu.SemaphoreType.DMA((8, parts)),
        pltpu.SemaphoreType.DMA((slots,)),
    ]
    cost = (256 * 8192 * 1536, 14 * MIB)
    total, bands, taps, direct = call(
        functools.partial(project_kernel, 0),
        (
            shape(256, 1536, dtype=F32),
            shape(4096, 256),
            shape(3, 3, 512, dtype=F32),
            shape(1, 512, dtype=F32),
        ),
        "project",
        [
            place,
            *pieces,
            weight,
            in_hbm(mr_filter.T),
            in_hbm(short_filter),
            in_hbm(mr_bias.reshape(1, 512)),
        ],
        scratch + [pltpu.VMEM((32, 128), F32), pltpu.SemaphoreType.DMA((3,))],
        cost,
        16,
        in_specs=[SM] + [ANY] * 12,
        out_specs=(VM,) * 4,
    )
    relays = call(
        halves_kernel,
        (shape(2, 512, 512),) * 2,
        "halves",
        [*weights[1:], direct],
        [pltpu.SemaphoreType.DMA((2,))],
        (0, 4 * MIB),
        in_specs=[VM, VM, ANY],
        out_specs=(VM, VM),
    )
    weights += [cross(relays[0], FAR, 1), cross(relays[1], FAR, -1)]
    projected, edge = call(
        functools.partial(project_kernel, 1),
        (shape(256, 1536), shape(176, 512)),
        "project",
        [place, *pieces, weight, total, taps, relays[0]],
        scratch + [pltpu.VMEM((256, 1536), F32), pltpu.VMEM((136, 512), F32)],
        cost,
        18,
        in_specs=[SM] + [ANY] * 9 + [VM, VM, ANY],
        out_specs=(VM, VM),
    )

    context = ("x", "y")
    count = lax.axis_size(context)
    earlier = lax.ppermute(edge, context, [(i, i + 1) for i in range(count - 1)])
    gated = call(
        mix_kernel,
        shape(256, 512),
        "mix",
        [projected, earlier, taps, direct, bands, *weights[3:]],
        [pltpu.VMEM((264, 512), F32), pltpu.VMEM((384, 512), BF16), pltpu.VMEM((256, 512), F32)],
        (2 * 4096 * 256 * 256, 4 * MIB),
        in_specs=[VM] * 5 + [ANY] * 2,
        out_specs=VM,
    )

    steps = (0, 1, -1, 2)
    chunks = (
        (weights[:3], [((n, f), g, m) for g, f in enumerate(steps[:3]) for m, n in enumerate(steps[:3])]),
        (
            weights,
            [((2, f), g, 3) for g, f in enumerate(steps[:3])]
            + [((n, 2), 3 + m // 2, m % 2) for m, n in enumerate(steps)],
        ),
    )
    sums = []
    plan = []
    for groups, blocks in chunks:
        width = 512 * len(blocks)
        keep, send = call(
            functools.partial(out_kernel, len(groups), blocks),
            (shape(128, width),) * 2,
            "out",
            [place, gated, *groups],
            [pltpu.VMEM((256, 512), BF16)],
            (2 * 256 * 512 * width, 512 * width * 2),
            in_specs=[SM] + [VM] * (1 + len(groups)),
            out_specs=(VM, VM),
        )
        here, front, back, across = call(
            pair_kernel,
            (shape(32, width),) * 4,
            "pair",
            [keep, swap(send)],
            cost=(0, 768 * width),
            in_specs=[VM, VM],
            out_specs=(VM,) * 4,
        )
        back = from_ahead(back, "z")
        joined = call(
            join_kernel,
            shape(32, width),
            "join",
            [front, from_behind(across, "z")],
            cost=(0, 192 * width),
            in_specs=[VM, VM],
            out_specs=VM,
        )
        parts = [here, back, from_behind(joined, "z")]
        sums += parts
        plan.append([block[0] for block in blocks])
    return call(
        functools.partial(finish_kernel, plan),
        shape(32, 8192),
        "finish",
        [place, *sums],
        cost=(0, 3 * MIB),
        in_specs=[SM] + [VM] * len(sums),
        out_specs=VM,
    )


def solution(mesh):
    grid = Mesh(mesh.devices.reshape(4, 4, 4, 2), ("x", "y", "z", "core"))
    channels = ("z", "core")
    context = ("x", "y")
    return jax.shard_map(
        shards,
        mesh=grid,
        in_specs=(
            P(context + channels, None),
            P(None, None, channels),
            P(None, None, channels),
            P(None, channels),
            P(channels),
            P(channels, context),
        ),
        out_specs=P(context + channels, None),
        check_vma=False,
    )
```

time: 115 us -> 105 us (0.913)
  starting transfers between devices: 41.3 us -> 30 us
  Pallas kernels: 22.2 us -> 30.3 us
  local copies, waits for them, and re-layouts: 6.07 us -> 1.84 us
  waiting for transfers between devices: 44.3 us -> 42.4 us
    ppermute x29 -> x22, starting transfers between devices: 39.4 us -> 27.5 us  [the longest x9 13.5 us: turn(): return lax.ppermute(shard, (axis, 'core'), pairs)]
    pallas_call x8 -> x12, Pallas kernels: 22.2 us -> 30.3 us  [call(): pl.pallas_call(body, out_shape=out, scratch_shapes=list(scratch), name=na...]
    unnamed x12 -> x6, local copies, waits for them, and re-layouts: 5.01 us -> 1.84 us
    ppermute x1, waiting for transfers between devices: 9.57 us -> 6.97 us  [shards(): lax.ppermute(edge, context, [(i, i + 1) for i in range(count - 1)])]
    ppermute x29 -> x22, waiting for transfers between devices: 34.7 us -> 35.4 us  [the longest x9 21 us: turn(): return lax.ppermute(shard, (axis, 'core'), pairs)]
  transfers between devices with their start and end apart: 30 -> 23, of which waited for: 14 -> 14; matrix products, arithmetic and copies ran while one was open for 0% -> 0% of each run, Pallas kernels for 18% -> 20%
where the time goes in v3:
time: 105 us
  waiting for transfers between devices  42.4 us (40%)
  Pallas kernels  30.3 us (29%)
  starting transfers between devices  30 us (29%)
  local copies, waits for them, and re-layouts  1.84 us (2%)
    pallas_call x12, Pallas kernels, call(): pl.pallas_call(body, out_shape=out, scratch_shapes=list(scratch), name=na...  30.3 us
    ppermute x9, waiting for transfers between devices, turn(): return lax.ppermute(shard, (axis, 'core'), pairs)  21 us
    ppermute x9, starting transfers between devices, turn(): return lax.ppermute(shard, (axis, 'core'), pairs)  13.5 us
    ppermute x7, starting transfers between devices, cross(): return lax.ppermute(shard, ('x', 'y', 'core'), pairs)  11.9 us
    ppermute x7, waiting for transfers between devices, cross(): return lax.ppermute(shard, ('x', 'y', 'core'), pairs)  11 us
    ppermute x1, waiting for transfers between devices, shards(): lax.ppermute(edge, context, [(i, i + 1) for i in range(count - 1)])  6.97 us
    ppermute x6, waiting for transfers between devices, swap(): return lax.ppermute(shard, 'core', [(0, 1), (1, 0)])  3.4 us
    ppermute x1, starting transfers between devices, shards(): lax.ppermute(edge, context, [(i, i + 1) for i in range(count - 1)])  2.52 us
  transfers between devices with their start and end apart: 23, of which 14 were waited for; matrix products, arithmetic and copies ran while one was open for 0% of the time, Pallas kernels for 20%

profile of v3, /device:TPU:2, one launch (start us, length us, event | category | flops | bytes accessed | tf_op | source)
XLA Modules:
  0.0 104.8 jit_solution(2211513656390585826)
XLA Ops:
  0.0 0.0 copy-start.2
  0.0 1.5 %collective-permute-start.8 = (bf16[512,512]{1,0:T(8,128)(2,1)}, bf16[512,512]{1,0:T(8,128)(2,1)S(1)}, u32[]{:S(2)}, u32[]{:S(2)}) collective-permute-start(bf16[512,512]{1,0:T(8,128)(2,1)} %refs_0_.4), channel_id=1, source_target_pairs={{96,0},{25,1},{104,8},{1,9},{112,16},{9,17},{120,24},{17,25},{0,32... | collective-permute-start | bytes 1572872 | tf_op jit(solution)/shard_map/ppermute | solution.py:45
  1.5 0.5 collective-permute-start.7
  2.0 2.1 %collective-permute-start.9 = (bf16[512,512]{1,0:T(8,128)(2,1)}, bf16[512,512]{1,0:T(8,128)(2,1)S(1)}, u32[]{:S(2)}, u32[]{:S(2)}) collective-permute-start(bf16[512,512]{1,0:T(8,128)(2,1)} %refs_0_.4), channel_id=1, source_target_pairs={{64,0},{17,1},{72,8},{25,9},{80,16},{1,17},{88,24},{9,25},{96,32},... | collective-permute-start | bytes 1572872 | tf_op jit(solution)/shard_map/ppermute | solution.py:45
  4.2 1.9 %collective-permute-start.5 = (bf16[32,8192]{1,0:T(8,128)(2,1)}, bf16[32,8192]{1,0:T(8,128)(2,1)S(1)}, u32[]{:S(2)}, u32[]{:S(2)}) collective-permute-start(bf16[32,8192]{1,0:T(8,128)(2,1)} %refs_0_.5), channel_id=1, source_target_pairs={{6,0},{3,1},{0,2},{5,3},{2,4},{7,5},{4,6},{1,7},{14,8},{11,9},{8,1... | collective-permute-start | bytes 1572872 | tf_op jit(solution)/shard_map/ppermute | solution.py:25
  6.1 2.1 %collective-permute-start.1 = (bf16[32,8192]{1,0:T(8,128)(2,1)}, bf16[32,8192]{1,0:T(8,128)(2,1)S(1)}, u32[]{:S(2)}, u32[]{:S(2)}) collective-permute-start(bf16[32,8192]{1,0:T(8,128)(2,1)} %refs_0_.5), channel_id=1, source_target_pairs={{2,0},{7,1},{4,2},{1,3},{6,4},{3,5},{0,6},{5,7},{10,8},{15,9},{12,... | collective-permute-start | bytes 1572872 | tf_op jit(solution)/shard_map/ppermute | solution.py:25
  8.2 1.2 %collective-permute-done.8.refs_2_ = bf16[512,512]{1,0:T(8,128)(2,1)S(1)} collective-permute-done((bf16[512,512]{1,0:T(8,128)(2,1)}, bf16[512,512]{1,0:T(8,128)(2,1)S(1)}, u32[]{:S(2)}, u32[]{:S(2)}) %collective-permute-start.8) | collective-permute-done | bytes 524320 | tf_op jit(solution)/shard_map/ppermute | solution.py:45
  9.4 1.5 %collective-permute-done.7.refs_1_ = bf16[512,512]{1,0:T(8,128)(2,1)S(1)} collective-permute-done((bf16[512,512]{1,0:T(8,128)(2,1)}, bf16[512,512]{1,0:T(8,128)(2,1)S(1)}, u32[]{:S(2)}, u32[]{:S(2)}) %collective-permute-start.7) | collective-permute-done | bytes 524320 | tf_op jit(solution)/shard_map/ppermute | solution.py:45
  10.9 6.3 %collective-permute-done.9.refs_3_ = bf16[512,512]{1,0:T(8,128)(2,1)S(1)} collective-permute-done((bf16[512,512]{1,0:T(8,128)(2,1)}, bf16[512,512]{1,0:T(8,128)(2,1)S(1)}, u32[]{:S(2)}, u32[]{:S(2)}) %collective-permute-start.9) | collective-permute-done | bytes 524320 | tf_op jit(solution)/shard_map/ppermute | solution.py:45
  17.1 1.9 %collective-permute-done.5.refs_6_.refs_5_ = bf16[32,8192]{1,0:T(8,128)(2,1)S(1)} collective-permute-done((bf16[32,8192]{1,0:T(8,128)(2,1)}, bf16[32,8192]{1,0:T(8,128)(2,1)S(1)}, u32[]{:S(2)}, u32[]{:S(2)}) %collective-permute-start.5) | collective-permute-done | bytes 524320 | tf_op jit(solution)/shard_map/ppermute | solution.py:25
  19.1 0.9 collective-permute-done.1.refs_2_.refs_4_
  19.9 1.1 %stack.21.refs_0_ = bf16[4,512,512]{2,1,0:T(8,128)(2,1)S(1)} custom-call(bf16[512,512]{1,0:T(8,128)(2,1)} %refs_0_.4, bf16[512,512]{1,0:T(8,128)(2,1)S(1)} %collective-permute-done.7.refs_1_, bf16[512,512]{1,0:T(8,128)(2,1)S(1)} %collective-permute-done.8.refs_2_, bf16[512,512]{1,0:T(8,128)(2,1)S(1)} %collective-permute-done.9.refs_3_, ...), custom_call_target="tpu_custom_call" | custom-call | bytes 4194304 | tf_op jit(solution)/shard_map/stack/pallas_call | solution.py:53
  21.0 1.7 %collective-permute-start.11 = (bf16[4,512,512]{2,1,0:T(8,128)(2,1)S(1)}, bf16[4,512,512]{2,1,0:T(8,128)(2,1)}, u32[]{:S(2)}, u32[]{:S(2)}) collective-permute-start(bf16[4,512,512]{2,1,0:T(8,128)(2,1)S(1)} %stack.21.refs_0_), channel_id=1, source_target_pairs={{24,0},{97,1},{0,8},{105,9},{8,16},{113,17},{16,24},{121,25},{56,3... | collective-permute-start | bytes 6291464 | tf_op jit(solution)/shard_map/ppermute | solution.py:45
  22.7 2.6 %collective-permute-start.10 = (bf16[4,512,512]{2,1,0:T(8,128)(2,1)S(1)}, bf16[4,512,512]{2,1,0:T(8,128)(2,1)}, u32[]{:S(2)}, u32[]{:S(2)}) collective-permute-start(bf16[4,512,512]{2,1,0:T(8,128)(2,1)S(1)} %stack.21.refs_0_), channel_id=1, source_target_pairs={{8,0},{33,1},{16,8},{41,9},{24,16},{49,17},{0,24},{57,25},{40,32},... | collective-permute-start | bytes 6291464 | tf_op jit(solution)/shard_map/ppermute | solution.py:45
  25.3 0.0 copy-done.2
  25.3 0.0 collective-permute-start
  25.4 2.6 %collective-permute-start.3 = (bf16[32,8192]{1,0:T(8,128)(2,1)S(1)}, bf16[32,8192]{1,0:T(8,128)(2,1)}, u32[]{:S(2)}, u32[]{:S(2)}) collective-permute-start(bf16[32,8192]{1,0:T(8,128)(2,1)S(1)} %collective-permute-done.1.refs_2_.refs_4_), channel_id=1, source_target_pairs={{2,0},{7,1},{4,2},{1,3},{6,4},{3,5},{0,6},{5,7},{10,8},{15,9},{12,... | collective-permute-start | bytes 1572872 | tf_op jit(solution)/shard_map/ppermute | solution.py:25
  27.9 0.0 collective-permute-start.6
  27.9 0.0 collective-permute-done.refs_1_
  27.9 0.0 copy-start
  27.9 0.8 copy-done
  28.7 0.5 collective-permute-start.2
  29.2 5.4 %collective-permute-done.3.refs_4_ = bf16[32,8192]{1,0:T(8,128)(2,1)} collective-permute-done((bf16[32,8192]{1,0:T(8,128)(2,1)S(1)}, bf16[32,8192]{1,0:T(8,128)(2,1)}, u32[]{:S(2)}, u32[]{:S(2)}) %collective-permute-start.3) | collective-permute-done | bytes 524320 | tf_op jit(solution)/shard_map/ppermute | solution.py:25
  34.6 0.9 collective-permute-start.4
  35.5 0.1 pad_add_fusion.place
  35.6 0.0 collective-permute-done.6.refs_7_
  35.6 0.0 collective-permute-done.2.refs_3_
  35.6 1.8 %collective-permute-done.4.refs_5_ = bf16[32,8192]{1,0:T(8,128)(2,1)} collective-permute-done((bf16[32,8192]{1,0:T(8,128)(2,1)}, bf16[32,8192]{1,0:T(8,128)(2,1)}, u32[]{:S(2)}, u32[]{:S(2)}) %collective-permute-start.4) | collective-permute-done | bytes 524320 | tf_op jit(solution)/shard_map/ppermute | solution.py:49
  37.4 1.0 copy-done.1
  38.4 8.9 %project.2 = (f32[256,1536]{1,0:T(8,128)S(1)}, bf16[4096,256]{1,0:T(8,128)(2,1)S(1)}, f32[3,3,512]{2,1,0:T(4,128)S(1)}, f32[1,512]{1,0:T(1,128)S(1)}) custom-call(s32[4]{0:T(128)S(1)} %pad_add_fusion.place, bf16[32,8192]{1,0:T(8,128)(2,1)} %refs_0_.5, bf16[32,8192]{1,0:T(8,128)(2,1)S(1)} %copy-done.1, ...), custom_call_target="tpu_custom_call" | custom-call | flops 3221225472 | bytes 14680064 | tf_op jit(solution)/shard_map/project/pallas_call | solution.py:53
  47.3 2.0 %collective-permute-done.11.behind.refs_2_ = bf16[4,512,512]{2,1,0:T(8,128)(2,1)} collective-permute-done((bf16[4,512,512]{2,1,0:T(8,128)(2,1)S(1)}, bf16[4,512,512]{2,1,0:T(8,128)(2,1)}, u32[]{:S(2)}, u32[]{:S(2)}) %collective-permute-start.11) | collective-permute-done | bytes 2097184 | tf_op jit(solution)/shard_map/ppermute | solution.py:45
  49.4 0.0 collective-permute-done.10.ahead.refs_1_
  49.4 2.4 %halves.1 = (bf16[2,512,512]{2,1,0:T(8,128)(2,1)S(1)}, bf16[2,512,512]{2,1,0:T(8,128)(2,1)S(1)}) custom-call(bf16[4,512,512]{2,1,0:T(8,128)(2,1)} %collective-permute-done.10.ahead.refs_1_, bf16[4,512,512]{2,1,0:T(8,128)(2,1)} %collective-permute-done.11.behind.refs_2_, f32[1,512]{1,0:T(1,128)S(1)} %get-tuple-element.27.after.bias), custom_call_target="tpu_custom_call" | custom-call | bytes 4194304 | tf_op jit(solution)/shard_map/halves/pallas_call | solution.py:53
  51.8 1.9 %collective-permute-start.14 = (bf16[2,512,512]{2,1,0:T(8,128)(2,1)S(1)}, bf16[2,512,512]{2,1,0:T(8,128)(2,1)S(1)}, u32[]{:S(2)}, u32[]{:S(2)}) collective-permute-start(bf16[2,512,512]{2,1,0:T(8,128)(2,1)S(1)} %get-tuple-element.32), channel_id=1, source_target_pairs={{24,0},{97,1},{0,8},{105,9},{8,16},{113,17},{16,24},{121,25},{56,3... | collective-permute-start | bytes 3145736 | tf_op jit(solution)/shard_map/ppermute | solution.py:45
  53.6 1.6 %collective-permute-start.13 = (bf16[2,512,512]{2,1,0:T(8,128)(2,1)S(1)}, bf16[2,512,512]{2,1,0:T(8,128)(2,1)S(1)}, u32[]{:S(2)}, u32[]{:S(2)}) collective-permute-start(bf16[2,512,512]{2,1,0:T(8,128)(2,1)S(1)} %get-tuple-element.28.refs_11_), channel_id=1, source_target_pairs={{8,0},{33,1},{16,8},{41,9},{24,16},{49,17},{0,24},{57,25},{40,32},... | collective-permute-start | bytes 3145736 | tf_op jit(solution)/shard_map/ppermute | solution.py:45
  55.2 7.7 %project.3 = (bf16[256,1536]{1,0:T(8,128)(2,1)S(1)}, bf16[176,512]{1,0:T(8,128)(2,1)S(1)}) custom-call(s32[4]{0:T(128)S(1)} %pad_add_fusion.place, bf16[32,8192]{1,0:T(8,128)(2,1)} %refs_0_.5, bf16[32,8192]{1,0:T(8,128)(2,1)S(1)} %copy-done.1, bf16[32,8192]{1,0:T(8,128)(2,1)S(1)} %collective-permute-done.1.refs_2_.refs_4_, ...), custom_call_target="tpu_custom_call" | custom-call | flops 3221225472 | bytes 14680064 | tf_op jit(solution)/shard_map/project/pallas_call | solution.py:53
  63.0 2.5 %collective-permute-start.12 = (bf16[176,512]{1,0:T(8,128)(2,1)S(1)}, bf16[176,512]{1,0:T(8,128)(2,1)S(1)}, u32[]{:S(2)}, u32[]{:S(2)}) collective-permute-start(bf16[176,512]{1,0:T(8,128)(2,1)S(1)} %get-tuple-element.30), channel_id=1, source_target_pairs={{0,8},{8,16},{16,24},{24,32},{32,40},{40,48},{48,56},{56,64},{64,7... | collective-permute-start | bytes 540680 | tf_op jit(solution)/shard_map/ppermute | solution.py:366
  65.5 7.0 %collective-permute-done.12.edge = bf16[176,512]{1,0:T(8,128)(2,1)S(1)} collective-permute-done((bf16[176,512]{1,0:T(8,128)(2,1)S(1)}, bf16[176,512]{1,0:T(8,128)(2,1)S(1)}, u32[]{:S(2)}, u32[]{:S(2)}) %collective-permute-start.12) | collective-permute-done | bytes 180256 | tf_op jit(solution)/shard_map/ppermute | solution.py:366
  72.5 0.0 collective-permute-done.14.two.refs_4_
  72.5 0.0 collective-permute-done.13.one.refs_3_
  72.5 1.1 %mix.1.gated = bf16[256,512]{1,0:T(8,128)(2,1)S(1)} custom-call(bf16[256,1536]{1,0:T(8,128)(2,1)S(1)} %get-tuple-element.29.projected, bf16[176,512]{1,0:T(8,128)(2,1)S(1)} %collective-permute-done.12.edge, f32[3,3,512]{2,1,0:T(4,128)S(1)} %get-tuple-element.26.refs_10_.taps, f32[1,512]{1,0:T(1,128)S(1)} %get-tuple-element.27.after.bias, ...), custom_call_target="tpu_custom_call" | custom-call | flops 536870912 | bytes 4194304 | tf_op jit(solution)/shard_map/mix/pallas_call | solution.py:53
  73.6 3.6 %out.2 = (bf16[128,4608]{1,0:T(8,128)(2,1)S(1)}, bf16[128,4608]{1,0:T(8,128)(2,1)S(1)}) custom-call(s32[4]{0:T(128)S(1)} %pad_add_fusion.place, bf16[256,512]{1,0:T(8,128)(2,1)S(1)} %mix.1.gated, bf16[4,512,512]{2,1,0:T(8,128)(2,1)S(1)} %stack.21.refs_0_, bf16[4,512,512]{2,1,0:T(8,128)(2,1)} %collective-permute-done.10.ahead.refs_1_, ...), custom_call_target="tpu_custom_call" | custom-call | flops 1207959552 | bytes 4718592 | tf_op jit(solution)/shard_map/out/pallas_call | solution.py:53
  77.3 0.1 collective-permute-start.15
  77.3 3.4 %out.3 = (bf16[128,3584]{1,0:T(8,128)(2,1)S(1)}, bf16[128,3584]{1,0:T(8,128)(2,1)S(1)}) custom-call(s32[4]{0:T(128)S(1)} %pad_add_fusion.place, bf16[256,512]{1,0:T(8,128)(2,1)S(1)} %mix.1.gated, bf16[4,512,512]{2,1,0:T(8,128)(2,1)S(1)} %stack.21.refs_0_, bf16[4,512,512]{2,1,0:T(8,128)(2,1)} %collective-permute-done.10.ahead.refs_1_, ...), custom_call_target="tpu_custom_call" | custom-call | flops 939524096 | bytes 3670016 | tf_op jit(solution)/shard_map/out/pallas_call | solution.py:53
  80.7 0.6 collective-permute-start.19
  81.3 0.0 collective-permute-done.15.got
  81.3 0.3 pair.2
  81.6 0.2 collective-permute-start.17
  81.8 1.6 %collective-permute-done.19.got = bf16[128,3584]{1,0:T(8,128)(2,1)S(1)} collective-permute-done((bf16[128,3584]{1,0:T(8,128)(2,1)S(1)}, bf16[128,3584]{1,0:T(8,128)(2,1)S(1)}, u32[]{:S(2)}, u32[]{:S(2)}) %collective-permute-start.19) | collective-permute-done | bytes 917536 | tf_op jit(solution)/shard_map/ppermute | solution.py:49
  83.4 0.2 pair.3
  83.6 0.2 collective-permute-start.21
  83.8 3.1 %collective-permute-start.16 = (bf16[32,4608]{1,0:T(8,128)(2,1)S(1)}, bf16[32,4608]{1,0:T(8,128)(2,1)S(1)}, u32[]{:S(2)}, u32[]{:S(2)}) collective-permute-start(bf16[32,4608]{1,0:T(8,128)(2,1)S(1)} %get-tuple-element.36), channel_id=1, source_target_pairs={{2,0},{7,1},{4,2},{1,3},{6,4},{3,5},{0,6},{5,7},{10,8},{15,9},{12,... | collective-permute-start | bytes 884744 | tf_op jit(solution)/shard_map/ppermute | solution.py:25
  86.9 2.7 %collective-permute-done.17.b = bf16[32,4608]{1,0:T(8,128)(2,1)S(1)} collective-permute-done((bf16[32,4608]{1,0:T(8,128)(2,1)S(1)}, bf16[32,4608]{1,0:T(8,128)(2,1)S(1)}, u32[]{:S(2)}, u32[]{:S(2)}) %collective-permute-start.17) | collective-permute-done | bytes 294944 | tf_op jit(solution)/shard_map/ppermute | solution.py:25
  89.6 0.1 join.2
  89.6 0.1 collective-permute-start.18
  89.7 3.2 %collective-permute-start.20 = (bf16[32,3584]{1,0:T(8,128)(2,1)S(1)}, bf16[32,3584]{1,0:T(8,128)(2,1)S(1)}, u32[]{:S(2)}, u32[]{:S(2)}) collective-permute-start(bf16[32,3584]{1,0:T(8,128)(2,1)S(1)} %get-tuple-element.42), channel_id=1, source_target_pairs={{2,0},{7,1},{4,2},{1,3},{6,4},{3,5},{0,6},{5,7},{10,8},{15,9},{12,... | collective-permute-start | bytes 688136 | tf_op jit(solution)/shard_map/ppermute | solution.py:25
  92.9 0.9 collective-permute-done.21.b
  93.9 0.1 join.3
  93.9 0.1 collective-permute-start.22
  94.0 5.3 %collective-permute-done.20.refs_4_ = bf16[32,3584]{1,0:T(8,128)(2,1)S(1)} collective-permute-done((bf16[32,3584]{1,0:T(8,128)(2,1)S(1)}, bf16[32,3584]{1,0:T(8,128)(2,1)S(1)}, u32[]{:S(2)}, u32[]{:S(2)}) %collective-permute-start.20) | collective-permute-done | bytes 229408 | tf_op jit(solution)/shard_map/ppermute | solution.py:25
  99.3 4.0 %collective-permute-done.22.refs_5_ = bf16[32,3584]{1,0:T(8,128)(2,1)S(1)} collective-permute-done((bf16[32,3584]{1,0:T(8,128)(2,1)S(1)}, bf16[32,3584]{1,0:T(8,128)(2,1)S(1)}, u32[]{:S(2)}, u32[]{:S(2)}) %collective-permute-start.22) | collective-permute-done | bytes 229408 | tf_op jit(solution)/shard_map/ppermute | solution.py:25
  103.3 0.0 collective-permute-done.16.refs_1_
  103.3 0.0 collective-permute-done.18.refs_2_
  103.3 1.5 %finish.1 = bf16[32,8192]{1,0:T(8,128)(2,1)} custom-call(s32[4]{0:T(128)S(1)} %pad_add_fusion.place, bf16[32,4608]{1,0:T(8,128)(2,1)S(1)} %get-tuple-element.35.refs_0_, bf16[32,4608]{1,0:T(8,128)(2,1)S(1)} %collective-permute-done.16.refs_1_, bf16[32,4608]{1,0:T(8,128)(2,1)S(1)} %collective-permute-done.18.refs_2_, ...), custom_call_target="tpu_custom_call" | custom-call | bytes 3145728 | tf_op jit(solution)/shard_map/finish/pallas_call | solution.py:53
  (1 shorter events, 0.0 us)
Async XLA Ops:
  0.0 25.3 %copy-start.2 = (bf16[32,8192]{1,0:T(8,128)(2,1)S(1)}, bf16[32,8192]{1,0:T(8,128)(2,1)}, u32[]{:S(2)}) copy-start(bf16[32,8192]{1,0:T(8,128)(2,1)} %refs_0_.5) | copy-start | bytes 1572868
  0.0 9.4 %collective-permute-start.8 = (bf16[512,512]{1,0:T(8,128)(2,1)}, bf16[512,512]{1,0:T(8,128)(2,1)S(1)}, u32[]{:S(2)}, u32[]{:S(2)}) collective-permute-start(bf16[512,512]{1,0:T(8,128)(2,1)} %refs_0_.4), channel_id=1, source_target_pairs={{96,0},{25,1},{104,8},{1,9},{112,16},{9,17},{120,24},{17,25},{0,32... | collective-permute-start | bytes 1572872 | tf_op jit(solution)/shard_map/ppermute | solution.py:45
  1.5 9.4 %collective-permute-start.7 = (bf16[512,512]{1,0:T(8,128)(2,1)}, bf16[512,512]{1,0:T(8,128)(2,1)S(1)}, u32[]{:S(2)}, u32[]{:S(2)}) collective-permute-start(bf16[512,512]{1,0:T(8,128)(2,1)} %refs_0_.4), channel_id=1, source_target_pairs={{32,0},{9,1},{40,8},{17,9},{48,16},{25,17},{56,24},{1,25},{64,32},... | collective-permute-start | bytes 1572872 | tf_op jit(solution)/shard_map/ppermute | solution.py:45
  2.0 15.1 %collective-permute-start.9 = (bf16[512,512]{1,0:T(8,128)(2,1)}, bf16[512,512]{1,0:T(8,128)(2,1)S(1)}, u32[]{:S(2)}, u32[]{:S(2)}) collective-permute-start(bf16[512,512]{1,0:T(8,128)(2,1)} %refs_0_.4), channel_id=1, source_target_pairs={{64,0},{17,1},{72,8},{25,9},{80,16},{1,17},{88,24},{9,25},{96,32},... | collective-permute-start | bytes 1572872 | tf_op jit(solution)/shard_map/ppermute | solution.py:45
  4.2 14.9 %collective-permute-start.5 = (bf16[32,8192]{1,0:T(8,128)(2,1)}, bf16[32,8192]{1,0:T(8,128)(2,1)S(1)}, u32[]{:S(2)}, u32[]{:S(2)}) collective-permute-start(bf16[32,8192]{1,0:T(8,128)(2,1)} %refs_0_.5), channel_id=1, source_target_pairs={{6,0},{3,1},{0,2},{5,3},{2,4},{7,5},{4,6},{1,7},{14,8},{11,9},{8,1... | collective-permute-start | bytes 1572872 | tf_op jit(solution)/shard_map/ppermute | solution.py:25
  6.1 13.8 %collective-permute-start.1 = (bf16[32,8192]{1,0:T(8,128)(2,1)}, bf16[32,8192]{1,0:T(8,128)(2,1)S(1)}, u32[]{:S(2)}, u32[]{:S(2)}) collective-permute-start(bf16[32,8192]{1,0:T(8,128)(2,1)} %refs_0_.5), channel_id=1, source_target_pairs={{2,0},{7,1},{4,2},{1,3},{6,4},{3,5},{0,6},{5,7},{10,8},{15,9},{12,... | collective-permute-start | bytes 1572872 | tf_op jit(solution)/shard_map/ppermute | solution.py:25
  21.0 28.4 %collective-permute-start.11 = (bf16[4,512,512]{2,1,0:T(8,128)(2,1)S(1)}, bf16[4,512,512]{2,1,0:T(8,128)(2,1)}, u32[]{:S(2)}, u32[]{:S(2)}) collective-permute-start(bf16[4,512,512]{2,1,0:T(8,128)(2,1)S(1)} %stack.21.refs_0_), channel_id=1, source_target_pairs={{24,0},{97,1},{0,8},{105,9},{8,16},{113,17},{16,24},{121,25},{56,3... | collective-permute-start | bytes 6291464 | tf_op jit(solution)/shard_map/ppermute | solution.py:45
  22.7 26.6 %collective-permute-start.10 = (bf16[4,512,512]{2,1,0:T(8,128)(2,1)S(1)}, bf16[4,512,512]{2,1,0:T(8,128)(2,1)}, u32[]{:S(2)}, u32[]{:S(2)}) collective-permute-start(bf16[4,512,512]{2,1,0:T(8,128)(2,1)S(1)} %stack.21.refs_0_), channel_id=1, source_target_pairs={{8,0},{33,1},{16,8},{41,9},{24,16},{49,17},{0,24},{57,25},{40,32},... | collective-permute-start | bytes 6291464 | tf_op jit(solution)/shard_map/ppermute | solution.py:45
  25.3 2.6 %collective-permute-start = (bf16[32,8192]{1,0:T(8,128)(2,1)S(1)}, bf16[32,8192]{1,0:T(8,128)(2,1)S(1)}, u32[]{:S(2)}, u32[]{:S(2)}) collective-permute-start(bf16[32,8192]{1,0:T(8,128)(2,1)S(1)} %copy-done.2), channel_id=1, source_target_pairs={{0,1},{1,0},{2,3},{3,2},{4,5},{5,4},{6,7},{7,6},{8,9},{9,8},{10,11... | collective-permute-start | bytes 1572872 | tf_op jit(solution)/shard_map/ppermute | solution.py:49
  25.4 9.3 %collective-permute-start.3 = (bf16[32,8192]{1,0:T(8,128)(2,1)S(1)}, bf16[32,8192]{1,0:T(8,128)(2,1)}, u32[]{:S(2)}, u32[]{:S(2)}) collective-permute-start(bf16[32,8192]{1,0:T(8,128)(2,1)S(1)} %collective-permute-done.1.refs_2_.refs_4_), channel_id=1, source_target_pairs={{2,0},{7,1},{4,2},{1,3},{6,4},{3,5},{0,6},{5,7},{10,8},{15,9},{12,... | collective-permute-start | bytes 1572872 | tf_op jit(solution)/shard_map/ppermute | solution.py:25
  27.9 7.7 %collective-permute-start.6 = (bf16[32,8192]{1,0:T(8,128)(2,1)S(1)}, bf16[32,8192]{1,0:T(8,128)(2,1)}, u32[]{:S(2)}, u32[]{:S(2)}) collective-permute-start(bf16[32,8192]{1,0:T(8,128)(2,1)S(1)} %collective-permute-done.5.refs_6_.refs_5_), channel_id=1, source_target_pairs={{0,1},{1,0},{2,3},{3,2},{4,5},{5,4},{6,7},{7,6},{8,9},{9,8},{10,11... | collective-permute-start | bytes 1572872 | tf_op jit(solution)/shard_map/ppermute | solution.py:49
  27.9 0.8 copy-start
  28.7 6.9 %collective-permute-start.2 = (bf16[32,8192]{1,0:T(8,128)(2,1)S(1)}, bf16[32,8192]{1,0:T(8,128)(2,1)}, u32[]{:S(2)}, u32[]{:S(2)}) collective-permute-start(bf16[32,8192]{1,0:T(8,128)(2,1)S(1)} %collective-permute-done.1.refs_2_.refs_4_), channel_id=1, source_target_pairs={{0,1},{1,0},{2,3},{3,2},{4,5},{5,4},{6,7},{7,6},{8,9},{9,8},{10,11... | collective-permute-start | bytes 1572872 | tf_op jit(solution)/shard_map/ppermute | solution.py:49
  34.6 2.7 %collective-permute-start.4 = (bf16[32,8192]{1,0:T(8,128)(2,1)}, bf16[32,8192]{1,0:T(8,128)(2,1)}, u32[]{:S(2)}, u32[]{:S(2)}) collective-permute-start(bf16[32,8192]{1,0:T(8,128)(2,1)} %collective-permute-done.3.refs_4_), channel_id=1, source_target_pairs={{0,1},{1,0},{2,3},{3,2},{4,5},{5,4},{6,7},{7,6},{8,9},{9,8},{10,11... | collective-permute-start | bytes 1572872 | tf_op jit(solution)/shard_map/ppermute | solution.py:49
  37.4 1.0 copy-start.1
  51.8 20.7 %collective-permute-start.14 = (bf16[2,512,512]{2,1,0:T(8,128)(2,1)S(1)}, bf16[2,512,512]{2,1,0:T(8,128)(2,1)S(1)}, u32[]{:S(2)}, u32[]{:S(2)}) collective-permute-start(bf16[2,512,512]{2,1,0:T(8,128)(2,1)S(1)} %get-tuple-element.32), channel_id=1, source_target_pairs={{24,0},{97,1},{0,8},{105,9},{8,16},{113,17},{16,24},{121,25},{56,3... | collective-permute-start | bytes 3145736 | tf_op jit(solution)/shard_map/ppermute | solution.py:45
  53.6 18.8 %collective-permute-start.13 = (bf16[2,512,512]{2,1,0:T(8,128)(2,1)S(1)}, bf16[2,512,512]{2,1,0:T(8,128)(2,1)S(1)}, u32[]{:S(2)}, u32[]{:S(2)}) collective-permute-start(bf16[2,512,512]{2,1,0:T(8,128)(2,1)S(1)} %get-tuple-element.28.refs_11_), channel_id=1, source_target_pairs={{8,0},{33,1},{16,8},{41,9},{24,16},{49,17},{0,24},{57,25},{40,32},... | collective-permute-start | bytes 3145736 | tf_op jit(solution)/shard_map/ppermute | solution.py:45
  63.0 9.5 %collective-permute-start.12 = (bf16[176,512]{1,0:T(8,128)(2,1)S(1)}, bf16[176,512]{1,0:T(8,128)(2,1)S(1)}, u32[]{:S(2)}, u32[]{:S(2)}) collective-permute-start(bf16[176,512]{1,0:T(8,128)(2,1)S(1)} %get-tuple-element.30), channel_id=1, source_target_pairs={{0,8},{8,16},{16,24},{24,32},{32,40},{40,48},{48,56},{56,64},{64,7... | collective-permute-start | bytes 540680 | tf_op jit(solution)/shard_map/ppermute | solution.py:366
  77.3 4.0 %collective-permute-start.15 = (bf16[128,4608]{1,0:T(8,128)(2,1)S(1)}, bf16[128,4608]{1,0:T(8,128)(2,1)S(1)}, u32[]{:S(2)}, u32[]{:S(2)}) collective-permute-start(bf16[128,4608]{1,0:T(8,128)(2,1)S(1)} %get-tuple-element.34), channel_id=1, source_target_pairs={{0,1},{1,0},{2,3},{3,2},{4,5},{5,4},{6,7},{7,6},{8,9},{9,8},{10,11... | collective-permute-start | bytes 3538952 | tf_op jit(solution)/shard_map/ppermute | solution.py:49
  80.7 2.7 %collective-permute-start.19 = (bf16[128,3584]{1,0:T(8,128)(2,1)S(1)}, bf16[128,3584]{1,0:T(8,128)(2,1)S(1)}, u32[]{:S(2)}, u32[]{:S(2)}) collective-permute-start(bf16[128,3584]{1,0:T(8,128)(2,1)S(1)} %get-tuple-element.40), channel_id=1, source_target_pairs={{0,1},{1,0},{2,3},{3,2},{4,5},{5,4},{6,7},{7,6},{8,9},{9,8},{10,11... | collective-permute-start | bytes 2752520 | tf_op jit(solution)/shard_map/ppermute | solution.py:49
  81.6 8.0 %collective-permute-start.17 = (bf16[32,4608]{1,0:T(8,128)(2,1)S(1)}, bf16[32,4608]{1,0:T(8,128)(2,1)S(1)}, u32[]{:S(2)}, u32[]{:S(2)}) collective-permute-start(bf16[32,4608]{1,0:T(8,128)(2,1)S(1)} %get-tuple-element.38), channel_id=1, source_target_pairs={{6,0},{3,1},{0,2},{5,3},{2,4},{7,5},{4,6},{1,7},{14,8},{11,9},{8,1... | collective-permute-start | bytes 884744 | tf_op jit(solution)/shard_map/ppermute | solution.py:25
  83.6 10.3 %collective-permute-start.21 = (bf16[32,3584]{1,0:T(8,128)(2,1)S(1)}, bf16[32,3584]{1,0:T(8,128)(2,1)S(1)}, u32[]{:S(2)}, u32[]{:S(2)}) collective-permute-start(bf16[32,3584]{1,0:T(8,128)(2,1)S(1)} %get-tuple-element.44), channel_id=1, source_target_pairs={{6,0},{3,1},{0,2},{5,3},{2,4},{7,5},{4,6},{1,7},{14,8},{11,9},{8,1... | collective-permute-start | bytes 688136 | tf_op jit(solution)/shard_map/ppermute | solution.py:25
  83.8 19.4 %collective-permute-start.16 = (bf16[32,4608]{1,0:T(8,128)(2,1)S(1)}, bf16[32,4608]{1,0:T(8,128)(2,1)S(1)}, u32[]{:S(2)}, u32[]{:S(2)}) collective-permute-start(bf16[32,4608]{1,0:T(8,128)(2,1)S(1)} %get-tuple-element.36), channel_id=1, source_target_pairs={{2,0},{7,1},{4,2},{1,3},{6,4},{3,5},{0,6},{5,7},{10,8},{15,9},{12,... | collective-permute-start | bytes 884744 | tf_op jit(solution)/shard_map/ppermute | solution.py:25
  89.6 13.6 %collective-permute-start.18 = (bf16[32,4608]{1,0:T(8,128)(2,1)S(1)}, bf16[32,4608]{1,0:T(8,128)(2,1)S(1)}, u32[]{:S(2)}, u32[]{:S(2)}) collective-permute-start(bf16[32,4608]{1,0:T(8,128)(2,1)S(1)} %join.2), channel_id=1, source_target_pairs={{6,0},{3,1},{0,2},{5,3},{2,4},{7,5},{4,6},{1,7},{14,8},{11,9},{8,1... | collective-permute-start | bytes 884744 | tf_op jit(solution)/shard_map/ppermute | solution.py:25
  89.7 9.6 %collective-permute-start.20 = (bf16[32,3584]{1,0:T(8,128)(2,1)S(1)}, bf16[32,3584]{1,0:T(8,128)(2,1)S(1)}, u32[]{:S(2)}, u32[]{:S(2)}) collective-permute-start(bf16[32,3584]{1,0:T(8,128)(2,1)S(1)} %get-tuple-element.42), channel_id=1, source_target_pairs={{2,0},{7,1},{4,2},{1,3},{6,4},{3,5},{0,6},{5,7},{10,8},{15,9},{12,... | collective-permute-start | bytes 688136 | tf_op jit(solution)/shard_map/ppermute | solution.py:25
  93.9 9.3 %collective-permute-start.22 = (bf16[32,3584]{1,0:T(8,128)(2,1)S(1)}, bf16[32,3584]{1,0:T(8,128)(2,1)S(1)}, u32[]{:S(2)}, u32[]{:S(2)}) collective-permute-start(bf16[32,3584]{1,0:T(8,128)(2,1)S(1)} %join.3), channel_id=1, source_target_pairs={{6,0},{3,1},{0,2},{5,3},{2,4},{7,5},{4,6},{1,7},{14,8},{11,9},{8,1... | collective-permute-start | bytes 688136 | tf_op jit(solution)/shard_map/ppermute | solution.py:25

commit v4 on v3

--- a/solution.py
+++ b/solution.py
@@ -94,7 +94,7 @@
     )
 
 
-def project_kernel(half, place, *refs):
+def project_kernel(half, done, place, *refs):
     pieces, weight = refs[:8], refs[8]
     if half == 0:
         filters, short, bias = refs[9:12]
@@ -115,11 +115,11 @@
         z = lax.rem(place[0] + (far if n % 2 == 0 else -far) + 4, 4)
         core = place[1] if n % 2 == 0 else 1 - place[1]
         row = pl.ds(pl.multiple_of(z * 64 + core * 32, 32), 32)
-        depth = pl.ds((half * parts + t) * span, span)
+        depth = pl.ds((done + t) * span, span)
         return pltpu.make_async_copy(pieces[n].at[:, depth], rows.at[t, row, :], row_sems.at[n, t])
 
     def fetch(k):
-        depth = pl.ds((half * steps + k) * tile, tile)
+        depth = pl.ds(done * span + k * tile, tile)
         return pltpu.make_async_copy(
             weight.at[:, depth, :], held.at[k % slots], weight_sems.at[k % slots]
         )
@@ -208,7 +208,13 @@
 
 def out_kernel(count, blocks, place, gated, *refs):
     groups = refs[:count]
-    keep, send, left = refs[count:]
+    keep, send, left, held, sems = refs[count:]
+    copies = [
+        pltpu.make_async_copy(groups[group].at[n], held.at[at], sems.at[at])
+        for at, (_, group, n) in enumerate(blocks)
+    ]
+    for copy in copies:
+        copy.start()
     for m in range(2):
         core = place[1] if m == 0 else 1 - place[1]
         sign = 1 - 2 * core
@@ -218,8 +224,9 @@
             at = m * 128 + n * 32
             left[at : at + 32, :] = gated[pl.ds(row, 32), :]
     labels = [block[0] for block in blocks]
-    for at, ((near, far), group, n) in enumerate(blocks):
-        result = jnp.dot(left[...], groups[group][n], preferred_element_type=F32).astype(BF16)
+    for at, (near, far) in enumerate(labels):
+        copies[at].wait()
+        result = jnp.dot(left[...], held[at], preferred_element_type=F32).astype(BF16)
         to = labels.index((far, near))
         keep[:, at * 512 : (at + 1) * 512] = result[0:128]
         send[:, to * 512 : (to + 1) * 512] = result[128:256]
@@ -276,12 +283,12 @@
 
 
 def halves_kernel(ahead, behind, after, one, two, sems):
-    copies = [
-        pltpu.make_async_copy(ahead.at[pl.ds(0, 2)], one, sems.at[0]),
-        pltpu.make_async_copy(behind.at[pl.ds(2, 2)], two, sems.at[1]),
-    ]
-    for copy in copies:
-        copy.start()
+    copies = []
+    for n, (source, target) in enumerate(
+        ((ahead.at[0], one.at[0]), (ahead.at[1], one.at[1]), (behind.at[2], two.at[0]), (behind.at[3], two.at[1]))
+    ):
+        copies.append(pltpu.make_async_copy(source, target, sems.at[n]))
+        copies[-1].start()
     for copy in copies:
         copy.wait()
 
@@ -292,7 +299,7 @@
 def spread(block, after):
     blocks = [block] + [cross(block, NEAR, by) for by in (1, -1, 2)]
     own = stacked([in_hbm(block)] + [in_vmem(block) for block in blocks[1:]], after)
-    return [own] + [cross(own, FAR, by) for by in (1, -1)]
+    return [own] + [in_hbm(cross(own, FAR, by)) for by in (1, -1)]
 
 
 def shards(tokens, in_weight, short_filter, mr_filter, mr_bias, out_weight):
@@ -307,16 +314,19 @@
     weights = spread(out_weight, [pieces[2], pieces[6]])
 
     weight = in_hbm(jnp.transpose(in_weight, (1, 0, 2)))
-    parts, span, slots = 2, 2048, 5
-    scratch = [
-        pltpu.VMEM((parts, 256, span), BF16),
-        pltpu.VMEM((slots, 3, 512, 512), BF16),
-        pltpu.SemaphoreType.DMA((8, parts)),
-        pltpu.SemaphoreType.DMA((slots,)),
-    ]
+    span, slots, first = 1024, 5, 5
+
+    def room(parts):
+        return [
+            pltpu.VMEM((parts, 256, span), BF16),
+            pltpu.VMEM((slots, 3, 512, 512), BF16),
+            pltpu.SemaphoreType.DMA((8, parts)),
+            pltpu.SemaphoreType.DMA((slots,)),
+        ]
+
     cost = (256 * 8192 * 1536, 14 * MIB)
     total, bands, taps, direct = call(
-        functools.partial(project_kernel, 0),
+        functools.partial(project_kernel, 0, 0),
         (
             shape(256, 1536, dtype=F32),
             shape(4096, 256),
@@ -332,7 +342,7 @@
             in_hbm(short_filter),
             in_hbm(mr_bias.reshape(1, 512)),
         ],
-        scratch + [pltpu.VMEM((32, 128), F32), pltpu.SemaphoreType.DMA((3,))],
+        room(first) + [pltpu.VMEM((32, 128), F32), pltpu.SemaphoreType.DMA((3,))],
         cost,
         16,
         in_specs=[SM] + [ANY] * 12,
@@ -343,18 +353,18 @@
         (shape(2, 512, 512),) * 2,
         "halves",
         [*weights[1:], direct],
-        [pltpu.SemaphoreType.DMA((2,))],
+        [pltpu.SemaphoreType.DMA((4,))],
         (0, 4 * MIB),
-        in_specs=[VM, VM, ANY],
+        in_specs=[ANY] * 3,
         out_specs=(VM, VM),
     )
     weights += [cross(relays[0], FAR, 1), cross(relays[1], FAR, -1)]
     projected, edge = call(
-        functools.partial(project_kernel, 1),
+        functools.partial(project_kernel, 1, first),
         (shape(256, 1536), shape(176, 512)),
         "project",
         [place, *pieces, weight, total, taps, relays[0]],
-        scratch + [pltpu.VMEM((256, 1536), F32), pltpu.VMEM((136, 512), F32)],
+        room(8 - first) + [pltpu.VMEM((256, 1536), F32), pltpu.VMEM((136, 512), F32)],
         cost,
         18,
         in_specs=[SM] + [ANY] * 9 + [VM, VM, ANY],
@@ -393,9 +403,14 @@
             (shape(128, width),) * 2,
             "out",
             [place, gated, *groups],
-            [pltpu.VMEM((256, 512), BF16)],
+            [
+                pltpu.VMEM((256, 512), BF16),
+                pltpu.VMEM((len(blocks), 512, 512), BF16),
+                pltpu.SemaphoreType.DMA((len(blocks),)),
+            ],
             (2 * 256 * 512 * width, 512 * width * 2),
-            in_specs=[SM] + [VM] * (1 + len(groups)),
+            10,
+            in_specs=[SM, VM] + [ANY] * len(groups),
             out_specs=(VM, VM),
         )
         here, front, back, across = call(

time: 105 us -> 104 us (level)
  transfers between devices with their start and end apart: 23 -> 23, of which waited for: 14 -> 15; matrix products, arithmetic and copies ran while one was open for 0% -> 0% of each run, Pallas kernels for 20% -> 20%
where the time goes in v4:
time: 104 us; the launch traced here: 103 us
  waiting for transfers between devices  41.6 us (40%)
  starting transfers between devices  30.1 us (29%)
  Pallas kernels  29.6 us (28%)
  local copies, waits for them, and re-layouts  1.84 us (2%)
    pallas_call x12, Pallas kernels, call(): pl.pallas_call(body, out_shape=out, scratch_shapes=list(scratch), name=na...  29.6 us
    ppermute x9, waiting for transfers between devices, turn(): return lax.ppermute(shard, (axis, 'core'), pairs)  21 us
    ppermute x9, starting transfers between devices, turn(): return lax.ppermute(shard, (axis, 'core'), pairs)  13.6 us
    ppermute x7, starting transfers between devices, cross(): return lax.ppermute(shard, ('x', 'y', 'core'), pairs)  11.9 us
    ppermute x7, waiting for transfers between devices, cross(): return lax.ppermute(shard, ('x', 'y', 'core'), pairs)  10.2 us
    ppermute x1, waiting for transfers between devices, shards(): lax.ppermute(edge, context, [(i, i + 1) for i in range(count - 1)])  7.03 us
    ppermute x6, waiting for transfers between devices, swap(): return lax.ppermute(shard, 'core', [(0, 1), (1, 0)])  3.32 us
    ppermute x1, starting transfers between devices, shards(): lax.ppermute(edge, context, [(i, i + 1) for i in range(count - 1)])  2.52 us
  transfers between devices with their start and end apart: 23, of which 15 were waited for; matrix products, arithmetic and copies ran while one was open for 0% of the time, Pallas kernels for 20%

profile of v4, /device:TPU:2, one launch (start us, length us, event | category | flops | bytes accessed | tf_op | source)
XLA Modules:
  0.0 103.4 jit_solution(12223854641039818406)
XLA Ops:
  0.0 0.0 copy-start.2
  0.0 1.5 %collective-permute-start.8 = (bf16[512,512]{1,0:T(8,128)(2,1)}, bf16[512,512]{1,0:T(8,128)(2,1)S(1)}, u32[]{:S(2)}, u32[]{:S(2)}) collective-permute-start(bf16[512,512]{1,0:T(8,128)(2,1)} %refs_0_.4), channel_id=1, source_target_pairs={{96,0},{25,1},{104,8},{1,9},{112,16},{9,17},{120,24},{17,25},{0,32... | collective-permute-start | bytes 1572872 | tf_op jit(solution)/shard_map/ppermute | solution.py:45
  1.5 0.5 collective-permute-start.7
  2.0 2.1 %collective-permute-start.9 = (bf16[512,512]{1,0:T(8,128)(2,1)}, bf16[512,512]{1,0:T(8,128)(2,1)S(1)}, u32[]{:S(2)}, u32[]{:S(2)}) collective-permute-start(bf16[512,512]{1,0:T(8,128)(2,1)} %refs_0_.4), channel_id=1, source_target_pairs={{64,0},{17,1},{72,8},{25,9},{80,16},{1,17},{88,24},{9,25},{96,32},... | collective-permute-start | bytes 1572872 | tf_op jit(solution)/shard_map/ppermute | solution.py:45
  4.2 1.9 %collective-permute-start.5 = (bf16[32,8192]{1,0:T(8,128)(2,1)}, bf16[32,8192]{1,0:T(8,128)(2,1)S(1)}, u32[]{:S(2)}, u32[]{:S(2)}) collective-permute-start(bf16[32,8192]{1,0:T(8,128)(2,1)} %refs_0_.5), channel_id=1, source_target_pairs={{6,0},{3,1},{0,2},{5,3},{2,4},{7,5},{4,6},{1,7},{14,8},{11,9},{8,1... | collective-permute-start | bytes 1572872 | tf_op jit(solution)/shard_map/ppermute | solution.py:25
  6.1 2.1 %collective-permute-start.1 = (bf16[32,8192]{1,0:T(8,128)(2,1)}, bf16[32,8192]{1,0:T(8,128)(2,1)S(1)}, u32[]{:S(2)}, u32[]{:S(2)}) collective-permute-start(bf16[32,8192]{1,0:T(8,128)(2,1)} %refs_0_.5), channel_id=1, source_target_pairs={{2,0},{7,1},{4,2},{1,3},{6,4},{3,5},{0,6},{5,7},{10,8},{15,9},{12,... | collective-permute-start | bytes 1572872 | tf_op jit(solution)/shard_map/ppermute | solution.py:25
  8.2 1.2 %collective-permute-done.8.refs_2_ = bf16[512,512]{1,0:T(8,128)(2,1)S(1)} collective-permute-done((bf16[512,512]{1,0:T(8,128)(2,1)}, bf16[512,512]{1,0:T(8,128)(2,1)S(1)}, u32[]{:S(2)}, u32[]{:S(2)}) %collective-permute-start.8) | collective-permute-done | bytes 524320 | tf_op jit(solution)/shard_map/ppermute | solution.py:45
  9.4 1.5 %collective-permute-done.7.refs_1_ = bf16[512,512]{1,0:T(8,128)(2,1)S(1)} collective-permute-done((bf16[512,512]{1,0:T(8,128)(2,1)}, bf16[512,512]{1,0:T(8,128)(2,1)S(1)}, u32[]{:S(2)}, u32[]{:S(2)}) %collective-permute-start.7) | collective-permute-done | bytes 524320 | tf_op jit(solution)/shard_map/ppermute | solution.py:45
  10.9 6.3 %collective-permute-done.9.refs_3_ = bf16[512,512]{1,0:T(8,128)(2,1)S(1)} collective-permute-done((bf16[512,512]{1,0:T(8,128)(2,1)}, bf16[512,512]{1,0:T(8,128)(2,1)S(1)}, u32[]{:S(2)}, u32[]{:S(2)}) %collective-permute-start.9) | collective-permute-done | bytes 524320 | tf_op jit(solution)/shard_map/ppermute | solution.py:45
  17.1 1.9 %collective-permute-done.5.refs_6_.refs_5_ = bf16[32,8192]{1,0:T(8,128)(2,1)S(1)} collective-permute-done((bf16[32,8192]{1,0:T(8,128)(2,1)}, bf16[32,8192]{1,0:T(8,128)(2,1)S(1)}, u32[]{:S(2)}, u32[]{:S(2)}) %collective-permute-start.5) | collective-permute-done | bytes 524320 | tf_op jit(solution)/shard_map/ppermute | solution.py:25
  19.1 0.9 collective-permute-done.1.refs_2_.refs_4_
  19.9 1.1 %stack.21.refs_0_ = bf16[4,512,512]{2,1,0:T(8,128)(2,1)S(1)} custom-call(bf16[512,512]{1,0:T(8,128)(2,1)} %refs_0_.4, bf16[512,512]{1,0:T(8,128)(2,1)S(1)} %collective-permute-done.7.refs_1_, bf16[512,512]{1,0:T(8,128)(2,1)S(1)} %collective-permute-done.8.refs_2_, bf16[512,512]{1,0:T(8,128)(2,1)S(1)} %collective-permute-done.9.refs_3_, ...), custom_call_target="tpu_custom_call" | custom-call | bytes 4194304 | tf_op jit(solution)/shard_map/stack/pallas_call | solution.py:53
  21.0 1.7 %collective-permute-start.11 = (bf16[4,512,512]{2,1,0:T(8,128)(2,1)S(1)}, bf16[4,512,512]{2,1,0:T(8,128)(2,1)}, u32[]{:S(2)}, u32[]{:S(2)}) collective-permute-start(bf16[4,512,512]{2,1,0:T(8,128)(2,1)S(1)} %stack.21.refs_0_), channel_id=1, source_target_pairs={{24,0},{97,1},{0,8},{105,9},{8,16},{113,17},{16,24},{121,25},{56,3... | collective-permute-start | bytes 6291464 | tf_op jit(solution)/shard_map/ppermute | solution.py:45
  22.7 2.6 %collective-permute-start.10 = (bf16[4,512,512]{2,1,0:T(8,128)(2,1)S(1)}, bf16[4,512,512]{2,1,0:T(8,128)(2,1)}, u32[]{:S(2)}, u32[]{:S(2)}) collective-permute-start(bf16[4,512,512]{2,1,0:T(8,128)(2,1)S(1)} %stack.21.refs_0_), channel_id=1, source_target_pairs={{8,0},{33,1},{16,8},{41,9},{24,16},{49,17},{0,24},{57,25},{40,32},... | collective-permute-start | bytes 6291464 | tf_op jit(solution)/shard_map/ppermute | solution.py:45
  25.3 0.0 copy-done.2
  25.3 0.0 collective-permute-start
  25.4 2.6 %collective-permute-start.3 = (bf16[32,8192]{1,0:T(8,128)(2,1)S(1)}, bf16[32,8192]{1,0:T(8,128)(2,1)}, u32[]{:S(2)}, u32[]{:S(2)}) collective-permute-start(bf16[32,8192]{1,0:T(8,128)(2,1)S(1)} %collective-permute-done.1.refs_2_.refs_4_), channel_id=1, source_target_pairs={{2,0},{7,1},{4,2},{1,3},{6,4},{3,5},{0,6},{5,7},{10,8},{15,9},{12,... | collective-permute-start | bytes 1572872 | tf_op jit(solution)/shard_map/ppermute | solution.py:25
  27.9 0.0 collective-permute-start.6
  27.9 0.0 collective-permute-done.refs_1_
  27.9 0.0 copy-start
  27.9 0.8 copy-done
  28.7 0.5 collective-permute-start.2
  29.2 5.4 %collective-permute-done.3.refs_4_ = bf16[32,8192]{1,0:T(8,128)(2,1)} collective-permute-done((bf16[32,8192]{1,0:T(8,128)(2,1)S(1)}, bf16[32,8192]{1,0:T(8,128)(2,1)}, u32[]{:S(2)}, u32[]{:S(2)}) %collective-permute-start.3) | collective-permute-done | bytes 524320 | tf_op jit(solution)/shard_map/ppermute | solution.py:25
  34.6 0.9 collective-permute-start.4
  35.5 0.1 pad_add_fusion.place
  35.6 0.0 collective-permute-done.6.refs_7_
  35.6 0.0 collective-permute-done.2.refs_3_
  35.6 1.8 %collective-permute-done.4.refs_5_ = bf16[32,8192]{1,0:T(8,128)(2,1)} collective-permute-done((bf16[32,8192]{1,0:T(8,128)(2,1)}, bf16[32,8192]{1,0:T(8,128)(2,1)}, u32[]{:S(2)}, u32[]{:S(2)}) %collective-permute-start.4) | collective-permute-done | bytes 524320 | tf_op jit(solution)/shard_map/ppermute | solution.py:49
  37.4 1.0 %copy-done.1 = bf16[32,8192]{1,0:T(8,128)(2,1)S(1)} copy-done((bf16[32,8192]{1,0:T(8,128)(2,1)S(1)}, bf16[32,8192]{1,0:T(8,128)(2,1)}, u32[]{:S(2)}) %copy-start.1) | copy-done | bytes 524312
  38.4 10.0 %project.2 = (f32[256,1536]{1,0:T(8,128)S(1)}, bf16[4096,256]{1,0:T(8,128)(2,1)S(1)}, f32[3,3,512]{2,1,0:T(4,128)S(1)}, f32[1,512]{1,0:T(1,128)S(1)}) custom-call(s32[4]{0:T(128)S(1)} %pad_add_fusion.place, bf16[32,8192]{1,0:T(8,128)(2,1)} %refs_0_.5, bf16[32,8192]{1,0:T(8,128)(2,1)S(1)} %copy-done.1, ...), custom_call_target="tpu_custom_call" | custom-call | flops 3221225472 | bytes 14680064 | tf_op jit(solution)/shard_map/project/pallas_call | solution.py:53
  48.4 1.0 collective-permute-done.11.behind.refs_2_
  49.4 0.0 collective-permute-done.10.ahead.refs_1_
  49.4 1.5 %halves.1 = (bf16[2,512,512]{2,1,0:T(8,128)(2,1)S(1)}, bf16[2,512,512]{2,1,0:T(8,128)(2,1)S(1)}) custom-call(bf16[4,512,512]{2,1,0:T(8,128)(2,1)} %collective-permute-done.10.ahead.refs_1_, bf16[4,512,512]{2,1,0:T(8,128)(2,1)} %collective-permute-done.11.behind.refs_2_, f32[1,512]{1,0:T(1,128)S(1)} %get-tuple-element.27.after.bias), custom_call_target="tpu_custom_call" | custom-call | bytes 4194304 | tf_op jit(solution)/shard_map/halves/pallas_call | solution.py:53
  50.9 1.9 %collective-permute-start.14 = (bf16[2,512,512]{2,1,0:T(8,128)(2,1)S(1)}, bf16[2,512,512]{2,1,0:T(8,128)(2,1)S(1)}, u32[]{:S(2)}, u32[]{:S(2)}) collective-permute-start(bf16[2,512,512]{2,1,0:T(8,128)(2,1)S(1)} %get-tuple-element.32), channel_id=1, source_target_pairs={{24,0},{97,1},{0,8},{105,9},{8,16},{113,17},{16,24},{121,25},{56,3... | collective-permute-start | bytes 3145736 | tf_op jit(solution)/shard_map/ppermute | solution.py:45
  52.8 1.6 %collective-permute-start.13 = (bf16[2,512,512]{2,1,0:T(8,128)(2,1)S(1)}, bf16[2,512,512]{2,1,0:T(8,128)(2,1)S(1)}, u32[]{:S(2)}, u32[]{:S(2)}) collective-permute-start(bf16[2,512,512]{2,1,0:T(8,128)(2,1)S(1)} %get-tuple-element.28.refs_11_), channel_id=1, source_target_pairs={{8,0},{33,1},{16,8},{41,9},{24,16},{49,17},{0,24},{57,25},{40,32},... | collective-permute-start | bytes 3145736 | tf_op jit(solution)/shard_map/ppermute | solution.py:45
  54.4 6.7 %project.3 = (bf16[256,1536]{1,0:T(8,128)(2,1)S(1)}, bf16[176,512]{1,0:T(8,128)(2,1)S(1)}) custom-call(s32[4]{0:T(128)S(1)} %pad_add_fusion.place, bf16[32,8192]{1,0:T(8,128)(2,1)} %refs_0_.5, bf16[32,8192]{1,0:T(8,128)(2,1)S(1)} %copy-done.1, bf16[32,8192]{1,0:T(8,128)(2,1)S(1)} %collective-permute-done.1.refs_2_.refs_4_, ...), custom_call_target="tpu_custom_call" | custom-call | flops 3221225472 | bytes 14680064 | tf_op jit(solution)/shard_map/project/pallas_call | solution.py:53
  61.1 2.5 %collective-permute-start.12 = (bf16[176,512]{1,0:T(8,128)(2,1)S(1)}, bf16[176,512]{1,0:T(8,128)(2,1)S(1)}, u32[]{:S(2)}, u32[]{:S(2)}) collective-permute-start(bf16[176,512]{1,0:T(8,128)(2,1)S(1)} %get-tuple-element.30), channel_id=1, source_target_pairs={{0,8},{8,16},{16,24},{24,32},{32,40},{40,48},{48,56},{56,64},{64,7... | collective-permute-start | bytes 540680 | tf_op jit(solution)/shard_map/ppermute | solution.py:376
  63.6 7.0 %collective-permute-done.12.edge = bf16[176,512]{1,0:T(8,128)(2,1)S(1)} collective-permute-done((bf16[176,512]{1,0:T(8,128)(2,1)S(1)}, bf16[176,512]{1,0:T(8,128)(2,1)S(1)}, u32[]{:S(2)}, u32[]{:S(2)}) %collective-permute-start.12) | collective-permute-done | bytes 180256 | tf_op jit(solution)/shard_map/ppermute | solution.py:376
  70.7 0.3 collective-permute-done.14.two.refs_4_
  71.0 0.0 collective-permute-done.13.one.refs_3_
  71.0 1.1 %mix.1.gated = bf16[256,512]{1,0:T(8,128)(2,1)S(1)} custom-call(bf16[256,1536]{1,0:T(8,128)(2,1)S(1)} %get-tuple-element.29.projected, bf16[176,512]{1,0:T(8,128)(2,1)S(1)} %collective-permute-done.12.edge, f32[3,3,512]{2,1,0:T(4,128)S(1)} %get-tuple-element.26.refs_10_.taps, f32[1,512]{1,0:T(1,128)S(1)} %get-tuple-element.27.after.bias, ...), custom_call_target="tpu_custom_call" | custom-call | flops 536870912 | bytes 4194304 | tf_op jit(solution)/shard_map/mix/pallas_call | solution.py:53
  72.1 3.6 %out.2 = (bf16[128,4608]{1,0:T(8,128)(2,1)S(1)}, bf16[128,4608]{1,0:T(8,128)(2,1)S(1)}) custom-call(s32[4]{0:T(128)S(1)} %pad_add_fusion.place, bf16[256,512]{1,0:T(8,128)(2,1)S(1)} %mix.1.gated, bf16[4,512,512]{2,1,0:T(8,128)(2,1)S(1)} %stack.21.refs_0_, bf16[4,512,512]{2,1,0:T(8,128)(2,1)} %collective-permute-done.10.ahead.refs_1_, ...), custom_call_target="tpu_custom_call" | custom-call | flops 1207959552 | bytes 4718592 | tf_op jit(solution)/shard_map/out/pallas_call | solution.py:53
  75.7 0.1 collective-permute-start.15
  75.8 3.5 %out.3 = (bf16[128,3584]{1,0:T(8,128)(2,1)S(1)}, bf16[128,3584]{1,0:T(8,128)(2,1)S(1)}) custom-call(s32[4]{0:T(128)S(1)} %pad_add_fusion.place, bf16[256,512]{1,0:T(8,128)(2,1)S(1)} %mix.1.gated, bf16[4,512,512]{2,1,0:T(8,128)(2,1)S(1)} %stack.21.refs_0_, bf16[4,512,512]{2,1,0:T(8,128)(2,1)} %collective-permute-done.10.ahead.refs_1_, ...), custom_call_target="tpu_custom_call" | custom-call | flops 939524096 | bytes 3670016 | tf_op jit(solution)/shard_map/out/pallas_call | solution.py:53
  79.3 0.6 collective-permute-start.19
  79.9 0.0 collective-permute-done.15.got
  79.9 0.3 pair.2
  80.1 0.3 collective-permute-start.17
  80.4 1.5 %collective-permute-done.19.got = bf16[128,3584]{1,0:T(8,128)(2,1)S(1)} collective-permute-done((bf16[128,3584]{1,0:T(8,128)(2,1)S(1)}, bf16[128,3584]{1,0:T(8,128)(2,1)S(1)}, u32[]{:S(2)}, u32[]{:S(2)}) %collective-permute-start.19) | collective-permute-done | bytes 917536 | tf_op jit(solution)/shard_map/ppermute | solution.py:49
  82.0 0.2 pair.3
  82.2 0.3 collective-permute-start.21
  82.5 3.0 %collective-permute-start.16 = (bf16[32,4608]{1,0:T(8,128)(2,1)S(1)}, bf16[32,4608]{1,0:T(8,128)(2,1)S(1)}, u32[]{:S(2)}, u32[]{:S(2)}) collective-permute-start(bf16[32,4608]{1,0:T(8,128)(2,1)S(1)} %get-tuple-element.36), channel_id=1, source_target_pairs={{2,0},{7,1},{4,2},{1,3},{6,4},{3,5},{0,6},{5,7},{10,8},{15,9},{12,... | collective-permute-start | bytes 884744 | tf_op jit(solution)/shard_map/ppermute | solution.py:25
  85.5 2.7 %collective-permute-done.17.b = bf16[32,4608]{1,0:T(8,128)(2,1)S(1)} collective-permute-done((bf16[32,4608]{1,0:T(8,128)(2,1)S(1)}, bf16[32,4608]{1,0:T(8,128)(2,1)S(1)}, u32[]{:S(2)}, u32[]{:S(2)}) %collective-permute-start.17) | collective-permute-done | bytes 294944 | tf_op jit(solution)/shard_map/ppermute | solution.py:25
  88.1 0.1 join.2
  88.2 0.1 collective-permute-start.18
  88.3 3.2 %collective-permute-start.20 = (bf16[32,3584]{1,0:T(8,128)(2,1)S(1)}, bf16[32,3584]{1,0:T(8,128)(2,1)S(1)}, u32[]{:S(2)}, u32[]{:S(2)}) collective-permute-start(bf16[32,3584]{1,0:T(8,128)(2,1)S(1)} %get-tuple-element.42), channel_id=1, source_target_pairs={{2,0},{7,1},{4,2},{1,3},{6,4},{3,5},{0,6},{5,7},{10,8},{15,9},{12,... | collective-permute-start | bytes 688136 | tf_op jit(solution)/shard_map/ppermute | solution.py:25
  91.5 0.9 collective-permute-done.21.b
  92.4 0.1 join.3
  92.5 0.1 collective-permute-start.22
  92.6 5.3 %collective-permute-done.20.refs_4_ = bf16[32,3584]{1,0:T(8,128)(2,1)S(1)} collective-permute-done((bf16[32,3584]{1,0:T(8,128)(2,1)S(1)}, bf16[32,3584]{1,0:T(8,128)(2,1)S(1)}, u32[]{:S(2)}, u32[]{:S(2)}) %collective-permute-start.20) | collective-permute-done | bytes 229408 | tf_op jit(solution)/shard_map/ppermute | solution.py:25
  97.9 4.0 %collective-permute-done.22.refs_5_ = bf16[32,3584]{1,0:T(8,128)(2,1)S(1)} collective-permute-done((bf16[32,3584]{1,0:T(8,128)(2,1)S(1)}, bf16[32,3584]{1,0:T(8,128)(2,1)S(1)}, u32[]{:S(2)}, u32[]{:S(2)}) %collective-permute-start.22) | collective-permute-done | bytes 229408 | tf_op jit(solution)/shard_map/ppermute | solution.py:25
  101.8 0.0 collective-permute-done.16.refs_1_
  101.8 0.0 collective-permute-done.18.refs_2_
  101.8 1.5 %finish.1 = bf16[32,8192]{1,0:T(8,128)(2,1)} custom-call(s32[4]{0:T(128)S(1)} %pad_add_fusion.place, bf16[32,4608]{1,0:T(8,128)(2,1)S(1)} %get-tuple-element.35.refs_0_, bf16[32,4608]{1,0:T(8,128)(2,1)S(1)} %collective-permute-done.16.refs_1_, bf16[32,4608]{1,0:T(8,128)(2,1)S(1)} %collective-permute-done.18.refs_2_, ...), custom_call_target="tpu_custom_call" | custom-call | bytes 3145728 | tf_op jit(solution)/shard_map/finish/pallas_call | solution.py:53
  (1 shorter events, 0.0 us)
Async XLA Ops:
  0.0 25.3 %copy-start.2 = (bf16[32,8192]{1,0:T(8,128)(2,1)S(1)}, bf16[32,8192]{1,0:T(8,128)(2,1)}, u32[]{:S(2)}) copy-start(bf16[32,8192]{1,0:T(8,128)(2,1)} %refs_0_.5) | copy-start | bytes 1572868
  0.0 9.4 %collective-permute-start.8 = (bf16[512,512]{1,0:T(8,128)(2,1)}, bf16[512,512]{1,0:T(8,128)(2,1)S(1)}, u32[]{:S(2)}, u32[]{:S(2)}) collective-permute-start(bf16[512,512]{1,0:T(8,128)(2,1)} %refs_0_.4), channel_id=1, source_target_pairs={{96,0},{25,1},{104,8},{1,9},{112,16},{9,17},{120,24},{17,25},{0,32... | collective-permute-start | bytes 1572872 | tf_op jit(solution)/shard_map/ppermute | solution.py:45
  1.5 9.4 %collective-permute-start.7 = (bf16[512,512]{1,0:T(8,128)(2,1)}, bf16[512,512]{1,0:T(8,128)(2,1)S(1)}, u32[]{:S(2)}, u32[]{:S(2)}) collective-permute-start(bf16[512,512]{1,0:T(8,128)(2,1)} %refs_0_.4), channel_id=1, source_target_pairs={{32,0},{9,1},{40,8},{17,9},{48,16},{25,17},{56,24},{1,25},{64,32},... | collective-permute-start | bytes 1572872 | tf_op jit(solution)/shard_map/ppermute | solution.py:45
  2.0 15.1 %collective-permute-start.9 = (bf16[512,512]{1,0:T(8,128)(2,1)}, bf16[512,512]{1,0:T(8,128)(2,1)S(1)}, u32[]{:S(2)}, u32[]{:S(2)}) collective-permute-start(bf16[512,512]{1,0:T(8,128)(2,1)} %refs_0_.4), channel_id=1, source_target_pairs={{64,0},{17,1},{72,8},{25,9},{80,16},{1,17},{88,24},{9,25},{96,32},... | collective-permute-start | bytes 1572872 | tf_op jit(solution)/shard_map/ppermute | solution.py:45
  4.2 14.9 %collective-permute-start.5 = (bf16[32,8192]{1,0:T(8,128)(2,1)}, bf16[32,8192]{1,0:T(8,128)(2,1)S(1)}, u32[]{:S(2)}, u32[]{:S(2)}) collective-permute-start(bf16[32,8192]{1,0:T(8,128)(2,1)} %refs_0_.5), channel_id=1, source_target_pairs={{6,0},{3,1},{0,2},{5,3},{2,4},{7,5},{4,6},{1,7},{14,8},{11,9},{8,1... | collective-permute-start | bytes 1572872 | tf_op jit(solution)/shard_map/ppermute | solution.py:25
  6.1 13.8 %collective-permute-start.1 = (bf16[32,8192]{1,0:T(8,128)(2,1)}, bf16[32,8192]{1,0:T(8,128)(2,1)S(1)}, u32[]{:S(2)}, u32[]{:S(2)}) collective-permute-start(bf16[32,8192]{1,0:T(8,128)(2,1)} %refs_0_.5), channel_id=1, source_target_pairs={{2,0},{7,1},{4,2},{1,3},{6,4},{3,5},{0,6},{5,7},{10,8},{15,9},{12,... | collective-permute-start | bytes 1572872 | tf_op jit(solution)/shard_map/ppermute | solution.py:25
  21.0 28.4 %collective-permute-start.11 = (bf16[4,512,512]{2,1,0:T(8,128)(2,1)S(1)}, bf16[4,512,512]{2,1,0:T(8,128)(2,1)}, u32[]{:S(2)}, u32[]{:S(2)}) collective-permute-start(bf16[4,512,512]{2,1,0:T(8,128)(2,1)S(1)} %stack.21.refs_0_), channel_id=1, source_target_pairs={{24,0},{97,1},{0,8},{105,9},{8,16},{113,17},{16,24},{121,25},{56,3... | collective-permute-start | bytes 6291464 | tf_op jit(solution)/shard_map/ppermute | solution.py:45
  22.7 26.6 %collective-permute-start.10 = (bf16[4,512,512]{2,1,0:T(8,128)(2,1)S(1)}, bf16[4,512,512]{2,1,0:T(8,128)(2,1)}, u32[]{:S(2)}, u32[]{:S(2)}) collective-permute-start(bf16[4,512,512]{2,1,0:T(8,128)(2,1)S(1)} %stack.21.refs_0_), channel_id=1, source_target_pairs={{8,0},{33,1},{16,8},{41,9},{24,16},{49,17},{0,24},{57,25},{40,32},... | collective-permute-start | bytes 6291464 | tf_op jit(solution)/shard_map/ppermute | solution.py:45
  25.3 2.6 %collective-permute-start = (bf16[32,8192]{1,0:T(8,128)(2,1)S(1)}, bf16[32,8192]{1,0:T(8,128)(2,1)S(1)}, u32[]{:S(2)}, u32[]{:S(2)}) collective-permute-start(bf16[32,8192]{1,0:T(8,128)(2,1)S(1)} %copy-done.2), channel_id=1, source_target_pairs={{0,1},{1,0},{2,3},{3,2},{4,5},{5,4},{6,7},{7,6},{8,9},{9,8},{10,11... | collective-permute-start | bytes 1572872 | tf_op jit(solution)/shard_map/ppermute | solution.py:49
  25.4 9.3 %collective-permute-start.3 = (bf16[32,8192]{1,0:T(8,128)(2,1)S(1)}, bf16[32,8192]{1,0:T(8,128)(2,1)}, u32[]{:S(2)}, u32[]{:S(2)}) collective-permute-start(bf16[32,8192]{1,0:T(8,128)(2,1)S(1)} %collective-permute-done.1.refs_2_.refs_4_), channel_id=1, source_target_pairs={{2,0},{7,1},{4,2},{1,3},{6,4},{3,5},{0,6},{5,7},{10,8},{15,9},{12,... | collective-permute-start | bytes 1572872 | tf_op jit(solution)/shard_map/ppermute | solution.py:25
  27.9 7.7 %collective-permute-start.6 = (bf16[32,8192]{1,0:T(8,128)(2,1)S(1)}, bf16[32,8192]{1,0:T(8,128)(2,1)}, u32[]{:S(2)}, u32[]{:S(2)}) collective-permute-start(bf16[32,8192]{1,0:T(8,128)(2,1)S(1)} %collective-permute-done.5.refs_6_.refs_5_), channel_id=1, source_target_pairs={{0,1},{1,0},{2,3},{3,2},{4,5},{5,4},{6,7},{7,6},{8,9},{9,8},{10,11... | collective-permute-start | bytes 1572872 | tf_op jit(solution)/shard_map/ppermute | solution.py:49
  27.9 0.8 copy-start
  28.7 6.9 %collective-permute-start.2 = (bf16[32,8192]{1,0:T(8,128)(2,1)S(1)}, bf16[32,8192]{1,0:T(8,128)(2,1)}, u32[]{:S(2)}, u32[]{:S(2)}) collective-permute-start(bf16[32,8192]{1,0:T(8,128)(2,1)S(1)} %collective-permute-done.1.refs_2_.refs_4_), channel_id=1, source_target_pairs={{0,1},{1,0},{2,3},{3,2},{4,5},{5,4},{6,7},{7,6},{8,9},{9,8},{10,11... | collective-permute-start | bytes 1572872 | tf_op jit(solution)/shard_map/ppermute | solution.py:49
  34.6 2.7 %collective-permute-start.4 = (bf16[32,8192]{1,0:T(8,128)(2,1)}, bf16[32,8192]{1,0:T(8,128)(2,1)}, u32[]{:S(2)}, u32[]{:S(2)}) collective-permute-start(bf16[32,8192]{1,0:T(8,128)(2,1)} %collective-permute-done.3.refs_4_), channel_id=1, source_target_pairs={{0,1},{1,0},{2,3},{3,2},{4,5},{5,4},{6,7},{7,6},{8,9},{9,8},{10,11... | collective-permute-start | bytes 1572872 | tf_op jit(solution)/shard_map/ppermute | solution.py:49
  37.4 1.0 %copy-start.1 = (bf16[32,8192]{1,0:T(8,128)(2,1)S(1)}, bf16[32,8192]{1,0:T(8,128)(2,1)}, u32[]{:S(2)}) copy-start(bf16[32,8192]{1,0:T(8,128)(2,1)} %copy-done) | copy-start | bytes 1572868
  50.9 20.0 %collective-permute-start.14 = (bf16[2,512,512]{2,1,0:T(8,128)(2,1)S(1)}, bf16[2,512,512]{2,1,0:T(8,128)(2,1)S(1)}, u32[]{:S(2)}, u32[]{:S(2)}) collective-permute-start(bf16[2,512,512]{2,1,0:T(8,128)(2,1)S(1)} %get-tuple-element.32), channel_id=1, source_target_pairs={{24,0},{97,1},{0,8},{105,9},{8,16},{113,17},{16,24},{121,25},{56,3... | collective-permute-start | bytes 3145736 | tf_op jit(solution)/shard_map/ppermute | solution.py:45
  52.8 18.2 %collective-permute-start.13 = (bf16[2,512,512]{2,1,0:T(8,128)(2,1)S(1)}, bf16[2,512,512]{2,1,0:T(8,128)(2,1)S(1)}, u32[]{:S(2)}, u32[]{:S(2)}) collective-permute-start(bf16[2,512,512]{2,1,0:T(8,128)(2,1)S(1)} %get-tuple-element.28.refs_11_), channel_id=1, source_target_pairs={{8,0},{33,1},{16,8},{41,9},{24,16},{49,17},{0,24},{57,25},{40,32},... | collective-permute-start | bytes 3145736 | tf_op jit(solution)/shard_map/ppermute | solution.py:45
  61.1 9.6 %collective-permute-start.12 = (bf16[176,512]{1,0:T(8,128)(2,1)S(1)}, bf16[176,512]{1,0:T(8,128)(2,1)S(1)}, u32[]{:S(2)}, u32[]{:S(2)}) collective-permute-start(bf16[176,512]{1,0:T(8,128)(2,1)S(1)} %get-tuple-element.30), channel_id=1, source_target_pairs={{0,8},{8,16},{16,24},{24,32},{32,40},{40,48},{48,56},{56,64},{64,7... | collective-permute-start | bytes 540680 | tf_op jit(solution)/shard_map/ppermute | solution.py:376
  75.7 4.2 %collective-permute-start.15 = (bf16[128,4608]{1,0:T(8,128)(2,1)S(1)}, bf16[128,4608]{1,0:T(8,128)(2,1)S(1)}, u32[]{:S(2)}, u32[]{:S(2)}) collective-permute-start(bf16[128,4608]{1,0:T(8,128)(2,1)S(1)} %get-tuple-element.34), channel_id=1, source_target_pairs={{0,1},{1,0},{2,3},{3,2},{4,5},{5,4},{6,7},{7,6},{8,9},{9,8},{10,11... | collective-permute-start | bytes 3538952 | tf_op jit(solution)/shard_map/ppermute | solution.py:49
  79.3 2.7 %collective-permute-start.19 = (bf16[128,3584]{1,0:T(8,128)(2,1)S(1)}, bf16[128,3584]{1,0:T(8,128)(2,1)S(1)}, u32[]{:S(2)}, u32[]{:S(2)}) collective-permute-start(bf16[128,3584]{1,0:T(8,128)(2,1)S(1)} %get-tuple-element.40), channel_id=1, source_target_pairs={{0,1},{1,0},{2,3},{3,2},{4,5},{5,4},{6,7},{7,6},{8,9},{9,8},{10,11... | collective-permute-start | bytes 2752520 | tf_op jit(solution)/shard_map/ppermute | solution.py:49
  80.1 8.0 %collective-permute-start.17 = (bf16[32,4608]{1,0:T(8,128)(2,1)S(1)}, bf16[32,4608]{1,0:T(8,128)(2,1)S(1)}, u32[]{:S(2)}, u32[]{:S(2)}) collective-permute-start(bf16[32,4608]{1,0:T(8,128)(2,1)S(1)} %get-tuple-element.38), channel_id=1, source_target_pairs={{6,0},{3,1},{0,2},{5,3},{2,4},{7,5},{4,6},{1,7},{14,8},{11,9},{8,1... | collective-permute-start | bytes 884744 | tf_op jit(solution)/shard_map/ppermute | solution.py:25
  82.2 10.3 %collective-permute-start.21 = (bf16[32,3584]{1,0:T(8,128)(2,1)S(1)}, bf16[32,3584]{1,0:T(8,128)(2,1)S(1)}, u32[]{:S(2)}, u32[]{:S(2)}) collective-permute-start(bf16[32,3584]{1,0:T(8,128)(2,1)S(1)} %get-tuple-element.44), channel_id=1, source_target_pairs={{6,0},{3,1},{0,2},{5,3},{2,4},{7,5},{4,6},{1,7},{14,8},{11,9},{8,1... | collective-permute-start | bytes 688136 | tf_op jit(solution)/shard_map/ppermute | solution.py:25
  82.5 19.4 %collective-permute-start.16 = (bf16[32,4608]{1,0:T(8,128)(2,1)S(1)}, bf16[32,4608]{1,0:T(8,128)(2,1)S(1)}, u32[]{:S(2)}, u32[]{:S(2)}) collective-permute-start(bf16[32,4608]{1,0:T(8,128)(2,1)S(1)} %get-tuple-element.36), channel_id=1, source_target_pairs={{2,0},{7,1},{4,2},{1,3},{6,4},{3,5},{0,6},{5,7},{10,8},{15,9},{12,... | collective-permute-start | bytes 884744 | tf_op jit(solution)/shard_map/ppermute | solution.py:25
  88.2 13.6 %collective-permute-start.18 = (bf16[32,4608]{1,0:T(8,128)(2,1)S(1)}, bf16[32,4608]{1,0:T(8,128)(2,1)S(1)}, u32[]{:S(2)}, u32[]{:S(2)}) collective-permute-start(bf16[32,4608]{1,0:T(8,128)(2,1)S(1)} %join.2), channel_id=1, source_target_pairs={{6,0},{3,1},{0,2},{5,3},{2,4},{7,5},{4,6},{1,7},{14,8},{11,9},{8,1... | collective-permute-start | bytes 884744 | tf_op jit(solution)/shard_map/ppermute | solution.py:25
  88.3 9.6 %collective-permute-start.20 = (bf16[32,3584]{1,0:T(8,128)(2,1)S(1)}, bf16[32,3584]{1,0:T(8,128)(2,1)S(1)}, u32[]{:S(2)}, u32[]{:S(2)}) collective-permute-start(bf16[32,3584]{1,0:T(8,128)(2,1)S(1)} %get-tuple-element.42), channel_id=1, source_target_pairs={{2,0},{7,1},{4,2},{1,3},{6,4},{3,5},{0,6},{5,7},{10,8},{15,9},{12,... | collective-permute-start | bytes 688136 | tf_op jit(solution)/shard_map/ppermute | solution.py:25
  92.5 9.3 %collective-permute-start.22 = (bf16[32,3584]{1,0:T(8,128)(2,1)S(1)}, bf16[32,3584]{1,0:T(8,128)(2,1)S(1)}, u32[]{:S(2)}, u32[]{:S(2)}) collective-permute-start(bf16[32,3584]{1,0:T(8,128)(2,1)S(1)} %join.3), channel_id=1, source_target_pairs={{6,0},{3,1},{0,2},{5,3},{2,4},{7,5},{4,6},{1,7},{14,8},{11,9},{8,1... | collective-permute-start | bytes 688136 | tf_op jit(solution)/shard_map/ppermute | solution.py:25

commit v5 on v4

--- a/solution.py
+++ b/solution.py
@@ -126,7 +126,7 @@
 
     for n in range(8):
         bring(n, 0).start()
-    for k in range(slots):
+    for k in range(min(slots, steps)):
         fetch(k).start()
     if half == 0:
         little = [
@@ -314,7 +314,7 @@
     weights = spread(out_weight, [pieces[2], pieces[6]])
 
     weight = in_hbm(jnp.transpose(in_weight, (1, 0, 2)))
-    span, slots, first = 1024, 5, 5
+    span, slots, first = 1024, 5, 6
 
     def room(parts):
         return [

time: 104 us -> 104 us (level)
    ppermute x1, waiting for transfers between devices: 7.03 us -> 8.42 us  [shards(): lax.ppermute(edge, context, [(i, i + 1) for i in range(count - 1)])]
  transfers between devices with their start and end apart: 23 -> 23, of which waited for: 15 -> 13; matrix products, arithmetic and copies ran while one was open for 0% -> 0% of each run, Pallas kernels for 20% -> 20%
where the time goes in v5:
time: 104 us; the launch traced here: 103 us
  waiting for transfers between devices  41.6 us (40%)
  starting transfers between devices  30.6 us (29%)
  Pallas kernels  29.2 us (28%)
  local copies, waits for them, and re-layouts  1.84 us (2%)
    pallas_call x12, Pallas kernels, call(): pl.pallas_call(body, out_shape=out, scratch_shapes=list(scratch), name=na...  29.2 us
    ppermute x9, waiting for transfers between devices, turn(): return lax.ppermute(shard, (axis, 'core'), pairs)  20.5 us
    ppermute x9, starting transfers between devices, turn(): return lax.ppermute(shard, (axis, 'core'), pairs)  14.1 us
    ppermute x7, starting transfers between devices, cross(): return lax.ppermute(shard, ('x', 'y', 'core'), pairs)  11.9 us
    ppermute x7, waiting for transfers between devices, cross(): return lax.ppermute(shard, ('x', 'y', 'core'), pairs)  9.32 us
    ppermute x1, waiting for transfers between devices, shards(): lax.ppermute(edge, context, [(i, i + 1) for i in range(count - 1)])  8.42 us
    ppermute x6, waiting for transfers between devices, swap(): return lax.ppermute(shard, 'core', [(0, 1), (1, 0)])  3.32 us
    ppermute x1, starting transfers between devices, shards(): lax.ppermute(edge, context, [(i, i + 1) for i in range(count - 1)])  2.51 us
  transfers between devices with their start and end apart: 23, of which 13 were waited for; matrix products, arithmetic and copies ran while one was open for 0% of the time, Pallas kernels for 20%

profile of v5, /device:TPU:2, one launch (start us, length us, event | category | flops | bytes accessed | tf_op | source)
XLA Modules:
  0.0 103.4 jit_solution(13319565596184352198)
XLA Ops:
  0.0 0.0 copy-start.2
  0.0 1.5 %collective-permute-start.8 = (bf16[512,512]{1,0:T(8,128)(2,1)}, bf16[512,512]{1,0:T(8,128)(2,1)S(1)}, u32[]{:S(2)}, u32[]{:S(2)}) collective-permute-start(bf16[512,512]{1,0:T(8,128)(2,1)} %refs_0_.4), channel_id=1, source_target_pairs={{96,0},{25,1},{104,8},{1,9},{112,16},{9,17},{120,24},{17,25},{0,32... | collective-permute-start | bytes 1572872 | tf_op jit(solution)/shard_map/ppermute | solution.py:45
  1.5 0.5 collective-permute-start.7
  2.0 2.1 %collective-permute-start.9 = (bf16[512,512]{1,0:T(8,128)(2,1)}, bf16[512,512]{1,0:T(8,128)(2,1)S(1)}, u32[]{:S(2)}, u32[]{:S(2)}) collective-permute-start(bf16[512,512]{1,0:T(8,128)(2,1)} %refs_0_.4), channel_id=1, source_target_pairs={{64,0},{17,1},{72,8},{25,9},{80,16},{1,17},{88,24},{9,25},{96,32},... | collective-permute-start | bytes 1572872 | tf_op jit(solution)/shard_map/ppermute | solution.py:45
  4.2 1.9 %collective-permute-start.5 = (bf16[32,8192]{1,0:T(8,128)(2,1)}, bf16[32,8192]{1,0:T(8,128)(2,1)S(1)}, u32[]{:S(2)}, u32[]{:S(2)}) collective-permute-start(bf16[32,8192]{1,0:T(8,128)(2,1)} %refs_0_.5), channel_id=1, source_target_pairs={{6,0},{3,1},{0,2},{5,3},{2,4},{7,5},{4,6},{1,7},{14,8},{11,9},{8,1... | collective-permute-start | bytes 1572872 | tf_op jit(solution)/shard_map/ppermute | solution.py:25
  6.1 2.1 %collective-permute-start.1 = (bf16[32,8192]{1,0:T(8,128)(2,1)}, bf16[32,8192]{1,0:T(8,128)(2,1)S(1)}, u32[]{:S(2)}, u32[]{:S(2)}) collective-permute-start(bf16[32,8192]{1,0:T(8,128)(2,1)} %refs_0_.5), channel_id=1, source_target_pairs={{2,0},{7,1},{4,2},{1,3},{6,4},{3,5},{0,6},{5,7},{10,8},{15,9},{12,... | collective-permute-start | bytes 1572872 | tf_op jit(solution)/shard_map/ppermute | solution.py:25
  8.2 1.2 %collective-permute-done.8.refs_2_ = bf16[512,512]{1,0:T(8,128)(2,1)S(1)} collective-permute-done((bf16[512,512]{1,0:T(8,128)(2,1)}, bf16[512,512]{1,0:T(8,128)(2,1)S(1)}, u32[]{:S(2)}, u32[]{:S(2)}) %collective-permute-start.8) | collective-permute-done | bytes 524320 | tf_op jit(solution)/shard_map/ppermute | solution.py:45
  9.4 1.5 %collective-permute-done.7.refs_1_ = bf16[512,512]{1,0:T(8,128)(2,1)S(1)} collective-permute-done((bf16[512,512]{1,0:T(8,128)(2,1)}, bf16[512,512]{1,0:T(8,128)(2,1)S(1)}, u32[]{:S(2)}, u32[]{:S(2)}) %collective-permute-start.7) | collective-permute-done | bytes 524320 | tf_op jit(solution)/shard_map/ppermute | solution.py:45
  10.9 6.3 %collective-permute-done.9.refs_3_ = bf16[512,512]{1,0:T(8,128)(2,1)S(1)} collective-permute-done((bf16[512,512]{1,0:T(8,128)(2,1)}, bf16[512,512]{1,0:T(8,128)(2,1)S(1)}, u32[]{:S(2)}, u32[]{:S(2)}) %collective-permute-start.9) | collective-permute-done | bytes 524320 | tf_op jit(solution)/shard_map/ppermute | solution.py:45
  17.1 1.9 %collective-permute-done.5.refs_6_.refs_5_ = bf16[32,8192]{1,0:T(8,128)(2,1)S(1)} collective-permute-done((bf16[32,8192]{1,0:T(8,128)(2,1)}, bf16[32,8192]{1,0:T(8,128)(2,1)S(1)}, u32[]{:S(2)}, u32[]{:S(2)}) %collective-permute-start.5) | collective-permute-done | bytes 524320 | tf_op jit(solution)/shard_map/ppermute | solution.py:25
  19.1 0.9 collective-permute-done.1.refs_2_.refs_4_
  19.9 1.1 %stack.21.refs_0_ = bf16[4,512,512]{2,1,0:T(8,128)(2,1)S(1)} custom-call(bf16[512,512]{1,0:T(8,128)(2,1)} %refs_0_.4, bf16[512,512]{1,0:T(8,128)(2,1)S(1)} %collective-permute-done.7.refs_1_, bf16[512,512]{1,0:T(8,128)(2,1)S(1)} %collective-permute-done.8.refs_2_, bf16[512,512]{1,0:T(8,128)(2,1)S(1)} %collective-permute-done.9.refs_3_, ...), custom_call_target="tpu_custom_call" | custom-call | bytes 4194304 | tf_op jit(solution)/shard_map/stack/pallas_call | solution.py:53
  21.0 1.7 %collective-permute-start.11 = (bf16[4,512,512]{2,1,0:T(8,128)(2,1)S(1)}, bf16[4,512,512]{2,1,0:T(8,128)(2,1)}, u32[]{:S(2)}, u32[]{:S(2)}) collective-permute-start(bf16[4,512,512]{2,1,0:T(8,128)(2,1)S(1)} %stack.21.refs_0_), channel_id=1, source_target_pairs={{24,0},{97,1},{0,8},{105,9},{8,16},{113,17},{16,24},{121,25},{56,3... | collective-permute-start | bytes 6291464 | tf_op jit(solution)/shard_map/ppermute | solution.py:45
  22.7 2.6 %collective-permute-start.10 = (bf16[4,512,512]{2,1,0:T(8,128)(2,1)S(1)}, bf16[4,512,512]{2,1,0:T(8,128)(2,1)}, u32[]{:S(2)}, u32[]{:S(2)}) collective-permute-start(bf16[4,512,512]{2,1,0:T(8,128)(2,1)S(1)} %stack.21.refs_0_), channel_id=1, source_target_pairs={{8,0},{33,1},{16,8},{41,9},{24,16},{49,17},{0,24},{57,25},{40,32},... | collective-permute-start | bytes 6291464 | tf_op jit(solution)/shard_map/ppermute | solution.py:45
  25.3 0.0 copy-done.2
  25.3 0.0 collective-permute-start
  25.4 2.6 %collective-permute-start.3 = (bf16[32,8192]{1,0:T(8,128)(2,1)S(1)}, bf16[32,8192]{1,0:T(8,128)(2,1)}, u32[]{:S(2)}, u32[]{:S(2)}) collective-permute-start(bf16[32,8192]{1,0:T(8,128)(2,1)S(1)} %collective-permute-done.1.refs_2_.refs_4_), channel_id=1, source_target_pairs={{2,0},{7,1},{4,2},{1,3},{6,4},{3,5},{0,6},{5,7},{10,8},{15,9},{12,... | collective-permute-start | bytes 1572872 | tf_op jit(solution)/shard_map/ppermute | solution.py:25
  27.9 0.0 collective-permute-start.6
  27.9 0.0 collective-permute-done.refs_1_
  27.9 0.0 copy-start
  27.9 0.8 copy-done
  28.7 0.5 collective-permute-start.2
  29.2 5.4 %collective-permute-done.3.refs_4_ = bf16[32,8192]{1,0:T(8,128)(2,1)} collective-permute-done((bf16[32,8192]{1,0:T(8,128)(2,1)S(1)}, bf16[32,8192]{1,0:T(8,128)(2,1)}, u32[]{:S(2)}, u32[]{:S(2)}) %collective-permute-start.3) | collective-permute-done | bytes 524320 | tf_op jit(solution)/shard_map/ppermute | solution.py:25
  34.6 0.9 collective-permute-start.4
  35.5 0.1 pad_add_fusion.place
  35.6 0.0 collective-permute-done.6.refs_7_
  35.6 0.0 collective-permute-done.2.refs_3_
  35.6 1.8 %collective-permute-done.4.refs_5_ = bf16[32,8192]{1,0:T(8,128)(2,1)} collective-permute-done((bf16[32,8192]{1,0:T(8,128)(2,1)}, bf16[32,8192]{1,0:T(8,128)(2,1)}, u32[]{:S(2)}, u32[]{:S(2)}) %collective-permute-start.4) | collective-permute-done | bytes 524320 | tf_op jit(solution)/shard_map/ppermute | solution.py:49
  37.4 1.0 %copy-done.1 = bf16[32,8192]{1,0:T(8,128)(2,1)S(1)} copy-done((bf16[32,8192]{1,0:T(8,128)(2,1)S(1)}, bf16[32,8192]{1,0:T(8,128)(2,1)}, u32[]{:S(2)}) %copy-start.1) | copy-done | bytes 524312
  38.4 11.0 %project.2 = (f32[256,1536]{1,0:T(8,128)S(1)}, bf16[4096,256]{1,0:T(8,128)(2,1)S(1)}, f32[3,3,512]{2,1,0:T(4,128)S(1)}, f32[1,512]{1,0:T(1,128)S(1)}) custom-call(s32[4]{0:T(128)S(1)} %pad_add_fusion.place, bf16[32,8192]{1,0:T(8,128)(2,1)} %refs_0_.5, bf16[32,8192]{1,0:T(8,128)(2,1)S(1)} %copy-done.1, ...), custom_call_target="tpu_custom_call" | custom-call | flops 3221225472 | bytes 14680064 | tf_op jit(solution)/shard_map/project/pallas_call | solution.py:53
  49.4 0.0 collective-permute-done.11.behind.refs_2_
  49.4 0.0 collective-permute-done.10.ahead.refs_1_
  49.4 1.6 %halves.1 = (bf16[2,512,512]{2,1,0:T(8,128)(2,1)S(1)}, bf16[2,512,512]{2,1,0:T(8,128)(2,1)S(1)}) custom-call(bf16[4,512,512]{2,1,0:T(8,128)(2,1)} %collective-permute-done.10.ahead.refs_1_, bf16[4,512,512]{2,1,0:T(8,128)(2,1)} %collective-permute-done.11.behind.refs_2_, f32[1,512]{1,0:T(1,128)S(1)} %get-tuple-element.27.after.bias), custom_call_target="tpu_custom_call" | custom-call | bytes 4194304 | tf_op jit(solution)/shard_map/halves/pallas_call | solution.py:53
  51.0 1.8 %collective-permute-start.14 = (bf16[2,512,512]{2,1,0:T(8,128)(2,1)S(1)}, bf16[2,512,512]{2,1,0:T(8,128)(2,1)S(1)}, u32[]{:S(2)}, u32[]{:S(2)}) collective-permute-start(bf16[2,512,512]{2,1,0:T(8,128)(2,1)S(1)} %get-tuple-element.32), channel_id=1, source_target_pairs={{24,0},{97,1},{0,8},{105,9},{8,16},{113,17},{16,24},{121,25},{56,3... | collective-permute-start | bytes 3145736 | tf_op jit(solution)/shard_map/ppermute | solution.py:45
  52.8 1.6 %collective-permute-start.13 = (bf16[2,512,512]{2,1,0:T(8,128)(2,1)S(1)}, bf16[2,512,512]{2,1,0:T(8,128)(2,1)S(1)}, u32[]{:S(2)}, u32[]{:S(2)}) collective-permute-start(bf16[2,512,512]{2,1,0:T(8,128)(2,1)S(1)} %get-tuple-element.28.refs_11_), channel_id=1, source_target_pairs={{8,0},{33,1},{16,8},{41,9},{24,16},{49,17},{0,24},{57,25},{40,32},... | collective-permute-start | bytes 3145736 | tf_op jit(solution)/shard_map/ppermute | solution.py:45
  54.4 5.2 %project.3 = (bf16[256,1536]{1,0:T(8,128)(2,1)S(1)}, bf16[176,512]{1,0:T(8,128)(2,1)S(1)}) custom-call(s32[4]{0:T(128)S(1)} %pad_add_fusion.place, bf16[32,8192]{1,0:T(8,128)(2,1)} %refs_0_.5, bf16[32,8192]{1,0:T(8,128)(2,1)S(1)} %copy-done.1, bf16[32,8192]{1,0:T(8,128)(2,1)S(1)} %collective-permute-done.1.refs_2_.refs_4_, ...), custom_call_target="tpu_custom_call" | custom-call | flops 3221225472 | bytes 14680064 | tf_op jit(solution)/shard_map/project/pallas_call | solution.py:53
  59.7 2.5 %collective-permute-start.12 = (bf16[176,512]{1,0:T(8,128)(2,1)S(1)}, bf16[176,512]{1,0:T(8,128)(2,1)S(1)}, u32[]{:S(2)}, u32[]{:S(2)}) collective-permute-start(bf16[176,512]{1,0:T(8,128)(2,1)S(1)} %get-tuple-element.30), channel_id=1, source_target_pairs={{0,8},{8,16},{16,24},{24,32},{32,40},{40,48},{48,56},{56,64},{64,7... | collective-permute-start | bytes 540680 | tf_op jit(solution)/shard_map/ppermute | solution.py:376
  62.2 8.4 %collective-permute-done.12.edge = bf16[176,512]{1,0:T(8,128)(2,1)S(1)} collective-permute-done((bf16[176,512]{1,0:T(8,128)(2,1)S(1)}, bf16[176,512]{1,0:T(8,128)(2,1)S(1)}, u32[]{:S(2)}, u32[]{:S(2)}) %collective-permute-start.12) | collective-permute-done | bytes 180256 | tf_op jit(solution)/shard_map/ppermute | solution.py:376
  70.6 0.4 collective-permute-done.14.two.refs_4_
  71.0 0.0 collective-permute-done.13.one.refs_3_
  71.0 1.1 %mix.1.gated = bf16[256,512]{1,0:T(8,128)(2,1)S(1)} custom-call(bf16[256,1536]{1,0:T(8,128)(2,1)S(1)} %get-tuple-element.29.projected, bf16[176,512]{1,0:T(8,128)(2,1)S(1)} %collective-permute-done.12.edge, f32[3,3,512]{2,1,0:T(4,128)S(1)} %get-tuple-element.26.refs_10_.taps, f32[1,512]{1,0:T(1,128)S(1)} %get-tuple-element.27.after.bias, ...), custom_call_target="tpu_custom_call" | custom-call | flops 536870912 | bytes 4194304 | tf_op jit(solution)/shard_map/mix/pallas_call | solution.py:53
  72.1 3.6 %out.2 = (bf16[128,4608]{1,0:T(8,128)(2,1)S(1)}, bf16[128,4608]{1,0:T(8,128)(2,1)S(1)}) custom-call(s32[4]{0:T(128)S(1)} %pad_add_fusion.place, bf16[256,512]{1,0:T(8,128)(2,1)S(1)} %mix.1.gated, bf16[4,512,512]{2,1,0:T(8,128)(2,1)S(1)} %stack.21.refs_0_, bf16[4,512,512]{2,1,0:T(8,128)(2,1)} %collective-permute-done.10.ahead.refs_1_, ...), custom_call_target="tpu_custom_call" | custom-call | flops 1207959552 | bytes 4718592 | tf_op jit(solution)/shard_map/out/pallas_call | solution.py:53
  75.7 0.1 collective-permute-start.15
  75.8 3.5 %out.3 = (bf16[128,3584]{1,0:T(8,128)(2,1)S(1)}, bf16[128,3584]{1,0:T(8,128)(2,1)S(1)}) custom-call(s32[4]{0:T(128)S(1)} %pad_add_fusion.place, bf16[256,512]{1,0:T(8,128)(2,1)S(1)} %mix.1.gated, bf16[4,512,512]{2,1,0:T(8,128)(2,1)S(1)} %stack.21.refs_0_, bf16[4,512,512]{2,1,0:T(8,128)(2,1)} %collective-permute-done.10.ahead.refs_1_, ...), custom_call_target="tpu_custom_call" | custom-call | flops 939524096 | bytes 3670016 | tf_op jit(solution)/shard_map/out/pallas_call | solution.py:53
  79.3 0.6 collective-permute-start.19
  79.9 0.0 collective-permute-done.15.got
  79.9 0.3 pair.2
  80.1 0.3 collective-permute-start.17
  80.4 1.5 %collective-permute-done.19.got = bf16[128,3584]{1,0:T(8,128)(2,1)S(1)} collective-permute-done((bf16[128,3584]{1,0:T(8,128)(2,1)S(1)}, bf16[128,3584]{1,0:T(8,128)(2,1)S(1)}, u32[]{:S(2)}, u32[]{:S(2)}) %collective-permute-start.19) | collective-permute-done | bytes 917536 | tf_op jit(solution)/shard_map/ppermute | solution.py:49
  82.0 0.2 pair.3
  82.2 0.3 collective-permute-start.21
  82.5 3.1 %collective-permute-start.16 = (bf16[32,4608]{1,0:T(8,128)(2,1)S(1)}, bf16[32,4608]{1,0:T(8,128)(2,1)S(1)}, u32[]{:S(2)}, u32[]{:S(2)}) collective-permute-start(bf16[32,4608]{1,0:T(8,128)(2,1)S(1)} %get-tuple-element.36), channel_id=1, source_target_pairs={{2,0},{7,1},{4,2},{1,3},{6,4},{3,5},{0,6},{5,7},{10,8},{15,9},{12,... | collective-permute-start | bytes 884744 | tf_op jit(solution)/shard_map/ppermute | solution.py:25
  85.6 2.6 %collective-permute-done.17.b = bf16[32,4608]{1,0:T(8,128)(2,1)S(1)} collective-permute-done((bf16[32,4608]{1,0:T(8,128)(2,1)S(1)}, bf16[32,4608]{1,0:T(8,128)(2,1)S(1)}, u32[]{:S(2)}, u32[]{:S(2)}) %collective-permute-start.17) | collective-permute-done | bytes 294944 | tf_op jit(solution)/shard_map/ppermute | solution.py:25
  88.1 0.1 join.2
  88.2 0.1 collective-permute-start.18
  88.3 3.7 %collective-permute-start.20 = (bf16[32,3584]{1,0:T(8,128)(2,1)S(1)}, bf16[32,3584]{1,0:T(8,128)(2,1)S(1)}, u32[]{:S(2)}, u32[]{:S(2)}) collective-permute-start(bf16[32,3584]{1,0:T(8,128)(2,1)S(1)} %get-tuple-element.42), channel_id=1, source_target_pairs={{2,0},{7,1},{4,2},{1,3},{6,4},{3,5},{0,6},{5,7},{10,8},{15,9},{12,... | collective-permute-start | bytes 688136 | tf_op jit(solution)/shard_map/ppermute | solution.py:25
  92.0 0.0 collective-permute-done.21.b
  92.0 0.1 join.3
  92.0 0.1 collective-permute-start.22
  92.1 5.9 %collective-permute-done.20.refs_4_ = bf16[32,3584]{1,0:T(8,128)(2,1)S(1)} collective-permute-done((bf16[32,3584]{1,0:T(8,128)(2,1)S(1)}, bf16[32,3584]{1,0:T(8,128)(2,1)S(1)}, u32[]{:S(2)}, u32[]{:S(2)}) %collective-permute-start.20) | collective-permute-done | bytes 229408 | tf_op jit(solution)/shard_map/ppermute | solution.py:25
  98.0 3.8 %collective-permute-done.22.refs_5_ = bf16[32,3584]{1,0:T(8,128)(2,1)S(1)} collective-permute-done((bf16[32,3584]{1,0:T(8,128)(2,1)S(1)}, bf16[32,3584]{1,0:T(8,128)(2,1)S(1)}, u32[]{:S(2)}, u32[]{:S(2)}) %collective-permute-start.22) | collective-permute-done | bytes 229408 | tf_op jit(solution)/shard_map/ppermute | solution.py:25
  101.8 0.0 collective-permute-done.16.refs_1_
  101.8 0.0 collective-permute-done.18.refs_2_
  101.8 1.5 %finish.1 = bf16[32,8192]{1,0:T(8,128)(2,1)} custom-call(s32[4]{0:T(128)S(1)} %pad_add_fusion.place, bf16[32,4608]{1,0:T(8,128)(2,1)S(1)} %get-tuple-element.35.refs_0_, bf16[32,4608]{1,0:T(8,128)(2,1)S(1)} %collective-permute-done.16.refs_1_, bf16[32,4608]{1,0:T(8,128)(2,1)S(1)} %collective-permute-done.18.refs_2_, ...), custom_call_target="tpu_custom_call" | custom-call | bytes 3145728 | tf_op jit(solution)/shard_map/finish/pallas_call | solution.py:53
  (1 shorter events, 0.0 us)
Async XLA Ops:
  0.0 25.3 %copy-start.2 = (bf16[32,8192]{1,0:T(8,128)(2,1)S(1)}, bf16[32,8192]{1,0:T(8,128)(2,1)}, u32[]{:S(2)}) copy-start(bf16[32,8192]{1,0:T(8,128)(2,1)} %refs_0_.5) | copy-start | bytes 1572868
  0.0 9.4 %collective-permute-start.8 = (bf16[512,512]{1,0:T(8,128)(2,1)}, bf16[512,512]{1,0:T(8,128)(2,1)S(1)}, u32[]{:S(2)}, u32[]{:S(2)}) collective-permute-start(bf16[512,512]{1,0:T(8,128)(2,1)} %refs_0_.4), channel_id=1, source_target_pairs={{96,0},{25,1},{104,8},{1,9},{112,16},{9,17},{120,24},{17,25},{0,32... | collective-permute-start | bytes 1572872 | tf_op jit(solution)/shard_map/ppermute | solution.py:45
  1.5 9.4 %collective-permute-start.7 = (bf16[512,512]{1,0:T(8,128)(2,1)}, bf16[512,512]{1,0:T(8,128)(2,1)S(1)}, u32[]{:S(2)}, u32[]{:S(2)}) collective-permute-start(bf16[512,512]{1,0:T(8,128)(2,1)} %refs_0_.4), channel_id=1, source_target_pairs={{32,0},{9,1},{40,8},{17,9},{48,16},{25,17},{56,24},{1,25},{64,32},... | collective-permute-start | bytes 1572872 | tf_op jit(solution)/shard_map/ppermute | solution.py:45
  2.0 15.1 %collective-permute-start.9 = (bf16[512,512]{1,0:T(8,128)(2,1)}, bf16[512,512]{1,0:T(8,128)(2,1)S(1)}, u32[]{:S(2)}, u32[]{:S(2)}) collective-permute-start(bf16[512,512]{1,0:T(8,128)(2,1)} %refs_0_.4), channel_id=1, source_target_pairs={{64,0},{17,1},{72,8},{25,9},{80,16},{1,17},{88,24},{9,25},{96,32},... | collective-permute-start | bytes 1572872 | tf_op jit(solution)/shard_map/ppermute | solution.py:45
  4.2 14.9 %collective-permute-start.5 = (bf16[32,8192]{1,0:T(8,128)(2,1)}, bf16[32,8192]{1,0:T(8,128)(2,1)S(1)}, u32[]{:S(2)}, u32[]{:S(2)}) collective-permute-start(bf16[32,8192]{1,0:T(8,128)(2,1)} %refs_0_.5), channel_id=1, source_target_pairs={{6,0},{3,1},{0,2},{5,3},{2,4},{7,5},{4,6},{1,7},{14,8},{11,9},{8,1... | collective-permute-start | bytes 1572872 | tf_op jit(solution)/shard_map/ppermute | solution.py:25
  6.1 13.8 %collective-permute-start.1 = (bf16[32,8192]{1,0:T(8,128)(2,1)}, bf16[32,8192]{1,0:T(8,128)(2,1)S(1)}, u32[]{:S(2)}, u32[]{:S(2)}) collective-permute-start(bf16[32,8192]{1,0:T(8,128)(2,1)} %refs_0_.5), channel_id=1, source_target_pairs={{2,0},{7,1},{4,2},{1,3},{6,4},{3,5},{0,6},{5,7},{10,8},{15,9},{12,... | collective-permute-start | bytes 1572872 | tf_op jit(solution)/shard_map/ppermute | solution.py:25
  21.0 28.4 %collective-permute-start.11 = (bf16[4,512,512]{2,1,0:T(8,128)(2,1)S(1)}, bf16[4,512,512]{2,1,0:T(8,128)(2,1)}, u32[]{:S(2)}, u32[]{:S(2)}) collective-permute-start(bf16[4,512,512]{2,1,0:T(8,128)(2,1)S(1)} %stack.21.refs_0_), channel_id=1, source_target_pairs={{24,0},{97,1},{0,8},{105,9},{8,16},{113,17},{16,24},{121,25},{56,3... | collective-permute-start | bytes 6291464 | tf_op jit(solution)/shard_map/ppermute | solution.py:45
  22.7 26.7 %collective-permute-start.10 = (bf16[4,512,512]{2,1,0:T(8,128)(2,1)S(1)}, bf16[4,512,512]{2,1,0:T(8,128)(2,1)}, u32[]{:S(2)}, u32[]{:S(2)}) collective-permute-start(bf16[4,512,512]{2,1,0:T(8,128)(2,1)S(1)} %stack.21.refs_0_), channel_id=1, source_target_pairs={{8,0},{33,1},{16,8},{41,9},{24,16},{49,17},{0,24},{57,25},{40,32},... | collective-permute-start | bytes 6291464 | tf_op jit(solution)/shard_map/ppermute | solution.py:45
  25.3 2.6 %collective-permute-start = (bf16[32,8192]{1,0:T(8,128)(2,1)S(1)}, bf16[32,8192]{1,0:T(8,128)(2,1)S(1)}, u32[]{:S(2)}, u32[]{:S(2)}) collective-permute-start(bf16[32,8192]{1,0:T(8,128)(2,1)S(1)} %copy-done.2), channel_id=1, source_target_pairs={{0,1},{1,0},{2,3},{3,2},{4,5},{5,4},{6,7},{7,6},{8,9},{9,8},{10,11... | collective-permute-start | bytes 1572872 | tf_op jit(solution)/shard_map/ppermute | solution.py:49
  25.4 9.3 %collective-permute-start.3 = (bf16[32,8192]{1,0:T(8,128)(2,1)S(1)}, bf16[32,8192]{1,0:T(8,128)(2,1)}, u32[]{:S(2)}, u32[]{:S(2)}) collective-permute-start(bf16[32,8192]{1,0:T(8,128)(2,1)S(1)} %collective-permute-done.1.refs_2_.refs_4_), channel_id=1, source_target_pairs={{2,0},{7,1},{4,2},{1,3},{6,4},{3,5},{0,6},{5,7},{10,8},{15,9},{12,... | collective-permute-start | bytes 1572872 | tf_op jit(solution)/shard_map/ppermute | solution.py:25
  27.9 7.7 %collective-permute-start.6 = (bf16[32,8192]{1,0:T(8,128)(2,1)S(1)}, bf16[32,8192]{1,0:T(8,128)(2,1)}, u32[]{:S(2)}, u32[]{:S(2)}) collective-permute-start(bf16[32,8192]{1,0:T(8,128)(2,1)S(1)} %collective-permute-done.5.refs_6_.refs_5_), channel_id=1, source_target_pairs={{0,1},{1,0},{2,3},{3,2},{4,5},{5,4},{6,7},{7,6},{8,9},{9,8},{10,11... | collective-permute-start | bytes 1572872 | tf_op jit(solution)/shard_map/ppermute | solution.py:49
  27.9 0.8 copy-start
  28.7 6.9 %collective-permute-start.2 = (bf16[32,8192]{1,0:T(8,128)(2,1)S(1)}, bf16[32,8192]{1,0:T(8,128)(2,1)}, u32[]{:S(2)}, u32[]{:S(2)}) collective-permute-start(bf16[32,8192]{1,0:T(8,128)(2,1)S(1)} %collective-permute-done.1.refs_2_.refs_4_), channel_id=1, source_target_pairs={{0,1},{1,0},{2,3},{3,2},{4,5},{5,4},{6,7},{7,6},{8,9},{9,8},{10,11... | collective-permute-start | bytes 1572872 | tf_op jit(solution)/shard_map/ppermute | solution.py:49
  34.6 2.7 %collective-permute-start.4 = (bf16[32,8192]{1,0:T(8,128)(2,1)}, bf16[32,8192]{1,0:T(8,128)(2,1)}, u32[]{:S(2)}, u32[]{:S(2)}) collective-permute-start(bf16[32,8192]{1,0:T(8,128)(2,1)} %collective-permute-done.3.refs_4_), channel_id=1, source_target_pairs={{0,1},{1,0},{2,3},{3,2},{4,5},{5,4},{6,7},{7,6},{8,9},{9,8},{10,11... | collective-permute-start | bytes 1572872 | tf_op jit(solution)/shard_map/ppermute | solution.py:49
  37.4 1.0 %copy-start.1 = (bf16[32,8192]{1,0:T(8,128)(2,1)S(1)}, bf16[32,8192]{1,0:T(8,128)(2,1)}, u32[]{:S(2)}) copy-start(bf16[32,8192]{1,0:T(8,128)(2,1)} %copy-done) | copy-start | bytes 1572868
  51.0 20.0 %collective-permute-start.14 = (bf16[2,512,512]{2,1,0:T(8,128)(2,1)S(1)}, bf16[2,512,512]{2,1,0:T(8,128)(2,1)S(1)}, u32[]{:S(2)}, u32[]{:S(2)}) collective-permute-start(bf16[2,512,512]{2,1,0:T(8,128)(2,1)S(1)} %get-tuple-element.32), channel_id=1, source_target_pairs={{24,0},{97,1},{0,8},{105,9},{8,16},{113,17},{16,24},{121,25},{56,3... | collective-permute-start | bytes 3145736 | tf_op jit(solution)/shard_map/ppermute | solution.py:45
  52.8 18.2 %collective-permute-start.13 = (bf16[2,512,512]{2,1,0:T(8,128)(2,1)S(1)}, bf16[2,512,512]{2,1,0:T(8,128)(2,1)S(1)}, u32[]{:S(2)}, u32[]{:S(2)}) collective-permute-start(bf16[2,512,512]{2,1,0:T(8,128)(2,1)S(1)} %get-tuple-element.28.refs_11_), channel_id=1, source_target_pairs={{8,0},{33,1},{16,8},{41,9},{24,16},{49,17},{0,24},{57,25},{40,32},... | collective-permute-start | bytes 3145736 | tf_op jit(solution)/shard_map/ppermute | solution.py:45
  59.7 10.9 %collective-permute-start.12 = (bf16[176,512]{1,0:T(8,128)(2,1)S(1)}, bf16[176,512]{1,0:T(8,128)(2,1)S(1)}, u32[]{:S(2)}, u32[]{:S(2)}) collective-permute-start(bf16[176,512]{1,0:T(8,128)(2,1)S(1)} %get-tuple-element.30), channel_id=1, source_target_pairs={{0,8},{8,16},{16,24},{24,32},{32,40},{40,48},{48,56},{56,64},{64,7... | collective-permute-start | bytes 540680 | tf_op jit(solution)/shard_map/ppermute | solution.py:376
  75.7 4.2 %collective-permute-start.15 = (bf16[128,4608]{1,0:T(8,128)(2,1)S(1)}, bf16[128,4608]{1,0:T(8,128)(2,1)S(1)}, u32[]{:S(2)}, u32[]{:S(2)}) collective-permute-start(bf16[128,4608]{1,0:T(8,128)(2,1)S(1)} %get-tuple-element.34), channel_id=1, source_target_pairs={{0,1},{1,0},{2,3},{3,2},{4,5},{5,4},{6,7},{7,6},{8,9},{9,8},{10,11... | collective-permute-start | bytes 3538952 | tf_op jit(solution)/shard_map/ppermute | solution.py:49
  79.3 2.7 %collective-permute-start.19 = (bf16[128,3584]{1,0:T(8,128)(2,1)S(1)}, bf16[128,3584]{1,0:T(8,128)(2,1)S(1)}, u32[]{:S(2)}, u32[]{:S(2)}) collective-permute-start(bf16[128,3584]{1,0:T(8,128)(2,1)S(1)} %get-tuple-element.40), channel_id=1, source_target_pairs={{0,1},{1,0},{2,3},{3,2},{4,5},{5,4},{6,7},{7,6},{8,9},{9,8},{10,11... | collective-permute-start | bytes 2752520 | tf_op jit(solution)/shard_map/ppermute | solution.py:49
  80.1 8.0 %collective-permute-start.17 = (bf16[32,4608]{1,0:T(8,128)(2,1)S(1)}, bf16[32,4608]{1,0:T(8,128)(2,1)S(1)}, u32[]{:S(2)}, u32[]{:S(2)}) collective-permute-start(bf16[32,4608]{1,0:T(8,128)(2,1)S(1)} %get-tuple-element.38), channel_id=1, source_target_pairs={{6,0},{3,1},{0,2},{5,3},{2,4},{7,5},{4,6},{1,7},{14,8},{11,9},{8,1... | collective-permute-start | bytes 884744 | tf_op jit(solution)/shard_map/ppermute | solution.py:25
  82.2 9.8 %collective-permute-start.21 = (bf16[32,3584]{1,0:T(8,128)(2,1)S(1)}, bf16[32,3584]{1,0:T(8,128)(2,1)S(1)}, u32[]{:S(2)}, u32[]{:S(2)}) collective-permute-start(bf16[32,3584]{1,0:T(8,128)(2,1)S(1)} %get-tuple-element.44), channel_id=1, source_target_pairs={{6,0},{3,1},{0,2},{5,3},{2,4},{7,5},{4,6},{1,7},{14,8},{11,9},{8,1... | collective-permute-start | bytes 688136 | tf_op jit(solution)/shard_map/ppermute | solution.py:25
  82.5 19.4 %collective-permute-start.16 = (bf16[32,4608]{1,0:T(8,128)(2,1)S(1)}, bf16[32,4608]{1,0:T(8,128)(2,1)S(1)}, u32[]{:S(2)}, u32[]{:S(2)}) collective-permute-start(bf16[32,4608]{1,0:T(8,128)(2,1)S(1)} %get-tuple-element.36), channel_id=1, source_target_pairs={{2,0},{7,1},{4,2},{1,3},{6,4},{3,5},{0,6},{5,7},{10,8},{15,9},{12,... | collective-permute-start | bytes 884744 | tf_op jit(solution)/shard_map/ppermute | solution.py:25
  88.2 13.6 %collective-permute-start.18 = (bf16[32,4608]{1,0:T(8,128)(2,1)S(1)}, bf16[32,4608]{1,0:T(8,128)(2,1)S(1)}, u32[]{:S(2)}, u32[]{:S(2)}) collective-permute-start(bf16[32,4608]{1,0:T(8,128)(2,1)S(1)} %join.2), channel_id=1, source_target_pairs={{6,0},{3,1},{0,2},{5,3},{2,4},{7,5},{4,6},{1,7},{14,8},{11,9},{8,1... | collective-permute-start | bytes 884744 | tf_op jit(solution)/shard_map/ppermute | solution.py:25
  88.3 9.7 %collective-permute-start.20 = (bf16[32,3584]{1,0:T(8,128)(2,1)S(1)}, bf16[32,3584]{1,0:T(8,128)(2,1)S(1)}, u32[]{:S(2)}, u32[]{:S(2)}) collective-permute-start(bf16[32,3584]{1,0:T(8,128)(2,1)S(1)} %get-tuple-element.42), channel_id=1, source_target_pairs={{2,0},{7,1},{4,2},{1,3},{6,4},{3,5},{0,6},{5,7},{10,8},{15,9},{12,... | collective-permute-start | bytes 688136 | tf_op jit(solution)/shard_map/ppermute | solution.py:25
  92.0 9.8 %collective-permute-start.22 = (bf16[32,3584]{1,0:T(8,128)(2,1)S(1)}, bf16[32,3584]{1,0:T(8,128)(2,1)S(1)}, u32[]{:S(2)}, u32[]{:S(2)}) collective-permute-start(bf16[32,3584]{1,0:T(8,128)(2,1)S(1)} %join.3), channel_id=1, source_target_pairs={{6,0},{3,1},{0,2},{5,3},{2,4},{7,5},{4,6},{1,7},{14,8},{11,9},{8,1... | collective-permute-start | bytes 688136 | tf_op jit(solution)/shard_map/ppermute | solution.py:25
